TPU v7x, 32 devices: a whole 2x2x4 slice. The times are simulated.
32 devices in a mesh: exp: 8 (over y, x, core), dp: 4 (over z).
Axes of the slice: x: 2, y: 2, z: 4, core: 2. Of those that a mesh axis runs over, the one named last changes fastest.
Arguments:
- tokens: bfloat16 [49152, 768], P(('exp', 'dp')), may hold values from -6 to 6
- w_query: bfloat16 [768, 768], replicated, may hold values from -0.21875 to 0.21875
- w_key: bfloat16 [768, 768], replicated, may hold values from -0.21875 to 0.21875
- w_value: bfloat16 [768, 768], replicated, may hold values from -0.21875 to 0.21875
- w_output: bfloat16 [768, 768], replicated, may hold values from -1.75 to 1.75
- norm_attn: float32 [768], replicated, may hold values from 0.5 to 1.5
- norm_ffn: float32 [768], replicated, may hold values from 0.5 to 1.5
- relative_bias_table: float32 [32, 12], replicated, may hold values from -4 to 4
- w_router: float32 [768, 32], replicated, may hold values from -0.2 to 0.2
- w_in: bfloat16 [32, 768, 3072], P('exp'), may hold values from -0.21875 to 0.21875
- w_out: bfloat16 [32, 3072, 768], P('exp'), may hold values from -5 to 5
- expert_index: int32 [49152, 1], P(('exp', 'dp')), may hold values from 0 to 31
- priority: int32 [32, 1536], P(('exp', 'dp')), may hold values from 0 to 1535, each once within a row
- cotangent: bfloat16 [49152, 768], P(('exp', 'dp')), may hold values from -6 to 6
Outputs:
- mixed_out: bfloat16 [49152, 768], P(('exp', 'dp'))
- grad_tokens: float32 [49152, 768], P(('exp', 'dp'))
- grad_query: float32 [768, 768], replicated
- grad_key: float32 [768, 768], replicated
- grad_value: float32 [768, 768], replicated
- grad_output: float32 [768, 768], replicated
- grad_norm_attn: float32 [768], replicated
- grad_norm_ffn: float32 [768], replicated
- grad_table: float32 [32, 12], replicated
- grad_router: float32 [768, 32], replicated
- grad_in: float32 [32, 768, 3072], P('exp', None, 'dp')
- grad_out: float32 [32, 3072, 768], P('exp', 'dp')
Inputs may be any that keep to these rules, and one draw needn't show every extreme that they name: `expert_index`: the expert of each token; skewed over the experts. `priority`: each row orders the 1536 tokens of one device block, each value once; a lower value takes a slot first.
All inputs are finite; a program needn't handle non-finite values.
Results may differ from a plain program's by a relative error of at most 0.015.
Values may be sent and summed in bfloat16 or wider, within the bound.
A program may use at most 320 MiB of HBM per device.

v0:
```python
import jax
import jax.numpy as jnp
from jax import lax
from jax.sharding import PartitionSpec as P

HEADS = 12
HEAD_DIM = 64
SEQ = 512


LIMITS = (12, 16, 23, 32, 46, 64, 91)
EPSILON = 1e-06
FULL_PRECISION = lax.Precision.HIGHEST


def smooth(values):
    return jax.nn.gelu(values, approximate=True)


def bucket_onehot(length, count):
    places = jnp.arange(length, dtype=jnp.int32)
    offset = places[None, :] - places[:, None]
    distance = jnp.abs(offset)
    farther = jnp.zeros_like(distance)
    for limit in LIMITS:
        farther = farther + (distance >= limit).astype(jnp.int32)
    nearer = jnp.where(distance < 8, distance, 8 + farther)
    indices = nearer + jnp.where(offset > 0, 16, 0)
    return (indices[None, :, :] == jnp.arange(count, dtype=jnp.int32)[:, None, None]).astype(
        jnp.float32
    )


def per_device(
    tokens,
    w_query,
    w_key,
    w_value,
    w_output,
    norm_attn,
    norm_ffn,
    relative_bias_table,
    w_router,
    w_in,
    w_out,
    expert_index,
    priority,
    cotangent,
):
    tok_rows, width = tokens.shape
    seq_count = tok_rows // SEQ
    local_experts = w_in.shape[0]
    exp_devices = lax.axis_size("exp")
    all_experts = local_experts * exp_devices
    capacity = (5 * tok_rows + 4 * all_experts - 1) // (4 * all_experts)
    slot_count = all_experts * capacity
    scale = HEAD_DIM ** (-0.5)
    bucket_indicator = bucket_onehot(SEQ, relative_bias_table.shape[0])
    position_bias = jnp.einsum(
        "fyd,fs->syd", bucket_indicator, relative_bias_table, precision=FULL_PRECISION
    )

    def per_seq(array):
        return array.reshape(seq_count, SEQ, HEADS, HEAD_DIM)

    def score_block(q_block, k_block):
        return (
            jnp.einsum("qhd,khd->hqk", q_block, k_block, preferred_element_type=jnp.float32) * scale
            + position_bias
        )

    inputs = tokens.astype(jnp.float32)
    inv_first = lax.rsqrt(jnp.mean(inputs * inputs, axis=-1, keepdims=True) + EPSILON)
    unit_first = inputs * inv_first
    normed = (unit_first * norm_attn).astype(jnp.bfloat16)
    query = jnp.dot(normed, w_query, preferred_element_type=jnp.float32).astype(jnp.bfloat16)
    keys = jnp.dot(normed, w_key, preferred_element_type=jnp.float32).astype(jnp.bfloat16)
    values = jnp.dot(normed, w_value, preferred_element_type=jnp.float32).astype(jnp.bfloat16)

    def attention_forward(triple):
        q_block, k_block, v_block = triple
        scores = score_block(q_block, k_block)
        highest = jnp.max(scores, axis=-1, keepdims=True)
        totals = jnp.log(jnp.sum(jnp.exp(scores - highest), axis=-1, keepdims=True)) + highest
        weights = jnp.exp(scores - totals).astype(jnp.bfloat16)
        context_block = jnp.einsum(
            "hqk,khd->qhd", weights, v_block, preferred_element_type=jnp.float32
        ).astype(jnp.bfloat16)
        return (context_block, totals[..., 0])

    context, log_totals = lax.map(
        attention_forward, (per_seq(query), per_seq(keys), per_seq(values))
    )
    context = context.reshape(tok_rows, width)
    mixed = inputs + jnp.dot(context, w_output, preferred_element_type=jnp.float32)
    inv_second = lax.rsqrt(jnp.mean(mixed * mixed, axis=-1, keepdims=True) + EPSILON)
    unit_second = mixed * inv_second
    normed_ffn = unit_second * norm_ffn
    logits = jnp.dot(normed_ffn, w_router, precision=FULL_PRECISION)
    router_probs = jax.nn.softmax(logits, axis=-1)
    chosen = expert_index[:, 0]
    picked = (chosen[:, None] == jnp.arange(all_experts, dtype=jnp.int32)[None, :]).astype(
        jnp.float32
    )
    gate = jnp.sum(router_probs * picked, axis=-1, keepdims=True)
    order = priority[0]
    ahead = (chosen[:, None] == chosen[None, :]) & (order[None, :] < order[:, None])
    rank = jnp.sum(ahead.astype(jnp.int32), axis=1)
    slots = jnp.where(rank < capacity, chosen * capacity + rank, slot_count)

    def to_buffer(rows):
        filled = jnp.zeros((slot_count, width), jnp.bfloat16).at[slots].set(rows, mode="drop")
        return filled.reshape(exp_devices, local_experts, capacity, width)

    def from_buffer(buffer):
        flat = buffer.reshape(slot_count, width)
        return jnp.take(flat, slots, axis=0, mode="fill", fill_value=0).astype(jnp.float32)

    arrived_rows = lax.all_to_all(
        to_buffer(normed_ffn.astype(jnp.bfloat16)), "exp", split_axis=0, concat_axis=0, tiled=True
    )
    inner_rows = jnp.einsum(
        "sekd,edf->sekf", arrived_rows, w_in, preferred_element_type=jnp.float32
    )
    hidden_rows = smooth(inner_rows).astype(jnp.bfloat16)
    produced = jnp.einsum(
        "sekf,efd->sekd", hidden_rows, w_out, preferred_element_type=jnp.float32
    ).astype(jnp.bfloat16)
    answered_rows = lax.all_to_all(produced, "exp", split_axis=0, concat_axis=0, tiled=True)
    returned = from_buffer(answered_rows)
    mixed_out = (mixed + gate * returned).astype(jnp.bfloat16)
    upstream = cotangent.astype(jnp.float32)
    gate_grad = jnp.sum(upstream * returned, axis=-1, keepdims=True)
    produced_grad = lax.all_to_all(
        to_buffer((gate * upstream).astype(jnp.bfloat16)),
        "exp",
        split_axis=0,
        concat_axis=0,
        tiled=True,
    )
    hidden_grad = jnp.einsum(
        "sekd,efd->sekf", produced_grad, w_out, preferred_element_type=jnp.float32
    )
    unused, smooth_pull = jax.vjp(smooth, inner_rows)
    inner_grad = smooth_pull(hidden_grad)[0].astype(jnp.bfloat16)
    arrived_grad = jnp.einsum(
        "sekf,edf->sekd", inner_grad, w_in, preferred_element_type=jnp.float32
    ).astype(jnp.bfloat16)
    sent_grad = from_buffer(
        lax.all_to_all(arrived_grad, "exp", split_axis=0, concat_axis=0, tiled=True)
    )
    first_term = jnp.einsum(
        "sekd,sekf->edf", arrived_rows, inner_grad, preferred_element_type=jnp.float32
    )
    second_term = jnp.einsum(
        "sekf,sekd->efd", hidden_rows, produced_grad, preferred_element_type=jnp.float32
    )
    grad_in, grad_out = (
        lax.psum_scatter(
            first_term.astype(jnp.bfloat16), "dp", scatter_dimension=2, tiled=True
        ).astype(jnp.float32),
        lax.psum_scatter(
            second_term.astype(jnp.bfloat16), "dp", scatter_dimension=1, tiled=True
        ).astype(jnp.float32),
    )
    logit_grad = gate_grad * gate * (picked - router_probs)
    router_part = jnp.einsum("td,te->de", normed_ffn, logit_grad, precision=FULL_PRECISION)
    normed_grad = (
        jnp.einsum("te,de->td", logit_grad, w_router, precision=FULL_PRECISION) + sent_grad
    )
    norm_ffn_part = jnp.sum(normed_grad * unit_second, axis=0)
    unit_grad = normed_grad * norm_ffn
    mixed_grad = upstream + inv_second * (
        unit_grad - unit_second * jnp.mean(unit_grad * unit_second, axis=-1, keepdims=True)
    )
    branch_grad = mixed_grad.astype(jnp.bfloat16)
    output_part = jnp.einsum("td,te->de", context, branch_grad, preferred_element_type=jnp.float32)
    context_grad = jnp.einsum(
        "te,de->td", branch_grad, w_output, preferred_element_type=jnp.float32
    ).astype(jnp.bfloat16)

    def attend_back(pack):
        q_block, k_block, v_block, c_grad, totals = pack
        weights = jnp.exp(score_block(q_block, k_block) - totals[..., None])
        weights_low = weights.astype(jnp.bfloat16)
        value_grad = jnp.einsum(
            "hqk,qhd->khd", weights_low, c_grad, preferred_element_type=jnp.float32
        )
        weight_grad = jnp.einsum(
            "qhd,khd->hqk", c_grad, v_block, preferred_element_type=jnp.float32
        )
        scores_gradient = weights * (
            weight_grad - jnp.sum(weights * weight_grad, axis=-1, keepdims=True)
        )
        relative_table_gradient = jnp.einsum(
            "oxt,sxt->os", bucket_indicator, scores_gradient, precision=FULL_PRECISION
        )
        score_low = scores_gradient.astype(jnp.bfloat16)
        query_grad = (
            jnp.einsum("hqk,khd->qhd", score_low, k_block, preferred_element_type=jnp.float32)
            * scale
        )
        key_grad = (
            jnp.einsum("hqk,qhd->khd", score_low, q_block, preferred_element_type=jnp.float32)
            * scale
        )
        return (
            query_grad.astype(jnp.bfloat16),
            key_grad.astype(jnp.bfloat16),
            value_grad.astype(jnp.bfloat16),
            relative_table_gradient,
        )

    query_grad, key_grad, value_grad, table_parts = lax.map(
        attend_back,
        (per_seq(query), per_seq(keys), per_seq(values), per_seq(context_grad), log_totals),
    )
    query_grad = query_grad.reshape(tok_rows, width)
    key_grad = key_grad.reshape(tok_rows, width)
    value_grad = value_grad.reshape(tok_rows, width)
    table_part = jnp.sum(table_parts, axis=0)
    query_part = jnp.einsum("td,te->de", normed, query_grad, preferred_element_type=jnp.float32)
    key_part = jnp.einsum("td,te->de", normed, key_grad, preferred_element_type=jnp.float32)
    value_part = jnp.einsum("td,te->de", normed, value_grad, preferred_element_type=jnp.float32)
    normed_attn_grad = jnp.einsum(
        "te,de->td", query_grad, w_query, preferred_element_type=jnp.float32
    )
    normed_attn_grad = normed_attn_grad + jnp.einsum(
        "te,de->td", key_grad, w_key, preferred_element_type=jnp.float32
    )
    normed_attn_grad = normed_attn_grad + jnp.einsum(
        "te,de->td", value_grad, w_value, preferred_element_type=jnp.float32
    )
    norm_attn_part = jnp.sum(normed_attn_grad * unit_first, axis=0)
    unit_grad_first = normed_attn_grad * norm_attn
    grad_tokens = mixed_grad + inv_first * (
        unit_grad_first
        - unit_first * jnp.mean(unit_grad_first * unit_first, axis=-1, keepdims=True)
    )
    bucket_totals = lax.psum(
        (
            query_part,
            key_part,
            value_part,
            output_part,
            norm_attn_part,
            norm_ffn_part,
            table_part,
            router_part,
        ),
        ("exp", "dp"),
    )
    return (
        mixed_out,
        grad_tokens,
        bucket_totals[0],
        bucket_totals[1],
        bucket_totals[2],
        bucket_totals[3],
        bucket_totals[4],
        bucket_totals[5],
        bucket_totals[6],
        bucket_totals[7],
        grad_in,
        grad_out,
    )


def solution(mesh):
    return jax.shard_map(
        per_device,
        mesh=mesh,
        in_specs=(
            P(("exp", "dp"), None),
            P(),
            P(),
            P(),
            P(),
            P(),
            P(),
            P(),
            P(),
            P("exp", None, None),
            P("exp", None, None),
            P(("exp", "dp"), None),
            P(("exp", "dp"), None),
            P(("exp", "dp"), None),
        ),
        out_specs=(
            P(("exp", "dp"), None),
            P(("exp", "dp"), None),
            P(),
            P(),
            P(),
            P(),
            P(),
            P(),
            P(),
            P(),
            P("exp", None, "dp"),
            P("exp", "dp", None),
        ),
        check_vma=False,
    )
```

profile of v0, /device:TPU:0, one launch (start us, length us, event | category | flops | bytes accessed | tf_op | source)
XLA Modules:
  0.0 1246.5 jit_solution(2466249730183572459)
XLA Ops:
  78.1 13.9 %fusion.103 = f32[12,512,512]{2,0,1:T(8,128)} fusion(s32[512,512]{1,0:T(8,128)S(1)} %copy.144, f32[32,12]{0,1:T(8,128)S(1)} %copy-done.52), kind=kOutput, calls=%fused_computation.99 | convolution fusion | flops 1216348160 | bytes 13633024 | tf_op jit(solution)/shard_map/fyd,fs->syd/dot_general | solution.py:59
  91.9 17.7 %copy.148 = f32[12,512,512]{1,2,0:T(8,128)} copy(f32[12,512,512]{2,0,1:T(8,128)} %fusion.103) | data formatting | bytes 25165824 | tf_op jit(solution)/shard_map/while | solution.py:91
  109.9 38.1 %while.29 = (s32[]{:T(128)}, bf16[3,512,12,64]{1,3,2,0:T(8,128)(2,1)S(1)}, f32[3,12,512]{2,1,0:T(8,128)}, bf16[3,512,12,64]{1,3,2,0:T(8,128)(2,1)}, bf16[3,512,1...) while((s32[]{:T(128)}, ...), condition=%wide.region_4.5_spmd, body=%wide.region_1.4_spmd.sunk | while | flops 827713536 | bytes 53693012 | solution.py:91
  184.2 41.0 %all_to_all.20 = bf16[8,4,60,768]{3,1,2,0:T(4,128)(2,1)} all-to-all(bf16[8,4,60,768]{3,1,2,0:T(4,128)(2,1)S(1)} %copy.151), channel_id=1, replica_groups=mesh['exp'=8,'dp'=4] {'exp'}, dimensions={0} | all-to-all | bytes 5898240 | tf_op jit(solution)/shard_map/all_to_all | solution.py:119
  225.2 19.6 %fusion.94 = f32[4,8,60,3072]{3,2,1,0:T(8,128)} fusion(bf16[4,768,3072]{2,1,0:T(8,128)(2,1)} %param.29, bf16[8,4,60,768]{3,1,2,0:T(4,128)(2,1)} %all_to_all.20), kind=kOutput, calls=%fused_computation.91 | convolution fusion | flops 9059696640 | bytes 45416448 | tf_op jit(solution)/shard_map/sekd,edf->sekf/dot_general | solution.py:122
  244.8 22.6 %convert_bitcast_fusion.1 = bf16[8,4,60,768]{3,2,0,1:T(8,128)(2,1)} fusion(bf16[4,3072,768]{2,1,0:T(8,128)(2,1)} %param.30, f32[4,8,60,3072]{3,2,1,0:T(8,128)} %fusion.94), kind=kOutput, calls=%fused_computation.139 | convolution fusion | flops 9114255360 | bytes 45416448 | tf_op jit(solution)/shard_map/sekf,efd->sekd/dot_general | solution.py:126
  289.7 23.6 %all-to-all-done.1 = bf16[8,4,60,768]{3,1,2,0:T(4,128)(2,1)} async-done(((bf16[8,4,60,768]{3,1,2,0:T(4,128)(2,1)}), bf16[8,4,60,768]{3,1,2,0:T(4,128)(2,1)}, u32[]{:S(2)}, u32[]{:S(2)}) %all-to-all-start.1) | async-done | bytes 2949152 | tf_op jit(solution)/shard_map/all_to_all | solution.py:129
  362.8 38.9 %all_to_all.21 = bf16[8,4,60,768]{3,1,2,0:T(4,128)(2,1)} all-to-all(bf16[8,4,60,768]{3,1,2,0:T(4,128)(2,1)S(1)} %copy.158), channel_id=1, replica_groups=mesh['exp'=8,'dp'=4] {'exp'}, dimensions={0} | all-to-all | bytes 5898240 | tf_op jit(solution)/shard_map/all_to_all | solution.py:134
  401.7 22.0 %bitcast_convert_fusion = bf16[4,3072,768]{2,1,0:T(8,128)(2,1)} fusion(bf16[8,4,60,768]{3,1,2,0:T(4,128)(2,1)} %all_to_all.21, f32[4,8,60,3072]{3,2,1,0:T(8,128)} %fusion.94), kind=kOutput, calls=%fused_computation.69 | convolution fusion | flops 9122217984 | bytes 45416448 | tf_op jit(solution)/shard_map/sekf,sekd->efd/dot_general | solution.py:155
  423.8 30.7 %fusion.87 = bf16[8,4,60,3072]{3,2,0,1:T(8,128)(2,1)} fusion(f32[4,8,60,3072]{3,2,1,0:T(8,128)} %fusion.94, bf16[4,3072,768]{2,1,0:T(8,128)(2,1)} %param.30, bf16[8,4,60,768]{3,1,2,0:T(4,128)(2,1)} %all_to_all.21), kind=kOutput, calls=%fused_computation.81 | convolution fusion | flops 9177661440 | bytes 57212928 | tf_op jit(solution)/shard_map/sekd,efd->sekf/dot_general | solution.py:141
  454.5 19.2 %bitcast_convert_fusion.1 = bf16[4,768,3072]{2,1,0:T(8,128)(2,1)} fusion(bf16[8,4,60,3072]{3,2,0,1:T(8,128)(2,1)} %fusion.87, bf16[8,4,60,768]{3,1,2,0:T(4,128)(2,1)} %all_to_all.20), kind=kOutput, calls=%fused_computation.70 | convolution fusion | flops 9069133824 | bytes 33619968 | tf_op jit(solution)/shard_map/sekd,sekf->edf/dot_general | solution.py:152
  473.8 18.0 %convert_bitcast_fusion = bf16[8,4,60,768]{3,2,0,1:T(8,128)(2,1)} fusion(bf16[8,4,60,3072]{3,2,0,1:T(8,128)(2,1)} %fusion.87, bf16[4,768,3072]{2,1,0:T(8,128)(2,1)} %param.29), kind=kOutput, calls=%fused_computation.138 | convolution fusion | flops 9061171200 | bytes 33619968 | tf_op jit(solution)/shard_map/sekf,edf->sekd/dot_general | solution.py:146
  509.9 28.1 %all-to-all-done.3 = bf16[8,4,60,768]{3,1,2,0:T(4,128)(2,1)} async-done(((bf16[8,4,60,768]{3,1,2,0:T(4,128)(2,1)}), bf16[8,4,60,768]{3,1,2,0:T(4,128)(2,1)}, u32[]{:S(2)}, u32[]{:S(2)}) %all-to-all-start.3) | async-done | bytes 2949152 | tf_op jit(solution)/shard_map/all_to_all | solution.py:150
  594.4 240.6 %while.30 = (s32[]{:T(128)}, bf16[3,512,12,64]{1,3,2,0:T(8,128)(2,1)}, bf16[3,512,12,64]{1,3,2,0:T(8,128)(2,1)}, bf16[3,512,12,64]{1,3,2,0:T(8,128)(2,1)}, f32[3...) while((s32[]{:T(128)}, ...), condition=%wide.region_16.18_spmd.clone, body=%wide.region_14.17_spmd.clone.sunk | while | flops 3271419904 | bytes 271193856 | solution.py:214
  603.5 10.6 multiply_reduce_fusion.5
  614.1 10.5 subtract_multiply_fusion.5
  633.0 33.7 %fusion.234 = f32[3,32,12]{1,2,0:T(8,128)} fusion(f32[3,32,12]{1,2,0:T(8,128)} %get-tuple-element.510, s32[]{:T(128)} %get-tuple-element.506, s32[512,512]{0,1:T(8,128)S(1)} %copy-done.4, f32[12,512,512]{1,2,0:T(8,128)} %copy-done.1), kind=kOutput, calls=%fused_computation.47.clone.1 | convolution fusion | flops 1224736768 | bytes 13640192 | tf_op jit(solution)/shard_map/while/body/eval_jaxpr/oxt,sxt->os/dot_general | solution.py:195
  683.5 10.7 multiply_reduce_fusion.5
  713.0 33.6 %fusion.234 = f32[3,32,12]{1,2,0:T(8,128)} fusion(f32[3,32,12]{1,2,0:T(8,128)} %get-tuple-element.510, s32[]{:T(128)} %get-tuple-element.506, s32[512,512]{0,1:T(8,128)S(1)} %copy-done.4, f32[12,512,512]{1,2,0:T(8,128)} %copy-done.1), kind=kOutput, calls=%fused_computation.47.clone.1 | convolution fusion | flops 1224736768 | bytes 13640192 | tf_op jit(solution)/shard_map/while/body/eval_jaxpr/oxt,sxt->os/dot_general | solution.py:195
  763.8 10.7 multiply_reduce_fusion.5
  793.3 33.6 %fusion.234 = f32[3,32,12]{1,2,0:T(8,128)} fusion(f32[3,32,12]{1,2,0:T(8,128)} %get-tuple-element.510, s32[]{:T(128)} %get-tuple-element.506, s32[512,512]{0,1:T(8,128)S(1)} %copy-done.4, f32[12,512,512]{1,2,0:T(8,128)} %copy-done.1), kind=kOutput, calls=%fused_computation.47.clone.1 | convolution fusion | flops 1224736768 | bytes 13640192 | tf_op jit(solution)/shard_map/while/body/eval_jaxpr/oxt,sxt->os/dot_general | solution.py:195
  884.5 46.1 %all-reduce = (f32[768]{0:T(1024)}, f32[768]{0:T(1024)}, f32[32,12]{0,1:T(8,128)}) all-reduce(f32[768]{0:T(1024)S(1)} %get-tuple-element.275, f32[768]{0:T(1024)S(1)} %copy-done.49, f32[32,12]{0,1:T(8,128)S(1)} %reduce_sum.130), channel_id=1, replica_groups=mesh['exp'=8,'dp'=4] {'exp','dp'}, use_global_device_ids=true, to_apply=%region_23.25 | all-reduce | flops 1920 | bytes 15360 | tf_op jit(solution)/shard_map/psum | solution.py:240
  937.5 163.0 %reduce-scatter.3.cloned.1.call-done = bf16[4,768,768]{2,1,0:T(8,128)(2,1)} async-done(((bf16[4,768,3072]{2,1,0:T(8,128)(2,1)}), bf16[4,768,768]{2,1,0:T(8,128)(2,1)}) %reduce-scatter.3.cloned.1.call-update) | async-done | bytes 4718608 | tf_op jit(solution)/shard_map/reduce_scatter | solution.py:159
  1107.3 122.9 %all-reduce.4.cloned.1.call-done = (f32[768,768]{1,0:T(8,128)}, f32[768,768]{1,0:T(8,128)}, f32[768,768]{1,0:T(8,128)}, f32[768,768]{1,0:T(8,128)}, f32[768,32]{0,1:T(8,128)}) async-done(((f32[768,768]{1,0:T(8,128)}, f32[768,768]{1,0:T(8,128)}, f32[768,768]{1,0:T(8,128)}, f32[768,768]{1,0:T(8,128)}, f32[768,32]{0,1:T(8,128)}), (f32[768,768]{1,0:T(8,128)}, f32[768,768]{1,0:T(8,128)}, f32[768,768]{1,0:T(8,128)}, ...) | async-done | bytes 9535504 | tf_op jit(solution)/shard_map/psum | solution.py:240
  (278 shorter events, 458.1 us)
Async XLA Ops:
  8.5 69.2 %copy-start.3 = (s32[512,512]{0,1:T(8,128)}, s32[512,512]{0,1:T(8,128)S(1)}, u32[]{:S(2)}) copy-start(s32[512,512]{0,1:T(8,128)S(1)} %fusion.144) | copy-start | bytes 3145732
  15.3 41.6 %copy-start.42 = (f32[1536]{0:T(1024)}, f32[1536]{0:T(1024)S(1)}, u32[]{:S(2)}) copy-start(f32[1536]{0:T(1024)S(1)} %add_rsqrt_fusion.1) | copy-start | bytes 18436
  155.5 127.1 %copy-start.28 = (f32[1536]{0:T(1024)}, f32[1536]{0:T(1024)S(1)}, u32[]{:S(2)}) copy-start(f32[1536]{0:T(1024)S(1)} %add_rsqrt_fusion) | copy-start | bytes 18436
  155.5 132.9 %copy-start.32 = (s32[1536]{0:T(1024)}, s32[1536]{0:T(1024)S(1)}, u32[]{:S(2)}) copy-start(s32[1536]{0:T(1024)S(1)} %reduce) | copy-start | bytes 18436
  164.8 19.4 %copy-start.53 = (s32[1536]{0:T(1024)}, s32[1536]{0:T(1024)S(1)}, u32[]{:S(2)}) copy-start(s32[1536]{0:T(1024)S(1)} %fusion.161) | copy-start | bytes 18436
  273.1 40.2 %all-to-all-start.1 = ((bf16[8,4,60,768]{3,1,2,0:T(4,128)(2,1)}), bf16[8,4,60,768]{3,1,2,0:T(4,128)(2,1)}, u32[]{:S(2)}, u32[]{:S(2)}) async-start(bf16[8,4,60,768]{3,1,2,0:T(4,128)(2,1)} %copy.153), calls=%async_computation.1 | async-start | bytes 5898240 | tf_op jit(solution)/shard_map/all_to_all | solution.py:129
  277.5 653.0 %reduce-scatter.5.cloned.1.call-start = ((), (), s32[]{:S(2)}) async-start(), calls=%async_computation.7 | async-start | bytes 23592960 | tf_op jit(solution)/shard_map/reduce_scatter | solution.py:162
  280.7 55.2 %copy-start.9 = (bf16[1536,768]{0,1:T(8,128)(2,1)}, bf16[1536,768]{0,1:T(8,128)(2,1)S(1)}, u32[]{:S(2)}) copy-start(bf16[1536,768]{0,1:T(8,128)(2,1)S(1)} %copy.156) | copy-start | bytes 7077892
  289.7 46.2 %copy-start.34 = (f32[1536]{0:T(1024)}, f32[1536]{0:T(1024)S(1)}, u32[]{:S(2)}) copy-start(f32[1536]{0:T(1024)S(1)} %select_reduce_fusion) | copy-start | bytes 18436
  289.7 33.0 %copy-start.40 = (s32[2048]{0:T(1024)S(1)}, s32[2048]{0:T(1024)}, u32[]{:S(2)}) copy-start(s32[2048]{0:T(1024)} %pad_clamp_fusion) | copy-start | bytes 24580
  423.7 676.7 %reduce-scatter.3.cloned.1.call-start = ((), (), s32[]{:S(2)}) async-start(), calls=%async_computation.6 | async-start | bytes 23592960 | tf_op jit(solution)/shard_map/reduce_scatter | solution.py:159
  491.8 10.5 copy-start.35
  491.8 10.5 copy-start.45
  491.8 10.5 copy-start.18
  491.8 10.5 copy-start.29
  491.8 10.5 copy-start.31
  491.8 10.5 copy-start.33
  491.8 10.5 copy-start.37
  491.8 10.5 copy-start.38
  497.7 40.2 %all-to-all-start.3 = ((bf16[8,4,60,768]{3,1,2,0:T(4,128)(2,1)}), bf16[8,4,60,768]{3,1,2,0:T(4,128)(2,1)}, u32[]{:S(2)}, u32[]{:S(2)}) async-start(bf16[8,4,60,768]{3,1,2,0:T(4,128)(2,1)} %copy.160), calls=%async_computation.3 | async-start | bytes 5898240 | tf_op jit(solution)/shard_map/all_to_all | solution.py:150
  502.2 728.1 %all-reduce.4.cloned.1.call-start = ((), (), s32[]{:S(2)}) async-start(), calls=%async_computation.8 | async-start | bytes 19070976 | tf_op jit(solution)/shard_map/psum | solution.py:240
  509.9 37.8 %copy-start.41 = (s32[2048]{0:T(1024)S(1)}, s32[2048]{0:T(1024)}, u32[]{:S(2)}) copy-start(s32[2048]{0:T(1024)} %pad_clamp_fusion) | copy-start | bytes 24580
  556.6 12.7 %slice-start = ((s8[4718592]{0:T(1024)(128)(4,1)}), s8[524288]{0:T(1024)(128)(4,1)S(1)}, s32[]{:S(2)}) async-start(s8[4718592]{0:T(1024)(128)(4,1)} %bitcast.208), calls=%async_computation.9 | async-start | bytes 1048576
  839.6 15.3 %copy-start.24 = (bf16[96,8,3,512]{3,1,2,0:T(8,128)(2,1)}, bf16[96,8,3,512]{3,1,2,0:T(8,128)(2,1)S(1)}, u32[]{:S(2)}) copy-start(bf16[96,8,3,512]{3,1,2,0:T(8,128)(2,1)S(1)} %copy.201) | copy-start | bytes 7077892
  (56 other events, 295.1 us)
Sparse Core Ops, SparseCore 0:
  423.9 313.1 reduce-scatter.4
  739.4 360.9 reduce-scatter.2
Sparse Core Ops, SparseCore 1:
  862.3 368.0 all-reduce.3
where the time goes:
time: 1260 us; the launch traced here: 1250 us
  matrix products  450 us (36%)
  waiting for transfers between devices  338 us (27%)
  local copies, waits for them, and re-layouts  230 us (18%)
  blocking collectives  126 us (10%)
  other arithmetic  76 us (6%)
  between operations  16.7 us (1%)
    reduce_scatter x1, waiting for transfers between devices, per_device(): lax.psum_scatter(first_term.astype(jnp.bfloat16), 'dp', scatter_dimension...  163 us
    psum x1, waiting for transfers between devices, per_device(): lax.psum((query_part, key_part, value_part, output_part, norm_attn_part,...  123 us
    dot_general x3, matrix products, attend_back(): jnp.einsum('oxt,sxt->os', bucket_indicator, scores_gradient, precision=FU...  101 us
    dot_general x6, matrix products, score_block(): jnp.einsum('qhd,khd->hqk', q_block, k_block, preferred_element_type=jnp.f...  52.8 us
    psum x1, blocking collectives, per_device(): lax.psum((query_part, key_part, value_part, output_part, norm_attn_part,...  46.1 us
    while x5, local copies, waits for them, and re-layouts, per_device(): lax.map(attention_forward, (per_seq(query), per_seq(keys), per_seq(values)))  41.9 us
    all_to_all x1, blocking collectives, per_device(): lax.all_to_all(to_buffer(normed_ffn.astype(jnp.bfloat16)), 'exp', split_a...  41 us
    all_to_all x1, blocking collectives, per_device(): lax.all_to_all(to_buffer((gate * upstream).astype(jnp.bfloat16)), 'exp',...  38.9 us
  transfers between devices with their start and end apart: 5, of which 4 were waited for; matrix products, arithmetic and copies ran while one was open for 36% of the time, Pallas kernels for 0%

commit v1 on v0

v1 whole, which is shorter than its diff:
```python
import functools

import jax
import jax.numpy as jnp
from jax import lax
from jax.experimental import pallas as pl
from jax.experimental.pallas import tpu as pltpu
from jax.sharding import PartitionSpec as P

HEADS = 12
HEAD_DIM = 64
SEQ = 512
LIMITS = (12, 16, 23, 32, 46, 64, 91)
EPSILON = 1e-06
FULL_PRECISION = lax.Precision.HIGHEST
BF = jnp.bfloat16
F32 = jnp.float32
PAIR = 2 * HEAD_DIM
TILE = 128
CHUNK = 256
GELU_A = 0.7978845608028654
GELU_B = 0.044715 * GELU_A
VMEM_MIB = 50


def params(**more):
    return pltpu.CompilerParams(vmem_limit_bytes=VMEM_MIB * 2**20, **more)


def mm(left, right):
    return jnp.dot(left, right, preferred_element_type=F32)


def mm_nt(left, right):
    return lax.dot_general(left, right, (((1,), (1,)), ((), ())), preferred_element_type=F32)


def bucket_of(offset):
    distance = jnp.abs(offset)
    farther = jnp.zeros_like(distance)
    for limit in LIMITS:
        farther = farther + (distance >= limit).astype(jnp.int32)
    return jnp.where(distance < 8, distance, 8 + farther) + jnp.where(offset > 0, 16, 0)


def diagonal_onehot(count):
    places = jnp.arange(TILE, dtype=jnp.int32)
    offsets = jnp.concatenate([-places, TILE - places, 0 * places - SEQ, 0 * places + SEQ])
    return (bucket_of(offsets)[:, None] == jnp.arange(count, dtype=jnp.int32)[None, :]).astype(F32)


def dispatch_kernel(slot_ref, rows_ref, out_ref):
    block, tokens = out_ref.shape[0], rows_ref.shape[0]
    ids = lax.broadcasted_iota(jnp.int32, (block, tokens), 0) + pl.program_id(0) * block
    picks = jnp.where(slot_ref[...] == ids, 1.0, 0.0).astype(BF)
    out_ref[...] = mm(picks, rows_ref[...]).astype(BF)


def dispatch_gate_kernel(experts, capacity, padded, slot_ref, gate_ref, rows_ref, out_ref):
    block, tokens = out_ref.shape[0], rows_ref.shape[0]
    width = out_ref.shape[1]
    step = pl.program_id(0)
    ids = lax.broadcasted_iota(jnp.int32, (block, tokens), 0) + step * block
    picks = jnp.where(slot_ref[...] == ids, 1.0, 0.0).astype(BF)
    out = mm(picks, rows_ref[...])
    gates = jnp.broadcast_to(gate_ref[...].astype(BF), (8, tokens))
    lanes = pl.num_programs(0) * padded
    in_slots = mm_nt(gates, picks)
    in_slots = jnp.concatenate([in_slots, jnp.zeros((8, lanes - block), F32)], axis=1)
    lane = lax.broadcasted_iota(jnp.int32, (8, lanes), 1)
    row = lax.broadcasted_iota(jnp.int32, (block, 1), 0)
    left = out[:, :lanes]
    for expert in range(experts):
        shift = lax.rem(step * padded - expert * padded + lanes, lanes)
        moved = pltpu.roll(in_slots, shift, 1)
        mine = (lane >= step * padded) & (lane < step * padded + capacity)
        moved = jnp.where(mine, moved, 0.0)[:1]
        left = jnp.where(row == expert * padded + capacity, moved, left)
    out_ref[:, :lanes] = left.astype(BF)
    out_ref[:, lanes:] = out[:, lanes:].astype(BF)


def dispatch(slot_row, rows, blocks, block, gate=None):
    tokens, width = rows.shape
    grid_spec = dict(
        grid=(blocks,),
        out_specs=pl.BlockSpec((block, width), lambda k: (k, 0)),
        out_shape=jax.ShapeDtypeStruct((blocks * block, width), BF),
    )
    line = pl.BlockSpec((1, tokens), lambda k: (0, 0))
    full = pl.BlockSpec((tokens, width), lambda k: (0, 0))
    cost = pl.CostEstimate(
        flops=2 * blocks * block * tokens * width,
        bytes_accessed=2 * width * (tokens + blocks * block),
        transcendentals=0,
    )
    if gate is None:
        return pl.pallas_call(
            dispatch_kernel, in_specs=[line, full], compiler_params=params(), cost_estimate=cost, **grid_spec
        )(slot_row, rows)
    values, experts, capacity, padded = gate
    return pl.pallas_call(
        functools.partial(dispatch_gate_kernel, experts, capacity, padded),
        in_specs=[line, line, full],
        compiler_params=params(),
        cost_estimate=cost,
        **grid_spec,
    )(slot_row, values, rows)


def qkv_kernel(x_ref, gain_ref, wq_ref, wk_ref, wv_ref, q_ref, k_ref, v_ref):
    rows = x_ref[...].astype(F32)
    inv = lax.rsqrt(jnp.mean(rows * rows, axis=-1, keepdims=True) + EPSILON)
    normed = (rows * inv * gain_ref[...]).astype(BF)
    q_ref[...] = (mm(normed, wq_ref[...]).astype(BF).astype(F32) * HEAD_DIM**-0.5).astype(BF)
    k_ref[...] = mm(normed, wk_ref[...]).astype(BF)
    v_ref[...] = mm(normed, wv_ref[...]).astype(BF)


def qkv(x, gain, wq, wk, wv):
    tokens, width = x.shape
    rows = pl.BlockSpec((SEQ, width), lambda t: (t, 0))
    square = pl.BlockSpec((width, width), lambda t: (0, 0))
    one = pl.BlockSpec((1, width), lambda t: (0, 0))
    return pl.pallas_call(
        qkv_kernel,
        grid=(tokens // SEQ,),
        in_specs=[rows, one, square, square, square],
        out_specs=[rows] * 3,
        out_shape=[jax.ShapeDtypeStruct((tokens, width), BF)] * 3,
        compiler_params=params(),
        cost_estimate=pl.CostEstimate(
            flops=6 * tokens * width * width, bytes_accessed=8 * tokens * width, transcendentals=0
        ),
    )(x, gain, wq, wk, wv)


def fill_bias(lines_ref, bias_ref):
    upper_right = lax.broadcasted_iota(jnp.int32, (TILE, TILE), 0) <= lax.broadcasted_iota(
        jnp.int32, (TILE, TILE), 1
    )
    tiles = SEQ // TILE
    for head in range(2):

        def sheared(line):
            whole = jnp.broadcast_to(lines_ref[head, line : line + 1, :], (TILE, TILE))
            return pltpu.roll(whole, 0, 1, stride=1, stride_axis=0)

        negative, positive = sheared(0), sheared(1)
        far_negative = jnp.broadcast_to(lines_ref[head, 2:3, :], (TILE, TILE))
        far_positive = jnp.broadcast_to(lines_ref[head, 3:4, :], (TILE, TILE))
        same = jnp.where(upper_right, negative, positive)
        above = jnp.where(upper_right, positive, far_positive)
        below = jnp.where(upper_right, far_negative, negative)
        for key in range(tiles):
            for query in range(tiles):
                gap = key - query
                tile = (
                    same
                    if gap == 0
                    else above
                    if gap == 1
                    else below
                    if gap == -1
                    else far_positive
                    if gap > 0
                    else far_negative
                )
                bias_ref[head, pl.ds(key * TILE, TILE), pl.ds(query * TILE, TILE)] = tile


def head_lanes(head):
    lane = lax.broadcasted_iota(jnp.int32, (1, PAIR), 1)
    return (lane >= head * HEAD_DIM) & (lane < (head + 1) * HEAD_DIM)


def only(head, array):
    return jnp.where(head_lanes(head), array, jnp.zeros_like(array))


def attention_kernel(lines_ref, q_ref, k_ref, v_ref, o_ref, lse_ref, bias_ref):
    @pl.when(pl.program_id(1) == 0)
    def _():
        fill_bias(lines_ref, bias_ref)

    keys = k_ref[...]
    values_t = v_ref[...].T
    masked = [only(head, keys) for head in range(2)]
    row = lax.broadcasted_iota(jnp.int32, (PAIR, 1), 0)
    for part in range(SEQ // CHUNK):
        places = pl.ds(part * CHUNK, CHUNK)
        queries = q_ref[places, :]
        out = None
        for head in range(2):
            scores = mm_nt(masked[head], queries) + bias_ref[head, :, places]
            highest = jnp.max(scores, axis=0, keepdims=True)
            weights = jnp.exp(scores - highest)
            total = jnp.sum(weights, axis=0, keepdims=True)
            lse_ref[0, 0, head : head + 1, places] = highest + jnp.log(total)
            mixed = mm(values_t, weights.astype(BF)) * (1.0 / total)
            out = mixed if out is None else jnp.where(row < HEAD_DIM, out, mixed)
        o_ref[places, :] = out.T.astype(BF)


def attention(lines, q, k, v):
    tokens, width = q.shape
    seqs, pairs = tokens // SEQ, width // PAIR
    block = pl.BlockSpec((SEQ, PAIR), lambda h, s: (s, h))
    return pl.pallas_call(
        attention_kernel,
        grid=(pairs, seqs),
        in_specs=[pl.BlockSpec((2, 8, TILE), lambda h, s: (h, 0, 0)), block, block, block],
        out_specs=[block, pl.BlockSpec((1, 1, 2, SEQ), lambda h, s: (h, s, 0, 0))],
        out_shape=[
            jax.ShapeDtypeStruct((tokens, width), BF),
            jax.ShapeDtypeStruct((pairs, seqs, 2, SEQ), F32),
        ],
        scratch_shapes=[pltpu.VMEM((2, SEQ, SEQ), F32)],
        compiler_params=params(),
        cost_estimate=pl.CostEstimate(
            flops=16 * pairs * seqs * SEQ * SEQ * PAIR,
            bytes_accessed=8 * tokens * width,
            transcendentals=2 * pairs * seqs * SEQ * SEQ,
        ),
    )(lines, q, k, v)


def attention_back_kernel(
    lines_ref, q_ref, k_ref, v_ref, do_ref, lse_ref, dq_ref, dk_ref, dv_ref, sums_ref, bias_ref, diag_ref
):
    seq = pl.program_id(1)

    @pl.when(seq == 0)
    def _():
        fill_bias(lines_ref, bias_ref)
        diag_ref[...] = jnp.zeros_like(diag_ref)

    keys, values = k_ref[...], v_ref[...]
    keys_t = keys.T
    masked_k = [only(head, keys) for head in range(2)]
    masked_v = [only(head, values) for head in range(2)]
    row = lax.broadcasted_iota(jnp.int32, (PAIR, 1), 0)
    grads_k, grads_v = [None, None], [None, None]
    tiles = SEQ // TILE
    for part in range(SEQ // CHUNK):
        places = pl.ds(part * CHUNK, CHUNK)
        queries, upstream = q_ref[places, :], do_ref[places, :]
        grad_q = None
        for head in range(2):
            scores = mm_nt(masked_k[head], queries) + bias_ref[head, :, places]
            weights = jnp.exp(scores - lse_ref[0, 0, head : head + 1, places])
            products = weights * mm_nt(masked_v[head], upstream)
            scores_grad = products - weights * jnp.sum(products, axis=0, keepdims=True)
            low = scores_grad.astype(BF)
            value_term = mm(weights.astype(BF), upstream)
            key_term = mm(low, queries)
            grads_v[head] = value_term if part == 0 else grads_v[head] + value_term
            grads_k[head] = key_term if part == 0 else grads_k[head] + key_term
            query_term = mm(keys_t, low)
            grad_q = query_term if head == 0 else jnp.where(row < HEAD_DIM, grad_q, query_term)
            groups = {}
            for query in range(CHUNK // TILE):
                for key in range(tiles):
                    gap = key - (query + part * (CHUNK // TILE))
                    kind = 0 if gap == 0 else 1 if gap == 1 else 2 if gap == -1 else 3 if gap > 0 else 4
                    tile = scores_grad[
                        key * TILE : (key + 1) * TILE, query * TILE : (query + 1) * TILE
                    ]
                    groups[kind] = tile if kind not in groups else groups[kind] + tile
            for kind, tile in groups.items():
                diag_ref[head, kind] += tile
        dq_ref[places, :] = (grad_q * HEAD_DIM**-0.5).T.astype(BF)
    first = head_lanes(0)
    dk_ref[...] = jnp.where(first, grads_k[0], grads_k[1]).astype(BF)
    dv_ref[...] = jnp.where(first, grads_v[0], grads_v[1]).astype(BF)

    @pl.when(seq == pl.num_programs(1) - 1)
    def _():
        upper_right = lax.broadcasted_iota(jnp.int32, (TILE, TILE), 0) <= lax.broadcasted_iota(
            jnp.int32, (TILE, TILE), 1
        )
        sums_ref[...] = jnp.zeros_like(sums_ref)
        for head in range(2):
            same, above, below = diag_ref[head, 0], diag_ref[head, 1], diag_ref[head, 2]

            def gathered(array):
                row_id = lax.broadcasted_iota(jnp.int32, (TILE, 1), 0)
                bit = 1
                while bit < TILE:
                    turned = pltpu.roll(array, TILE - bit, 1)
                    array = jnp.where((row_id & bit) != 0, turned, array)
                    bit *= 2
                return jnp.sum(array, axis=0, keepdims=True)

            zero = jnp.zeros_like(same)
            sums_ref[head, 0:1, :] = gathered(jnp.where(upper_right, same, below))
            sums_ref[head, 1:2, :] = gathered(jnp.where(upper_right, above, same))
            sums_ref[head, 2:3, :] = jnp.sum(
                diag_ref[head, 4] + jnp.where(upper_right, below, zero), axis=0, keepdims=True
            )
            sums_ref[head, 3:4, :] = jnp.sum(
                diag_ref[head, 3] + jnp.where(upper_right, zero, above), axis=0, keepdims=True
            )


def attention_back(lines, q, k, v, do, lse):
    tokens, width = q.shape
    seqs, pairs = tokens // SEQ, width // PAIR
    block = pl.BlockSpec((SEQ, PAIR), lambda h, s: (s, h))
    lines_spec = pl.BlockSpec((2, 8, TILE), lambda h, s: (h, 0, 0))
    return pl.pallas_call(
        attention_back_kernel,
        grid=(pairs, seqs),
        in_specs=[lines_spec, block, block, block, block]
        + [pl.BlockSpec((1, 1, 2, SEQ), lambda h, s: (h, s, 0, 0))],
        out_specs=[block, block, block, lines_spec],
        out_shape=[jax.ShapeDtypeStruct((tokens, width), BF)] * 3
        + [jax.ShapeDtypeStruct((2 * pairs, 8, TILE), F32)],
        scratch_shapes=[pltpu.VMEM((2, SEQ, SEQ), F32), pltpu.VMEM((2, 5, TILE, TILE), F32)],
        compiler_params=params(),
        cost_estimate=pl.CostEstimate(
            flops=40 * pairs * seqs * SEQ * SEQ * PAIR,
            bytes_accessed=14 * tokens * width,
            transcendentals=2 * pairs * seqs * SEQ * SEQ,
        ),
    )(lines, q, k, v, do, lse)


def router_kernel(
    o_ref, x_ref, wo_ref, gain_ref, wr_ref, expert_ref, h_ref, u_ref, probs_ref, gate_ref, line_ref
):
    mixed = x_ref[...].astype(F32) + mm(o_ref[...], wo_ref[...])
    h_ref[...] = mixed
    inv = lax.rsqrt(jnp.mean(mixed * mixed, axis=-1, keepdims=True) + EPSILON)
    normed = mixed * inv * gain_ref[...]
    u_ref[...] = normed.astype(BF)
    logits = jnp.dot(normed, wr_ref[...], precision=FULL_PRECISION, preferred_element_type=F32)
    spread = jnp.exp(logits - jnp.max(logits, axis=-1, keepdims=True))
    probs = spread / jnp.sum(spread, axis=-1, keepdims=True)
    probs_ref[...] = probs
    picked = expert_ref[...] == lax.broadcasted_iota(jnp.int32, probs.shape, 1)
    gate = jnp.sum(jnp.where(picked, probs, 0.0), axis=-1, keepdims=True)
    gate_ref[...] = gate
    size = gate.shape[0]
    diagonal = lax.broadcasted_iota(jnp.int32, (size, size), 0) == lax.broadcasted_iota(
        jnp.int32, (size, size), 1
    )
    line_ref[...] = jnp.sum(jnp.where(diagonal, gate, 0.0), axis=0, keepdims=True)


def router(o, x, wo, gain, wr, expert):
    tokens, width = x.shape
    experts = wr.shape[1]
    size = 256

    def rows(columns):
        return pl.BlockSpec((size, columns), lambda t: (t, 0))

    def whole(*shape):
        return pl.BlockSpec(shape, lambda t: (0, 0))

    return pl.pallas_call(
        router_kernel,
        grid=(tokens // size,),
        in_specs=[rows(width), rows(width), whole(width, width), whole(1, width)]
        + [whole(width, experts), rows(1)],
        out_specs=[rows(width), rows(width), rows(experts), rows(1)]
        + [pl.BlockSpec((1, size), lambda t: (0, t))],
        out_shape=[
            jax.ShapeDtypeStruct((tokens, width), F32),
            jax.ShapeDtypeStruct((tokens, width), BF),
            jax.ShapeDtypeStruct((tokens, experts), F32),
            jax.ShapeDtypeStruct((tokens, 1), F32),
            jax.ShapeDtypeStruct((1, tokens), F32),
        ],
        compiler_params=params(),
        cost_estimate=pl.CostEstimate(
            flops=2 * tokens * width * width, bytes_accessed=10 * tokens * width, transcendentals=0
        ),
    )(o, x, wo, gain, wr, expert)


def gelu_and_slope(z):
    square = z * z
    half = 0.5 + 0.5 * jnp.tanh(z * (GELU_A + GELU_B * square))
    value = z * half
    slope = half + 2.0 * value * (1.0 - half) * (GELU_A + 3.0 * GELU_B * square)
    return value, slope


def expert_kernel(parts, u_ref, c_ref, first_ref, second_ref, e_ref, d_ref, e_sum, d_sum):
    step = pl.program_id(1)
    rows, upstream = u_ref[0], c_ref[0]
    columns = first_ref.shape[2] // parts

    @pl.when(step == 0)
    def _():
        e_sum[...] = jnp.zeros_like(e_sum)
        d_sum[...] = jnp.zeros_like(d_sum)

    for part in range(parts):
        places = slice(part * columns, (part + 1) * columns)
        first, second = first_ref[0, :, places], second_ref[0, places, :]
        value, slope = gelu_and_slope(mm(rows, first))
        inner = (mm_nt(upstream, second) * slope).astype(BF)
        e_sum[...] += mm(value.astype(BF), second)
        d_sum[...] += mm_nt(inner, first)

    @pl.when(step == pl.num_programs(1) - 1)
    def _():
        e_ref[0] = e_sum[...].astype(BF)
        d_ref[0] = d_sum[...].astype(BF)


def expert_pass(u, c, w_in, w_out):
    experts, rows, width = u.shape
    hidden = w_in.shape[2]
    size = 768
    block = pl.BlockSpec((1, rows, width), lambda e, f: (e, 0, 0))
    return pl.pallas_call(
        functools.partial(expert_kernel, 3),
        grid=(experts, hidden // size),
        in_specs=[
            block,
            block,
            pl.BlockSpec((1, width, size), lambda e, f: (e, 0, f)),
            pl.BlockSpec((1, size, width), lambda e, f: (e, f, 0)),
        ],
        out_specs=[block, block],
        out_shape=[jax.ShapeDtypeStruct(u.shape, BF)] * 2,
        scratch_shapes=[pltpu.VMEM((rows, width), F32)] * 2,
        compiler_params=params(),
        cost_estimate=pl.CostEstimate(
            flops=8 * experts * rows * width * hidden,
            bytes_accessed=4 * experts * width * (hidden + 2 * rows),
            transcendentals=experts * rows * hidden,
        ),
    )(u, c, w_in, w_out)


def weights_kernel(parts, sources, capacity, padded, place_ref, *refs):
    u_refs, c_refs = refs[:sources], refs[sources : 2 * sources]
    first_ref, second_ref, own_in, own_out, far_in, far_out, in_sum, out_sum = refs[2 * sources :]
    width, size = first_ref.shape[1:]
    rows = u_refs[0].shape[1]
    columns = size // parts
    first_t = first_ref[0].T
    for source in range(sources):
        inputs, upstream = u_refs[source][0], c_refs[source][0]
        gate = jnp.zeros((1, rows), F32)
        for block in range(rows // padded):
            place = block * padded + capacity
            gate = gate + inputs[place : place + 1, :rows].astype(F32)
        for part in range(parts):
            places = slice(part * columns, (part + 1) * columns)
            value, slope = gelu_and_slope(mm_nt(first_t[places, :], inputs))
            inner = (mm_nt(second_ref[0, places, :], upstream) * (slope * gate)).astype(BF)
            in_term = mm(inner, inputs)
            out_term = mm((value * gate).astype(BF), upstream)
            if source == 0:
                in_sum[places, :] = in_term
                out_sum[places, :] = out_term
            else:
                in_sum[places, :] += in_term
                out_sum[places, :] += out_term
    mine = pl.program_id(1) == place_ref[2]

    @pl.when(mine)
    def _():
        own_in[0] = in_sum[...].T
        own_out[0] = out_sum[...]

    @pl.when(jnp.logical_not(mine))
    def _():
        far_in[0] = in_sum[...].T.astype(BF)
        far_out[0] = out_sum[...].astype(BF)


def weight_grads(place, us, cs, w_in, w_out, size, capacity, padded):
    sources = len(us)
    experts, rows, width = us[0].shape
    local = w_in.shape[0]
    block = pl.BlockSpec((1, rows, width), lambda e, f, p: (e, 0, 0))
    tile = pl.BlockSpec((1, width, size), lambda e, f, p: (e, 0, 0))
    turned = pl.BlockSpec((1, size, width), lambda e, f, p: (e, 0, 0))
    return pl.pallas_call(
        functools.partial(weights_kernel, 3, sources, capacity, padded),
        grid_spec=pltpu.PrefetchScalarGridSpec(
            num_scalar_prefetch=1,
            grid=(experts, 2),
            in_specs=[block] * (2 * sources)
            + [
                pl.BlockSpec((1, width, size), lambda e, f, p: (p[0] + e, 0, p[1] + f)),
                pl.BlockSpec((1, size, width), lambda e, f, p: (p[0] + e, p[1] + f, 0)),
            ],
            out_specs=[
                pl.BlockSpec((1, width, size), lambda e, f, p: (p[0] + e, 0, 0)),
                pl.BlockSpec((1, size, width), lambda e, f, p: (p[0] + e, 0, 0)),
                tile,
                turned,
            ],
            scratch_shapes=[pltpu.VMEM((size, width), F32)] * 2,
        ),
        out_shape=[
            jax.ShapeDtypeStruct((local, width, size), F32),
            jax.ShapeDtypeStruct((local, size, width), F32),
            jax.ShapeDtypeStruct((experts, width, size), BF),
            jax.ShapeDtypeStruct((experts, size, width), BF),
        ],
        compiler_params=params(),
        cost_estimate=pl.CostEstimate(
            flops=16 * sources * experts * rows * width * size,
            bytes_accessed=4 * experts * (sources * rows * width + 6 * size * width),
            transcendentals=2 * sources * experts * rows * size,
        ),
    )(place, *us, *cs, w_in, w_out)


def finish_kernel(place_ref, a_ref, b_ref, x_ref, y_ref, a_out, b_out):
    a_out[...] = x_ref[...].astype(F32)
    b_out[...] = y_ref[...].astype(F32)


def finish(place, own_in, own_out, came_in, came_out):
    experts, width, size = came_in.shape

    def spec(shape, moved):
        return pl.BlockSpec((1,) + shape, lambda e, p: ((p[0] if moved else 0) + e, 0, 0))

    return pl.pallas_call(
        finish_kernel,
        grid_spec=pltpu.PrefetchScalarGridSpec(
            num_scalar_prefetch=1,
            grid=(experts,),
            in_specs=[pl.BlockSpec(memory_space=pl.ANY)] * 2
            + [spec((width, size), False), spec((size, width), False)],
            out_specs=[spec((width, size), True), spec((size, width), True)],
        ),
        out_shape=[
            jax.ShapeDtypeStruct(own_in.shape, F32),
            jax.ShapeDtypeStruct(own_out.shape, F32),
        ],
        input_output_aliases={1: 0, 2: 1},
        compiler_params=params(),
    )(place, own_in, own_out, came_in, came_out)


def combine_kernel(
    slot_ref, expert_ref, gate_ref, probs_ref, h_ref, c_ref, o_ref, e_ref, d_ref, wo_ref, wr_ref, gain_ref,
    mixed_ref, dh_ref, do_ref, wo_sum, wr_sum, gain_sum,
):
    step = pl.program_id(0)
    tokens, slots = slot_ref.shape[0], e_ref.shape[0]
    picks = jnp.where(
        slot_ref[...] == lax.broadcasted_iota(jnp.int32, (tokens, slots), 1), 1.0, 0.0
    ).astype(BF)
    returned, arrived = mm(picks, e_ref[...]), mm(picks, d_ref[...])
    gate, probs, mixed = gate_ref[...], probs_ref[...], h_ref[...]
    upstream = c_ref[...].astype(F32)
    mixed_ref[...] = (mixed + gate * returned).astype(BF)
    gate_grad = jnp.sum(upstream * returned, axis=-1, keepdims=True)
    picked = jnp.where(expert_ref[...] == lax.broadcasted_iota(jnp.int32, probs.shape, 1), 1.0, 0.0)
    logit_grad = gate_grad * gate * (picked - probs)
    inv = lax.rsqrt(jnp.mean(mixed * mixed, axis=-1, keepdims=True) + EPSILON)
    unit = mixed * inv
    gain = gain_ref[...]
    normed_grad = (
        lax.dot_general(
            logit_grad,
            wr_ref[...],
            (((1,), (1,)), ((), ())),
            precision=FULL_PRECISION,
            preferred_element_type=F32,
        )
        + gate * arrived
    )
    unit_grad = normed_grad * gain
    mixed_grad = upstream + inv * (
        unit_grad - unit * jnp.mean(unit_grad * unit, axis=-1, keepdims=True)
    )
    dh_ref[...] = mixed_grad
    low = mixed_grad.astype(BF)
    do_ref[...] = mm_nt(low, wo_ref[...]).astype(BF)

    @pl.when(step == 0)
    def _():
        wo_sum[...] = jnp.zeros_like(wo_sum)
        wr_sum[...] = jnp.zeros_like(wr_sum)
        gain_sum[...] = jnp.zeros_like(gain_sum)

    wo_sum[...] += mm(o_ref[...].T, low)
    wr_sum[...] += jnp.dot(
        (unit * gain).T, logit_grad, precision=FULL_PRECISION, preferred_element_type=F32
    )
    gain_sum[...] += jnp.sum(normed_grad * unit, axis=0, keepdims=True)


def combine(slot, expert, gate, probs, h, c, o, e_out, du, wo, wr, gain):
    tokens, width = h.shape
    slots, experts = e_out.shape[0], wr.shape[1]
    size = 256

    def rows(columns):
        return pl.BlockSpec((size, columns), lambda t: (t, 0))

    def whole(*shape):
        return pl.BlockSpec(shape, lambda t: (0, 0))

    return pl.pallas_call(
        combine_kernel,
        grid=(tokens // size,),
        in_specs=[rows(1), rows(1), rows(1), rows(experts), rows(width), rows(width), rows(width)]
        + [whole(slots, width), whole(slots, width), whole(width, width), whole(width, experts)]
        + [whole(1, width)],
        out_specs=[rows(width), rows(width), rows(width), whole(width, width), whole(width, experts)]
        + [whole(1, width)],
        out_shape=[
            jax.ShapeDtypeStruct((tokens, width), BF),
            jax.ShapeDtypeStruct((tokens, width), F32),
            jax.ShapeDtypeStruct((tokens, width), BF),
            jax.ShapeDtypeStruct((width, width), F32),
            jax.ShapeDtypeStruct((width, experts), F32),
            jax.ShapeDtypeStruct((1, width), F32),
        ],
        compiler_params=params(),
        cost_estimate=pl.CostEstimate(
            flops=4 * tokens * width * (slots + width),
            bytes_accessed=16 * tokens * width + 4 * slots * width,
            transcendentals=0,
        ),
    )(slot, expert, gate, probs, h, c, o, e_out, du, wo, wr, gain)


def last_kernel(
    x_ref, dh_ref, dq_ref, dk_ref, dv_ref, wq_ref, wk_ref, wv_ref, gain_ref,
    grad_ref, q_sum, k_sum, v_sum, gain_sum,
):
    step = pl.program_id(0)

    @pl.when(step == 0)
    def _():
        for total in (q_sum, k_sum, v_sum, gain_sum):
            total[...] = jnp.zeros_like(total)

    rows = x_ref[...].astype(F32)
    inv = lax.rsqrt(jnp.mean(rows * rows, axis=-1, keepdims=True) + EPSILON)
    unit = rows * inv
    gain = gain_ref[...]
    normed_t = (unit * gain).astype(BF).T
    normed_grad = None
    for grad_ref_in, weight_ref, total in (
        (dq_ref, wq_ref, q_sum),
        (dk_ref, wk_ref, k_sum),
        (dv_ref, wv_ref, v_sum),
    ):
        grad = grad_ref_in[...]
        total[...] += mm(normed_t, grad)
        term = mm_nt(grad, weight_ref[...])
        normed_grad = term if normed_grad is None else normed_grad + term
    unit_grad = normed_grad * gain
    grad_ref[...] = dh_ref[...] + inv * (
        unit_grad - unit * jnp.mean(unit_grad * unit, axis=-1, keepdims=True)
    )
    gain_sum[...] += jnp.sum(normed_grad * unit, axis=0, keepdims=True)


def last(x, dh, dq, dk, dv, wq, wk, wv, gain):
    tokens, width = x.shape
    size = 256
    rows = pl.BlockSpec((size, width), lambda t: (t, 0))
    square = pl.BlockSpec((width, width), lambda t: (0, 0))
    one = pl.BlockSpec((1, width), lambda t: (0, 0))
    return pl.pallas_call(
        last_kernel,
        grid=(tokens // size,),
        in_specs=[rows] * 5 + [square] * 3 + [one],
        out_specs=[rows, square, square, square, one],
        out_shape=[jax.ShapeDtypeStruct((tokens, width), F32)]
        + [jax.ShapeDtypeStruct((width, width), F32)] * 3
        + [jax.ShapeDtypeStruct((1, width), F32)],
        compiler_params=params(),
        cost_estimate=pl.CostEstimate(
            flops=12 * tokens * width * width, bytes_accessed=16 * tokens * width, transcendentals=0
        ),
    )(x, dh, dq, dk, dv, wq, wk, wv, gain)


def per_device(
    tokens,
    w_query,
    w_key,
    w_value,
    w_output,
    norm_attn,
    norm_ffn,
    relative_bias_table,
    w_router,
    w_in,
    w_out,
    expert_index,
    priority,
    cotangent,
):
    tok_rows, width = tokens.shape
    local = w_in.shape[0]
    exp_n, dp_n = lax.axis_size("exp"), lax.axis_size("dp")
    exp_me, dp_me = lax.axis_index("exp"), lax.axis_index("dp")
    all_experts = local * exp_n
    capacity = (5 * tok_rows + 4 * all_experts - 1) // (4 * all_experts)
    padded = (capacity + 1 + 15) // 16 * 16
    block = local * padded
    buckets = relative_bias_table.shape[0]

    chosen = expert_index[:, 0]
    order = priority[0]
    ahead = (chosen[:, None] == chosen[None, :]) & (order[None, :] < order[:, None])
    rank = jnp.sum(ahead.astype(jnp.int32), axis=1)
    place = ((chosen // local) ^ exp_me) * block + (chosen % local) * padded + rank
    slots = jnp.where(rank < capacity, place, -1)
    slot_row, slot_column = slots[None, :], slots[:, None]

    def over_exp(array):
        pieces = [array[0]]
        for step in range(1, exp_n):
            pairs = [(i, i ^ step) for i in range(exp_n)]
            pieces.append(lax.ppermute(array[step], "exp", pairs))
        return pieces

    def to_experts(rows):
        pieces = over_exp(rows.reshape(exp_n, local, padded, width))
        return jnp.concatenate(pieces, axis=1)

    def to_tokens(rows):
        pieces = rows.reshape(local, exp_n, padded, width).transpose(1, 0, 2, 3)
        return jnp.concatenate(over_exp(pieces), axis=0).reshape(exp_n * block, width)

    half = local // 2
    group = dp_me % 2

    def over_dp(rows):
        mine = lax.dynamic_slice_in_dim(rows, group * half, half, 0)
        other = lax.dynamic_slice_in_dim(rows, (1 - group) * half, half, 0)
        pieces = [mine]
        for step in range(1, dp_n):
            pairs = [(i, i ^ step) for i in range(dp_n)]
            pieces.append(lax.ppermute(other if step % 2 else mine, "dp", pairs))
        return pieces

    c_rows = to_experts(dispatch(slot_row, cotangent, exp_n, block))
    c_all = over_dp(c_rows)

    lines = jnp.dot(
        relative_bias_table.T, diagonal_onehot(buckets).T, precision=FULL_PRECISION
    ).reshape(HEADS, 4, TILE)
    lines = jnp.concatenate([lines, jnp.zeros_like(lines)], axis=1)
    gain_attn, gain_ffn = norm_attn[None, :], norm_ffn[None, :]
    q, k, v = qkv(tokens, gain_attn, w_query, w_key, w_value)
    context, lse = attention(lines, q, k, v)
    mixed, u, probs, gate, gate_row = router(
        context, tokens, w_output, gain_ffn, w_router, expert_index
    )
    sent = dispatch(slot_row, u, exp_n, block, gate=(gate_row, local, capacity, padded))
    u_rows = to_experts(sent)
    u_all = over_dp(u_rows)
    e_rows, d_rows = expert_pass(u_rows, c_rows, w_in, w_out)
    e_back, d_back = to_tokens(e_rows), to_tokens(d_rows)
    mixed_out, mixed_grad, context_grad, output_part, router_part, norm_ffn_part = combine(
        slot_column, expert_index, gate, probs, mixed, cotangent, context,
        e_back, d_back, w_output, w_router, gain_ffn,
    )
    query_grad, key_grad, value_grad, sums = attention_back(lines, q, k, v, context_grad, lse)
    table_part = jnp.dot(
        diagonal_onehot(buckets).T,
        sums[:, :4].reshape(HEADS, 4 * TILE).T,
        precision=FULL_PRECISION,
    )
    grad_tokens, query_part, key_part, value_part, norm_attn_part = last(
        tokens, mixed_grad, query_grad, key_grad, value_grad, w_query, w_key, w_value, gain_attn
    )

    size = w_in.shape[2] // dp_n
    where = jnp.stack([group * half, (dp_me // 2) * 2, group]).astype(jnp.int32)
    own_in, own_out, far_in, far_out = weight_grads(
        where, u_all, c_all, w_in, w_out, size, capacity, padded
    )
    swap = [(i, i ^ 1) for i in range(dp_n)]
    came_in, came_out = lax.ppermute(far_in, "dp", swap), lax.ppermute(far_out, "dp", swap)
    there = ((1 - group) * half).astype(jnp.int32)[None]
    grad_in, grad_out = finish(there, own_in, own_out, came_in, came_out)

    axes = ("exp", "dp")
    big = lax.psum(
        tuple(part.astype(BF) for part in (query_part, key_part, value_part, output_part)), axes
    )
    small = lax.psum((norm_attn_part, norm_ffn_part, table_part, router_part), axes)
    return (
        mixed_out,
        grad_tokens,
        *(part.astype(F32) for part in big),
        small[0][0],
        small[1][0],
        small[2],
        small[3],
        grad_in,
        grad_out,
    )


def solution(mesh):
    return jax.shard_map(
        per_device,
        mesh=mesh,
        in_specs=(
            P(("exp", "dp"), None),
            P(),
            P(),
            P(),
            P(),
            P(),
            P(),
            P(),
            P(),
            P("exp", None, None),
            P("exp", None, None),
            P(("exp", "dp"), None),
            P(("exp", "dp"), None),
            P(("exp", "dp"), None),
        ),
        out_specs=(
            P(("exp", "dp"), None),
            P(("exp", "dp"), None),
            P(),
            P(),
            P(),
            P(),
            P(),
            P(),
            P(),
            P(),
            P("exp", None, "dp"),
            P("exp", "dp", None),
        ),
        check_vma=False,
    )
```

time: 1260 us -> 797 us (0.63)
  matrix products: 450 us -> 1.27 us
  Pallas kernels: 0 us -> 308 us
  local copies, waits for them, and re-layouts: 230 us -> 45.1 us
  waiting for transfers between devices: 338 us -> 194 us
  other arithmetic: 76 us -> 18 us
  starting transfers between devices: 9.02 us -> 43.5 us
  blocking collectives: 126 us -> 158 us
    dot_general x46 -> x2, matrix products: 450 us -> 1.27 us  [the longest x1 0.96 us: per_device(): jnp.dot(diagonal_onehot(buckets).T, sums[:, :4].reshape(HEADS, 4 * TILE)....]
    pallas_call x0 -> x11, Pallas kernels: none -> 308 us  [the longest x1 67.5 us: weight_grads(): pl.pallas_call(functools.partial(weights_kernel, 3, sources, capacity, pa...]
    ppermute x0 -> x36, waiting for transfers between devices: none -> 184 us  [the longest x28 96.2 us: over_exp(): pieces.append(lax.ppermute(array[step], 'exp', pairs))]
    reduce_scatter x2 -> x0, waiting for transfers between devices: 163 us -> none  [the longest x1 163 us: per_device(): lax.psum_scatter(first_term.astype(jnp.bfloat16), 'dp', scatter_dimension...]
    psum x1 -> x2, waiting for transfers between devices: 123 us -> 9.77 us  [the longest x1 9.77 us: per_device(): lax.psum(tuple((part.astype(BF) for part in (query_part, key_part, value_...]
    psum x1, blocking collectives: 46.1 us -> 158 us  [per_device(): lax.psum((norm_attn_part, norm_ffn_part, table_part, router_part), axes)]
    all_to_all x2 -> x0, blocking collectives: 79.9 us -> none  [the longest x1 41 us: per_device(): lax.all_to_all(to_buffer(normed_ffn.astype(jnp.bfloat16)), 'exp', split_a...]
    reshape x10 -> x3, local copies, waits for them, and re-layouts: 60.5 us -> 2.55 us  [the longest x2 2.52 us: to_tokens(): pieces = rows.reshape(local, exp_n, padded, width).transpose(1, 0, 2, 3)]
  transfers between devices with their start and end apart: 5 -> 38, of which waited for: 4 -> 13; matrix products, arithmetic and copies ran while one was open for 36% -> 5% of each run, Pallas kernels for 0% -> 30%
where the time goes in v1:
time: 797 us; the launch traced here: 783 us
  Pallas kernels  308 us (39%)
  waiting for transfers between devices  194 us (24%)
  blocking collectives  158 us (20%)
  local copies, waits for them, and re-layouts  45.1 us (6%)
  starting transfers between devices  43.5 us (5%)
  other arithmetic  18 us (2%)
  between operations  14.9 us (2%)
    psum x1, blocking collectives, per_device(): lax.psum((norm_attn_part, norm_ffn_part, table_part, router_part), axes)  158 us
    ppermute x28, waiting for transfers between devices, over_exp(): pieces.append(lax.ppermute(array[step], 'exp', pairs))  96.2 us
    ppermute x6, waiting for transfers between devices, over_dp(): pieces.append(lax.ppermute(other if step % 2 else mine, 'dp', pairs))  88.1 us
    pallas_call x1, Pallas kernels, weight_grads(): pl.pallas_call(functools.partial(weights_kernel, 3, sources, capacity, pa...  67.5 us
    pallas_call x1, Pallas kernels, expert_pass(): pl.pallas_call(functools.partial(expert_kernel, 3), grid=(experts, hidden...  56.5 us
    pallas_call x1, Pallas kernels, attention_back(): pl.pallas_call(attention_back_kernel, grid=(pairs, seqs), in_specs=[lines...  51.1 us
    pallas_call x1, Pallas kernels, attention(): pl.pallas_call(attention_kernel, grid=(pairs, seqs), in_specs=[pl.BlockSp...  36.6 us
    pallas_call x1, Pallas kernels, combine(): pl.pallas_call(combine_kernel, grid=(tokens // size,), in_specs=[rows(1),...  32.9 us
  transfers between devices with their start and end apart: 38, of which 13 were waited for; matrix products, arithmetic and copies ran while one was open for 5% of the time, Pallas kernels for 30%

profile of v1, /device:TPU:0, one launch (start us, length us, event | category | flops | bytes accessed | tf_op | source)
XLA Modules:
  0.0 782.9 jit_solution(14744606946141020362)
XLA Ops:
  13.1 7.2 shard_map.233
  35.2 8.5 %shard_map.229 = (bf16[1536,768]{1,0:T(8,128)(2,1)}, bf16[1536,768]{1,0:T(8,128)(2,1)}, bf16[1536,768]{1,0:T(8,128)(2,1)}) custom-call(bf16[1536,768]{1,0:T(8,128)(2,1)} %x_ref.5, f32[1,768]{1,0:T(1,128)S(1)} %broadcast_in_dim.14.gain_ref, bf16[768,768]{1,0:T(8,128)(2,1)S(1)} %copy-done.10, bf16[768,768]{1,0:T(8,128)(2,1)S(1)} %copy-done.12, ...), custom_call_target="tpu_custom_call" | custom-call | flops 5435817984 | bytes 9437184 | tf_op jit(solution)/shard_map/pallas_call | solution.py:125
  43.7 36.6 %shard_map.230 = (bf16[1536,768]{1,0:T(8,128)(2,1)S(1)}, f32[6,3,2,512]{3,2,1,0:T(2,128)S(1)}) custom-call(f32[12,8,128]{2,1,0:T(8,128)S(1)} %concatenate.33.lines_ref, bf16[1536,768]{1,0:T(8,128)(2,1)} %get-tuple-element.45.q_ref, bf16[1536,768]{1,0:T(8,128)(2,1)} %get-tuple-element.46.k_ref, bf16[1536,768]{1,0:T(8,128)(2,1)} %get-tuple-element.47.v_ref), custom_call_target="tpu_custom_call" | custom-call | flops 9663676416 | bytes 9437184 | tf_op jit(solution)/shard_map/pallas_call | solution.py:209
  81.7 14.5 %shard_map.231 = (f32[1536,768]{1,0:T(8,128)}, bf16[1536,768]{1,0:T(8,128)(2,1)}, f32[1536,32]{1,0:T(8,128)S(1)}, f32[1536,1]{1,0:T(8,128)S(1)}, f32[1,1536]{1,0:T(1,128)S(1)}) custom-call(bf16[1536,768]{1,0:T(8,128)(2,1)} %copy-done.2, bf16[1536,768]{1,0:T(8,128)(2,1)} %x_ref.5, bf16[768,768]{1,0:T(8,128)(2,1)S(1)} %copy-done.3, ...), custom_call_target="tpu_custom_call" | custom-call | flops 1811939328 | bytes 11796480 | tf_op jit(solution)/shard_map/pallas_call | solution.py:362
  99.1 9.2 %shard_map.232 = bf16[2048,768]{1,0:T(8,128)(2,1)} custom-call(s32[1,1536]{1,0:T(1,128)S(1)} %compare_select_fusion.slot_ref, f32[1,1536]{1,0:T(1,128)S(1)} %get-tuple-element.52.gate_ref, bf16[1536,768]{1,0:T(8,128)(2,1)S(1)} %copy-done.9), custom_call_target="tpu_custom_call" | custom-call | flops 4831838208 | bytes 5505024 | tf_op jit(solution)/shard_map/pallas_call | solution.py:102
  125.2 16.8 %collective-permute-done.11 = bf16[4,64,768]{2,1,0:T(8,128)(2,1)S(1)} collective-permute-done((bf16[4,64,768]{2,1,0:T(8,128)(2,1)S(1)}, bf16[4,64,768]{2,1,0:T(8,128)(2,1)S(1)}, u32[]{:S(2)}, u32[]{:S(2)}) %collective-permute-start.11) | collective-permute-done | bytes 393248 | tf_op jit(solution)/shard_map/ppermute | solution.py:726
  148.9 5.3 collective-permute-done.1
  154.2 6.7 collective-permute-done.2
  161.0 13.3 %collective-permute-done.4 = bf16[4,64,768]{2,1,0:T(8,128)(2,1)S(1)} collective-permute-done((bf16[4,64,768]{2,1,0:T(8,128)(2,1)S(1)}, bf16[4,64,768]{2,1,0:T(8,128)(2,1)S(1)}, u32[]{:S(2)}, u32[]{:S(2)}) %collective-permute-start.4) | collective-permute-done | bytes 393248 | tf_op jit(solution)/shard_map/ppermute | solution.py:726
  176.0 56.5 %shard_map.234 = (bf16[4,512,768]{2,1,0:T(8,128)(2,1)S(1)}, bf16[4,512,768]{2,1,0:T(8,128)(2,1)}) custom-call(bf16[4,512,768]{2,1,0:T(8,128)(2,1)} %copy-done.24, bf16[4,512,768]{2,1,0:T(8,128)(2,1)} %constant_dynamic-update-slice_fusion.8.c_ref, bf16[4,768,3072]{2,1,0:T(8,128)(2,1)} %refs_8_.1, bf16[4,3072,768]{2,1,0:T(8,128)(2,1)} %refs_9_.1), custom_call_target="tpu_custom_call" | custom-call | flops 38654705664 | bytes 50331648 | tf_op jit(solution)/shard_map/pallas_call | solution.py:420
  246.1 11.3 %collective-permute-done.22 = bf16[4,64,768]{2,1,0:T(8,128)(2,1)S(1)} collective-permute-done((bf16[4,64,768]{2,1,0:T(8,128)(2,1)S(1)}, bf16[4,64,768]{2,1,0:T(8,128)(2,1)S(1)}, u32[]{:S(2)}, u32[]{:S(2)}) %collective-permute-start.22) | collective-permute-done | bytes 393248 | tf_op jit(solution)/shard_map/ppermute | solution.py:726
  261.1 9.1 %collective-permute-done.26 = bf16[4,64,768]{2,1,0:T(8,128)(2,1)S(1)} collective-permute-done((bf16[4,64,768]{2,1,0:T(8,128)(2,1)S(1)}, bf16[4,64,768]{2,1,0:T(8,128)(2,1)S(1)}, u32[]{:S(2)}, u32[]{:S(2)}) %collective-permute-start.26) | collective-permute-done | bytes 393248 | tf_op jit(solution)/shard_map/ppermute | solution.py:726
  270.3 6.4 collective-permute-done.27
  280.4 5.8 collective-permute-done.15
  297.5 16.4 %collective-permute-done.18 = bf16[4,64,768]{2,1,0:T(8,128)(2,1)S(1)} collective-permute-done((bf16[4,64,768]{2,1,0:T(8,128)(2,1)S(1)}, bf16[4,64,768]{2,1,0:T(8,128)(2,1)S(1)}, u32[]{:S(2)}, u32[]{:S(2)}) %collective-permute-start.18) | collective-permute-done | bytes 393248 | tf_op jit(solution)/shard_map/ppermute | solution.py:726
  320.2 32.9 %shard_map.235 = (bf16[1536,768]{1,0:T(8,128)(2,1)}, f32[1536,768]{1,0:T(8,128)}, bf16[1536,768]{1,0:T(8,128)(2,1)}, f32[768,768]{1,0:T(8,128)}, f32[768,32]{1,0:T(8,128)S(1)}, /*index=5*/f32[1,768]{1,0:T(1,128)S(1)}) custom-call(s32[1536,1]{1,0:T(8,128)S(1)} %fusion.slot_ref, s32[1536,1]{1,0:T(8,128)S(1)} %copy.59.expert_ref, f32[1536,1]{1,0:T(8,128)S(1)} %copy-done.19, ...), custom_call_target="tpu_custom_call" | custom-call | flops 13287555072 | bytes 25165824 | tf_op jit(solution)/shard_map/pallas_call | solution.py:609
  357.8 51.1 %shard_map.236 = (bf16[1536,768]{1,0:T(8,128)(2,1)S(1)}, bf16[1536,768]{1,0:T(8,128)(2,1)}, bf16[1536,768]{1,0:T(8,128)(2,1)}, f32[12,8,128]{2,1,0:T(8,128)S(1)}) custom-call(f32[12,8,128]{2,1,0:T(8,128)S(1)} %copy-done.6, bf16[1536,768]{1,0:T(8,128)(2,1)} %get-tuple-element.45.q_ref, bf16[1536,768]{1,0:T(8,128)(2,1)} %get-tuple-element.46.k_ref, ...), custom_call_target="tpu_custom_call" | custom-call | flops 24159191040 | bytes 16515072 | tf_op jit(solution)/shard_map/pallas_call | solution.py:311
  410.4 18.4 %shard_map.237 = (f32[1536,768]{1,0:T(8,128)}, f32[768,768]{1,0:T(8,128)}, f32[768,768]{1,0:T(8,128)}, f32[768,768]{1,0:T(8,128)}, f32[1,768]{1,0:T(1,128)S(1)}) custom-call(bf16[1536,768]{1,0:T(8,128)(2,1)} %x_ref.5, f32[1536,768]{1,0:T(8,128)} %get-tuple-element.57.dh_ref, bf16[1536,768]{1,0:T(8,128)(2,1)} %copy-done.20, ...), custom_call_target="tpu_custom_call" | custom-call | flops 10871635968 | bytes 18874368 | tf_op jit(solution)/shard_map/pallas_call | solution.py:673
  434.3 56.0 %collective-permute-done.32.refs_6_ = bf16[2,512,768]{2,1,0:T(8,128)(2,1)} collective-permute-done((bf16[2,512,768]{2,1,0:T(8,128)(2,1)}, bf16[2,512,768]{2,1,0:T(8,128)(2,1)}, u32[]{:S(2)}, u32[]{:S(2)}) %collective-permute-start.32) | collective-permute-done | bytes 1572896 | tf_op jit(solution)/shard_map/ppermute | solution.py:746
  490.3 32.0 %collective-permute-done.29.refs_2_ = bf16[2,512,768]{2,1,0:T(8,128)(2,1)} collective-permute-done((bf16[2,512,768]{2,1,0:T(8,128)(2,1)S(1)}, bf16[2,512,768]{2,1,0:T(8,128)(2,1)}, u32[]{:S(2)}, u32[]{:S(2)}) %collective-permute-start.29) | collective-permute-done | bytes 1572896 | tf_op jit(solution)/shard_map/ppermute | solution.py:746
  522.4 67.5 %shard_map.238 = (f32[4,768,768]{2,1,0:T(8,128)}, f32[4,768,768]{2,1,0:T(8,128)}, bf16[2,768,768]{2,1,0:T(8,128)(2,1)}, bf16[2,768,768]{2,1,0:T(8,128)(2,1)}) custom-call(s32[3]{0:T(128)S(1)} %copy-done.7, bf16[2,512,768]{2,1,0:T(8,128)(2,1)S(1)} %get-tuple-element.124.refs_0_, bf16[2,512,768]{2,1,0:T(8,128)(2,1)} %collective-permute-done.28.refs_1_, ...), custom_call_target="tpu_custom_call" | custom-call | flops 38654705664 | bytes 40894464 | tf_op jit(solution)/shard_map/pallas_call | solution.py:486
  593.0 158.4 %all-reduce.1 = (f32[768]{0:T(1024)}, f32[768]{0:T(1024)}, f32[32,12]{0,1:T(8,128)}) all-reduce(f32[768]{0:T(1024)S(1)} %reduce.2, f32[768]{0:T(1024)S(1)} %reduce.3, f32[32,12]{0,1:T(8,128)S(1)} %fusion.11), channel_id=1, replica_groups=mesh['exp'=8,'dp'=4] {'exp','dp'}, use_global_device_ids=true, to_apply=%region_5.6 | all-reduce | flops 1920 | bytes 15360 | tf_op jit(solution)/shard_map/psum | solution.py:795
  753.2 9.8 %all-reduce.8.cloned.1.call-done = (bf16[768,768]{1,0:T(8,128)(2,1)}, bf16[768,768]{1,0:T(8,128)(2,1)}, bf16[768,768]{1,0:T(8,128)(2,1)}, bf16[768,768]{1,0:T(8,128)(2,1)}) async-done(((bf16[768,768]{1,0:T(8,128)(2,1)}, bf16[768,768]{1,0:T(8,128)(2,1)}, bf16[768,768]{1,0:T(8,128)(2,1)}, bf16[768,768]{1,0:T(8,128)(2,1)}), (bf16[768,768]{1,0:T(8,128)(2,1)}, bf16[768,768]{1,0:T(8,128)(2,1)}, ...) | async-done | bytes 4718608 | tf_op jit(solution)/shard_map/psum | solution.py:792
  770.7 5.2 shard_map.239
  (232 shorter events, 113.1 us)
Async XLA Ops:
  7.2 744.2 %all-reduce.6.cloned.1.call-start = ((), (), s32[]{:S(2)}) async-start(), calls=%async_computation | async-start | bytes 786432 | tf_op jit(solution)/shard_map/psum | solution.py:795
  23.8 118.9 %collective-permute-start.12 = (bf16[4,64,768]{2,1,0:T(8,128)(2,1)}, bf16[4,64,768]{2,1,0:T(8,128)(2,1)}, u32[]{:S(2)}, u32[]{:S(2)}) collective-permute-start(bf16[4,64,768]{2,1,0:T(8,128)(2,1)} %bitcast.16), channel_id=1, source_target_pairs={{0,24},{4,28},{8,16},{12,20},{16,8},{20,12},{24,0},{28,4},{1,25},{... | collective-permute-start | bytes 1179656 | tf_op jit(solution)/shard_map/ppermute | solution.py:726
  27.8 95.6 %collective-permute-start.10 = (bf16[4,64,768]{2,1,0:T(8,128)(2,1)}, bf16[4,64,768]{2,1,0:T(8,128)(2,1)}, u32[]{:S(2)}, u32[]{:S(2)}) collective-permute-start(bf16[4,64,768]{2,1,0:T(8,128)(2,1)} %bitcast.14), channel_id=1, source_target_pairs={{0,16},{4,20},{8,24},{12,28},{16,0},{20,4},{24,8},{28,12},{1,17},{... | collective-permute-start | bytes 1179656 | tf_op jit(solution)/shard_map/ppermute | solution.py:726
  28.3 90.8 %collective-permute-start.9 = (bf16[4,64,768]{2,1,0:T(8,128)(2,1)}, bf16[4,64,768]{2,1,0:T(8,128)(2,1)}, u32[]{:S(2)}, u32[]{:S(2)}) collective-permute-start(bf16[4,64,768]{2,1,0:T(8,128)(2,1)} %bitcast.13), channel_id=1, source_target_pairs={{0,12},{4,8},{8,4},{12,0},{16,28},{20,24},{24,20},{28,16},{1,13},{... | collective-permute-start | bytes 1179656 | tf_op jit(solution)/shard_map/ppermute | solution.py:726
  28.3 88.5 %collective-permute-start.8 = (bf16[4,64,768]{2,1,0:T(8,128)(2,1)}, bf16[4,64,768]{2,1,0:T(8,128)(2,1)}, u32[]{:S(2)}, u32[]{:S(2)}) collective-permute-start(bf16[4,64,768]{2,1,0:T(8,128)(2,1)} %bitcast.12), channel_id=1, source_target_pairs={{0,8},{4,12},{8,0},{12,4},{16,24},{20,28},{24,16},{28,20},{1,9},{5... | collective-permute-start | bytes 1179656 | tf_op jit(solution)/shard_map/ppermute | solution.py:726
  29.2 84.6 %collective-permute-start.7 = (bf16[4,64,768]{2,1,0:T(8,128)(2,1)}, bf16[4,64,768]{2,1,0:T(8,128)(2,1)}, u32[]{:S(2)}, u32[]{:S(2)}) collective-permute-start(bf16[4,64,768]{2,1,0:T(8,128)(2,1)} %bitcast.11), channel_id=1, source_target_pairs={{0,4},{4,0},{8,12},{12,8},{16,20},{20,16},{24,28},{28,24},{1,5},{5... | collective-permute-start | bytes 1179656 | tf_op jit(solution)/shard_map/ppermute | solution.py:726
  113.8 28.1 %collective-permute-start.11 = (bf16[4,64,768]{2,1,0:T(8,128)(2,1)S(1)}, bf16[4,64,768]{2,1,0:T(8,128)(2,1)S(1)}, u32[]{:S(2)}, u32[]{:S(2)}) collective-permute-start(bf16[4,64,768]{2,1,0:T(8,128)(2,1)S(1)} %bitcast.96), channel_id=1, source_target_pairs={{0,20},{4,16},{8,28},{12,24},{16,4},{20,0},{24,12},{28,8},{1,21},{... | collective-permute-start | bytes 1179656 | tf_op jit(solution)/shard_map/ppermute | solution.py:726
  116.8 29.2 %collective-permute-start.13 = (bf16[4,64,768]{2,1,0:T(8,128)(2,1)S(1)}, bf16[4,64,768]{2,1,0:T(8,128)(2,1)S(1)}, u32[]{:S(2)}, u32[]{:S(2)}) collective-permute-start(bf16[4,64,768]{2,1,0:T(8,128)(2,1)S(1)} %bitcast.94), channel_id=1, source_target_pairs={{0,28},{4,24},{8,20},{12,16},{16,12},{20,8},{24,4},{28,0},{1,29},{... | collective-permute-start | bytes 1179656 | tf_op jit(solution)/shard_map/ppermute | solution.py:726
  119.1 55.2 %collective-permute-start.5 = (bf16[4,64,768]{2,1,0:T(8,128)(2,1)S(1)}, bf16[4,64,768]{2,1,0:T(8,128)(2,1)S(1)}, u32[]{:S(2)}, u32[]{:S(2)}) collective-permute-start(bf16[4,64,768]{2,1,0:T(8,128)(2,1)S(1)} %bitcast.97), channel_id=1, source_target_pairs={{0,24},{4,28},{8,16},{12,20},{16,8},{20,12},{24,0},{28,4},{1,25},{... | collective-permute-start | bytes 1179656 | tf_op jit(solution)/shard_map/ppermute | solution.py:726
  123.4 24.9 %collective-permute-start = (bf16[4,64,768]{2,1,0:T(8,128)(2,1)}, bf16[4,64,768]{2,1,0:T(8,128)(2,1)S(1)}, u32[]{:S(2)}, u32[]{:S(2)}) collective-permute-start(bf16[4,64,768]{2,1,0:T(8,128)(2,1)} %bitcast.102), channel_id=1, source_target_pairs={{0,4},{4,0},{8,12},{12,8},{16,20},{20,16},{24,28},{28,24},{1,5},{5... | collective-permute-start | bytes 1179656 | tf_op jit(solution)/shard_map/ppermute | solution.py:726
  148.3 26.0 %collective-permute-start.4 = (bf16[4,64,768]{2,1,0:T(8,128)(2,1)S(1)}, bf16[4,64,768]{2,1,0:T(8,128)(2,1)S(1)}, u32[]{:S(2)}, u32[]{:S(2)}) collective-permute-start(bf16[4,64,768]{2,1,0:T(8,128)(2,1)S(1)} %bitcast.98), channel_id=1, source_target_pairs={{0,20},{4,16},{8,28},{12,24},{16,4},{20,0},{24,12},{28,8},{1,21},{... | collective-permute-start | bytes 1179656 | tf_op jit(solution)/shard_map/ppermute | solution.py:726
  242.4 111.5 %collective-permute-start.33 = (bf16[2,512,768]{2,1,0:T(8,128)(2,1)}, bf16[2,512,768]{2,1,0:T(8,128)(2,1)}, u32[]{:S(2)}, u32[]{:S(2)}) collective-permute-start(bf16[2,512,768]{2,1,0:T(8,128)(2,1)} %get-tuple-element.121), channel_id=1, source_target_pairs={{0,3},{1,2},{2,1},{3,0},{4,7},{5,6},{6,5},{7,4},{8,11},{9,10},{10,... | collective-permute-start | bytes 4718600 | tf_op jit(solution)/shard_map/ppermute | solution.py:746
  260.7 25.5 %collective-permute-start.15 = (bf16[4,64,768]{2,1,0:T(8,128)(2,1)S(1)}, bf16[4,64,768]{2,1,0:T(8,128)(2,1)S(1)}, u32[]{:S(2)}, u32[]{:S(2)}) collective-permute-start(bf16[4,64,768]{2,1,0:T(8,128)(2,1)S(1)} %get-tuple-element.137), channel_id=1, source_target_pairs={{0,8},{4,12},{8,0},{12,4},{16,24},{20,28},{24,16},{28,20},{1,9},{5... | collective-permute-start | bytes 1179656 | tf_op jit(solution)/shard_map/ppermute | solution.py:726
  277.2 36.7 %collective-permute-start.18 = (bf16[4,64,768]{2,1,0:T(8,128)(2,1)S(1)}, bf16[4,64,768]{2,1,0:T(8,128)(2,1)S(1)}, u32[]{:S(2)}, u32[]{:S(2)}) collective-permute-start(bf16[4,64,768]{2,1,0:T(8,128)(2,1)S(1)} %get-tuple-element.134), channel_id=1, source_target_pairs={{0,20},{4,16},{8,28},{12,24},{16,4},{20,0},{24,12},{28,8},{1,21},{... | collective-permute-start | bytes 1179656 | tf_op jit(solution)/shard_map/ppermute | solution.py:726
  286.2 31.4 %collective-permute-start.19 = (bf16[4,64,768]{2,1,0:T(8,128)(2,1)S(1)}, bf16[4,64,768]{2,1,0:T(8,128)(2,1)S(1)}, u32[]{:S(2)}, u32[]{:S(2)}) collective-permute-start(bf16[4,64,768]{2,1,0:T(8,128)(2,1)S(1)} %get-tuple-element.133), channel_id=1, source_target_pairs={{0,24},{4,28},{8,16},{12,20},{16,8},{20,12},{24,0},{28,4},{1,25},{... | collective-permute-start | bytes 1179656 | tf_op jit(solution)/shard_map/ppermute | solution.py:726
  292.6 25.1 %collective-permute-start.20 = (bf16[4,64,768]{2,1,0:T(8,128)(2,1)S(1)}, bf16[4,64,768]{2,1,0:T(8,128)(2,1)S(1)}, u32[]{:S(2)}, u32[]{:S(2)}) collective-permute-start(bf16[4,64,768]{2,1,0:T(8,128)(2,1)S(1)} %get-tuple-element.132), channel_id=1, source_target_pairs={{0,28},{4,24},{8,20},{12,16},{16,12},{20,8},{24,4},{28,0},{1,29},{... | collective-permute-start | bytes 1179656 | tf_op jit(solution)/shard_map/ppermute | solution.py:726
  295.6 138.6 %collective-permute-start.31 = (bf16[2,512,768]{2,1,0:T(8,128)(2,1)}, bf16[2,512,768]{2,1,0:T(8,128)(2,1)}, u32[]{:S(2)}, u32[]{:S(2)}) collective-permute-start(bf16[2,512,768]{2,1,0:T(8,128)(2,1)} %get-tuple-element.121), channel_id=1, source_target_pairs={{0,1},{1,0},{2,3},{3,2},{4,5},{5,4},{6,7},{7,6},{8,9},{9,8},{10,11... | collective-permute-start | bytes 4718600 | tf_op jit(solution)/shard_map/ppermute | solution.py:746
  313.9 176.4 %collective-permute-start.30 = (bf16[2,512,768]{2,1,0:T(8,128)(2,1)}, bf16[2,512,768]{2,1,0:T(8,128)(2,1)}, u32[]{:S(2)}, u32[]{:S(2)}) collective-permute-start(bf16[2,512,768]{2,1,0:T(8,128)(2,1)} %get-tuple-element.123), channel_id=1, source_target_pairs={{0,3},{1,2},{2,1},{3,0},{4,7},{5,6},{6,5},{7,4},{8,11},{9,10},{10,... | collective-permute-start | bytes 4718600 | tf_op jit(solution)/shard_map/ppermute | solution.py:746
  317.6 172.7 %collective-permute-start.28 = (bf16[2,512,768]{2,1,0:T(8,128)(2,1)}, bf16[2,512,768]{2,1,0:T(8,128)(2,1)}, u32[]{:S(2)}, u32[]{:S(2)}) collective-permute-start(bf16[2,512,768]{2,1,0:T(8,128)(2,1)} %get-tuple-element.123), channel_id=1, source_target_pairs={{0,1},{1,0},{2,3},{3,2},{4,5},{5,4},{6,7},{7,6},{8,9},{9,8},{10,11... | collective-permute-start | bytes 4718600 | tf_op jit(solution)/shard_map/ppermute | solution.py:746
  317.7 172.6 %collective-permute-start.32 = (bf16[2,512,768]{2,1,0:T(8,128)(2,1)}, bf16[2,512,768]{2,1,0:T(8,128)(2,1)}, u32[]{:S(2)}, u32[]{:S(2)}) collective-permute-start(bf16[2,512,768]{2,1,0:T(8,128)(2,1)} %get-tuple-element.122.refs_4_), channel_id=1, source_target_pairs={{0,2},{1,3},{2,0},{3,1},{4,6},{5,7},{6,4},{7,5},{8,10},{9,11},{10,... | collective-permute-start | bytes 4718600 | tf_op jit(solution)/shard_map/ppermute | solution.py:746
  353.9 409.0 %all-reduce.8.cloned.1.call-start = ((), (), s32[]{:S(2)}) async-start(), calls=%async_computation.1 | async-start | bytes 9437184 | tf_op jit(solution)/shard_map/psum | solution.py:792
  354.0 168.4 %collective-permute-start.29 = (bf16[2,512,768]{2,1,0:T(8,128)(2,1)S(1)}, bf16[2,512,768]{2,1,0:T(8,128)(2,1)}, u32[]{:S(2)}, u32[]{:S(2)}) collective-permute-start(bf16[2,512,768]{2,1,0:T(8,128)(2,1)S(1)} %get-tuple-element.124.refs_0_), channel_id=1, source_target_pairs={{0,2},{1,3},{2,0},{3,1},{4,6},{5,7},{6,4},{7,5},{8,10},{9,11},{10,... | collective-permute-start | bytes 4718600 | tf_op jit(solution)/shard_map/ppermute | solution.py:746
  589.9 180.8 %collective-permute-start.34 = (bf16[2,768,768]{2,1,0:T(8,128)(2,1)}, bf16[2,768,768]{2,1,0:T(8,128)(2,1)S(1)}, u32[]{:S(2)}, u32[]{:S(2)}) collective-permute-start(bf16[2,768,768]{2,1,0:T(8,128)(2,1)} %get-tuple-element.74), channel_id=1, source_target_pairs={{0,1},{1,0},{2,3},{3,2},{4,5},{5,4},{6,7},{7,6},{8,9},{9,8},{10,11... | collective-permute-start | bytes 7077896 | tf_op jit(solution)/shard_map/ppermute | solution.py:787
  589.9 180.7 %collective-permute-start.35 = (bf16[2,768,768]{2,1,0:T(8,128)(2,1)}, bf16[2,768,768]{2,1,0:T(8,128)(2,1)}, u32[]{:S(2)}, u32[]{:S(2)}) collective-permute-start(bf16[2,768,768]{2,1,0:T(8,128)(2,1)} %get-tuple-element.75), channel_id=1, source_target_pairs={{0,1},{1,0},{2,3},{3,2},{4,5},{5,4},{6,7},{7,6},{8,9},{9,8},{10,11... | collective-permute-start | bytes 7077896 | tf_op jit(solution)/shard_map/ppermute | solution.py:787
  (60 other events, 952.8 us)
Sparse Core Ops, SparseCore 0:
  354.0 235.5 all-reduce.5
  597.4 165.5 all-reduce.7

commit v2 on v1

--- a/solution.py
+++ b/solution.py
@@ -33,6 +33,15 @@
 
 def mm_nt(left, right):
     return lax.dot_general(left, right, (((1,), (1,)), ((), ())), preferred_element_type=F32)
+
+
+def flipped(index, step):
+    bit = 1
+    while bit <= step:
+        if step & bit:
+            index = index + bit * (1 - 2 * ((index // bit) % 2))
+        bit *= 2
+    return index
 
 
 def bucket_of(offset):
@@ -178,8 +187,41 @@
     return jnp.where(head_lanes(head), array, jnp.zeros_like(array))
 
 
-def attention_kernel(lines_ref, q_ref, k_ref, v_ref, o_ref, lse_ref, bias_ref):
-    @pl.when(pl.program_id(1) == 0)
+def attention_kernel(
+    lines_ref, sent_ref, q_ref, k_ref, v_ref, o_ref, lse_ref, came_ref, bias_ref, local_sem, send_sem, recv_sem
+):
+    pair, seq = pl.program_id(0), pl.program_id(1)
+    blocks = sent_ref.shape[0]
+    me = lax.axis_index("exp")
+
+    def there(block):
+        return {"exp": flipped(me, block)}
+
+    def outgoing(block):
+        return pltpu.make_async_remote_copy(
+            src_ref=sent_ref.at[block],
+            dst_ref=came_ref.at[:, block],
+            send_sem=send_sem.at[block],
+            recv_sem=recv_sem.at[block],
+            device_id=there(block),
+            device_id_type=pl.DeviceIdType.MESH,
+        )
+
+    own = pltpu.make_async_copy(sent_ref.at[0], came_ref.at[:, 0], local_sem)
+
+    @pl.when((pair == 0) & (seq == 0))
+    def _():
+        barrier = pltpu.get_barrier_semaphore()
+        for block in range(1, blocks):
+            pl.semaphore_signal(
+                barrier, inc=1, device_id=there(block), device_id_type=pl.DeviceIdType.MESH
+            )
+        pl.semaphore_wait(barrier, blocks - 1)
+        own.start()
+        for block in range(1, blocks):
+            outgoing(block).start()
+
+    @pl.when(seq == 0)
     def _():
         fill_bias(lines_ref, bias_ref)
 
@@ -201,28 +243,43 @@
             out = mixed if out is None else jnp.where(row < HEAD_DIM, out, mixed)
         o_ref[places, :] = out.T.astype(BF)
 
-
-def attention(lines, q, k, v):
+    @pl.when((pair == pl.num_programs(0) - 1) & (seq == pl.num_programs(1) - 1))
+    def _():
+        own.wait()
+        for block in range(1, blocks):
+            outgoing(block).wait()
+
+
+def attention(lines, sent, q, k, v):
+    blocks, experts, padded, width = sent.shape
     tokens, width = q.shape
     seqs, pairs = tokens // SEQ, width // PAIR
     block = pl.BlockSpec((SEQ, PAIR), lambda h, s: (s, h))
     return pl.pallas_call(
         attention_kernel,
         grid=(pairs, seqs),
-        in_specs=[pl.BlockSpec((2, 8, TILE), lambda h, s: (h, 0, 0)), block, block, block],
-        out_specs=[block, pl.BlockSpec((1, 1, 2, SEQ), lambda h, s: (h, s, 0, 0))],
+        in_specs=[pl.BlockSpec((2, 8, TILE), lambda h, s: (h, 0, 0)), pl.BlockSpec(memory_space=pl.ANY)]
+        + [block, block, block],
+        out_specs=[block, pl.BlockSpec((1, 1, 2, SEQ), lambda h, s: (h, s, 0, 0))]
+        + [pl.BlockSpec(memory_space=pl.ANY)],
         out_shape=[
             jax.ShapeDtypeStruct((tokens, width), BF),
             jax.ShapeDtypeStruct((pairs, seqs, 2, SEQ), F32),
+            jax.ShapeDtypeStruct((experts, blocks, padded, width), BF),
         ],
-        scratch_shapes=[pltpu.VMEM((2, SEQ, SEQ), F32)],
-        compiler_params=params(),
+        scratch_shapes=[
+            pltpu.VMEM((2, SEQ, SEQ), F32),
+            pltpu.SemaphoreType.DMA,
+            pltpu.SemaphoreType.DMA((blocks,)),
+            pltpu.SemaphoreType.DMA((blocks,)),
+        ],
+        compiler_params=params(collective_id=1, has_side_effects=True),
         cost_estimate=pl.CostEstimate(
             flops=16 * pairs * seqs * SEQ * SEQ * PAIR,
             bytes_accessed=8 * tokens * width,
             transcendentals=2 * pairs * seqs * SEQ * SEQ,
         ),
-    )(lines, q, k, v)
+    )(lines, sent, q, k, v)
 
 
 def attention_back_kernel(
@@ -388,16 +445,75 @@
     return value, slope
 
 
-def expert_kernel(parts, u_ref, c_ref, first_ref, second_ref, e_ref, d_ref, e_sum, d_sum):
-    step = pl.program_id(1)
-    rows, upstream = u_ref[0], c_ref[0]
+def expert_kernel(
+    parts, sent_ref, c_ref, first_ref, second_ref, u_ref, e_ref, d_ref,
+    rows_ref, e_sum, d_sum, e_held, d_held, local_sem, send_sem, recv_sem, back_send, back_recv,
+):
+    expert, step = pl.program_id(0), pl.program_id(1)
+    experts, last_step = pl.num_programs(0), pl.num_programs(1) - 1
+    blocks, padded, width = rows_ref.shape[1:]
+    me = lax.axis_index("exp")
     columns = first_ref.shape[2] // parts
 
+    def there(block):
+        return {"exp": flipped(me, block)}
+
+    def outgoing(which, block):
+        return pltpu.make_async_remote_copy(
+            src_ref=sent_ref.at[block, which],
+            dst_ref=rows_ref.at[which, block],
+            send_sem=send_sem.at[which, block],
+            recv_sem=recv_sem.at[which, block],
+            device_id=there(block),
+            device_id_type=pl.DeviceIdType.MESH,
+        )
+
+    def returning(kind, which, block):
+        held, target = (e_held, e_ref) if kind == 0 else (d_held, d_ref)
+        return pltpu.make_async_remote_copy(
+            src_ref=held.at[which, block],
+            dst_ref=target.at[block, which],
+            send_sem=back_send.at[kind, which, block],
+            recv_sem=back_recv.at[kind, which, block],
+            device_id=there(block),
+            device_id_type=pl.DeviceIdType.MESH,
+        )
+
+    def own_in(which):
+        return pltpu.make_async_copy(sent_ref.at[0, which], rows_ref.at[which, 0], local_sem.at[0, which])
+
+    def own_back(kind, which):
+        held, target = (e_held, e_ref) if kind == 0 else (d_held, d_ref)
+        return pltpu.make_async_copy(
+            held.at[which, 0], target.at[0, which], local_sem.at[1 + kind, which]
+        )
+
+    def keep(which):
+        return pltpu.make_async_copy(rows_ref.at[which], u_ref.at[which], local_sem.at[3, which])
+
+    @pl.when((expert == 0) & (step == 0))
+    def _():
+        barrier = pltpu.get_barrier_semaphore()
+        for block in range(1, blocks):
+            pl.semaphore_signal(
+                barrier, inc=1, device_id=there(block), device_id_type=pl.DeviceIdType.MESH
+            )
+        pl.semaphore_wait(barrier, blocks - 1)
+        for which in range(rows_ref.shape[0]):
+            own_in(which).start()
+            for block in range(1, blocks):
+                outgoing(which, block).start()
+
     @pl.when(step == 0)
     def _():
+        own_in(expert).wait()
+        for block in range(1, blocks):
+            outgoing(expert, block).wait_recv()
+        keep(expert).start()
         e_sum[...] = jnp.zeros_like(e_sum)
         d_sum[...] = jnp.zeros_like(d_sum)
 
+    rows, upstream = rows_ref[expert].reshape(blocks * padded, width), c_ref[0]
     for part in range(parts):
         places = slice(part * columns, (part + 1) * columns)
         first, second = first_ref[0, :, places], second_ref[0, places, :]
@@ -406,36 +522,67 @@
         e_sum[...] += mm(value.astype(BF), second)
         d_sum[...] += mm_nt(inner, first)
 
-    @pl.when(step == pl.num_programs(1) - 1)
-    def _():
-        e_ref[0] = e_sum[...].astype(BF)
-        d_ref[0] = d_sum[...].astype(BF)
-
-
-def expert_pass(u, c, w_in, w_out):
-    experts, rows, width = u.shape
+    @pl.when(step == last_step)
+    def _():
+        e_held[expert] = e_sum[...].astype(BF).reshape(blocks, padded, width)
+        d_held[expert] = d_sum[...].astype(BF).reshape(blocks, padded, width)
+        for kind in range(2):
+            own_back(kind, expert).start()
+            for block in range(1, blocks):
+                returning(kind, expert, block).start()
+
+    @pl.when((step == last_step) & (expert == experts - 1))
+    def _():
+        for which in range(rows_ref.shape[0]):
+            keep(which).wait()
+            for block in range(1, blocks):
+                outgoing(which, block).wait_send()
+            for kind in range(2):
+                own_back(kind, which).wait()
+                for block in range(1, blocks):
+                    returning(kind, which, block).wait()
+
+
+def expert_pass(sent, c, w_in, w_out):
+    blocks, experts, padded, width = sent.shape
     hidden = w_in.shape[2]
     size = 768
-    block = pl.BlockSpec((1, rows, width), lambda e, f: (e, 0, 0))
+    rows = blocks * padded
+    anywhere = pl.BlockSpec(memory_space=pl.ANY)
     return pl.pallas_call(
         functools.partial(expert_kernel, 3),
         grid=(experts, hidden // size),
         in_specs=[
-            block,
-            block,
+            anywhere,
+            pl.BlockSpec((1, rows, width), lambda e, f: (e, 0, 0)),
             pl.BlockSpec((1, width, size), lambda e, f: (e, 0, f)),
             pl.BlockSpec((1, size, width), lambda e, f: (e, f, 0)),
         ],
-        out_specs=[block, block],
-        out_shape=[jax.ShapeDtypeStruct(u.shape, BF)] * 2,
-        scratch_shapes=[pltpu.VMEM((rows, width), F32)] * 2,
-        compiler_params=params(),
+        out_specs=[anywhere] * 3,
+        out_shape=[
+            jax.ShapeDtypeStruct((experts, blocks, padded, width), BF),
+            jax.ShapeDtypeStruct(sent.shape, BF),
+            jax.ShapeDtypeStruct(sent.shape, BF),
+        ],
+        scratch_shapes=[
+            pltpu.VMEM((experts, blocks, padded, width), BF),
+            pltpu.VMEM((rows, width), F32),
+            pltpu.VMEM((rows, width), F32),
+            pltpu.VMEM((experts, blocks, padded, width), BF),
+            pltpu.VMEM((experts, blocks, padded, width), BF),
+            pltpu.SemaphoreType.DMA((4, experts)),
+            pltpu.SemaphoreType.DMA((experts, blocks)),
+            pltpu.SemaphoreType.DMA((experts, blocks)),
+            pltpu.SemaphoreType.DMA((2, experts, blocks)),
+            pltpu.SemaphoreType.DMA((2, experts, blocks)),
+        ],
+        compiler_params=params(collective_id=0, has_side_effects=True),
         cost_estimate=pl.CostEstimate(
             flops=8 * experts * rows * width * hidden,
             bytes_accessed=4 * experts * width * (hidden + 2 * rows),
             transcendentals=experts * rows * hidden,
         ),
-    )(u, c, w_in, w_out)
+    )(sent, c, w_in, w_out)
 
 
 def weights_kernel(parts, sources, capacity, padded, place_ref, *refs):
@@ -719,21 +866,6 @@
     slots = jnp.where(rank < capacity, place, -1)
     slot_row, slot_column = slots[None, :], slots[:, None]
 
-    def over_exp(array):
-        pieces = [array[0]]
-        for step in range(1, exp_n):
-            pairs = [(i, i ^ step) for i in range(exp_n)]
-            pieces.append(lax.ppermute(array[step], "exp", pairs))
-        return pieces
-
-    def to_experts(rows):
-        pieces = over_exp(rows.reshape(exp_n, local, padded, width))
-        return jnp.concatenate(pieces, axis=1)
-
-    def to_tokens(rows):
-        pieces = rows.reshape(local, exp_n, padded, width).transpose(1, 0, 2, 3)
-        return jnp.concatenate(over_exp(pieces), axis=0).reshape(exp_n * block, width)
-
     half = local // 2
     group = dp_me % 2
 
@@ -746,24 +878,26 @@
             pieces.append(lax.ppermute(other if step % 2 else mine, "dp", pairs))
         return pieces
 
-    c_rows = to_experts(dispatch(slot_row, cotangent, exp_n, block))
-    c_all = over_dp(c_rows)
-
     lines = jnp.dot(
         relative_bias_table.T, diagonal_onehot(buckets).T, precision=FULL_PRECISION
     ).reshape(HEADS, 4, TILE)
     lines = jnp.concatenate([lines, jnp.zeros_like(lines)], axis=1)
     gain_attn, gain_ffn = norm_attn[None, :], norm_ffn[None, :]
     q, k, v = qkv(tokens, gain_attn, w_query, w_key, w_value)
-    context, lse = attention(lines, q, k, v)
+    c_sent = dispatch(slot_row, cotangent, exp_n, block).reshape(exp_n, local, padded, width)
+    context, lse, c_rows = attention(lines, c_sent, q, k, v)
+    c_rows = c_rows.reshape(local, exp_n * padded, width)
+    c_all = over_dp(c_rows)
     mixed, u, probs, gate, gate_row = router(
         context, tokens, w_output, gain_ffn, w_router, expert_index
     )
     sent = dispatch(slot_row, u, exp_n, block, gate=(gate_row, local, capacity, padded))
-    u_rows = to_experts(sent)
-    u_all = over_dp(u_rows)
-    e_rows, d_rows = expert_pass(u_rows, c_rows, w_in, w_out)
-    e_back, d_back = to_tokens(e_rows), to_tokens(d_rows)
+    u_rows, e_back, d_back = expert_pass(
+        sent.reshape(exp_n, local, padded, width), c_rows, w_in, w_out
+    )
+    e_back, *c_all = lax.optimization_barrier((e_back, *c_all))
+    e_back, d_back = e_back.reshape(exp_n * block, width), d_back.reshape(exp_n * block, width)
+    u_all = over_dp(u_rows.reshape(local, exp_n * padded, width))
     mixed_out, mixed_grad, context_grad, output_part, router_part, norm_ffn_part = combine(
         slot_column, expert_index, gate, probs, mixed, cotangent, context,
         e_back, d_back, w_output, w_router, gain_ffn,

time: 797 us -> 627 us (0.79)
  waiting for transfers between devices: 194 us -> 32.7 us
  Pallas kernels: 308 us -> 368 us
  starting transfers between devices: 43.5 us -> 11 us
  local copies, waits for them, and re-layouts: 45.1 us -> 20.4 us
    ppermute x28 -> x0, waiting for transfers between devices: 96.2 us -> none  [over_exp(): pieces.append(lax.ppermute(array[step], 'exp', pairs))]
    ppermute x6, waiting for transfers between devices: 88.1 us -> 9.72 us  [over_dp(): pieces.append(lax.ppermute(other if step % 2 else mine, 'dp', pairs))]
    pallas_call x1, Pallas kernels: 56.5 us -> 109 us  [expert_pass(): pl.pallas_call(functools.partial(expert_kernel, 3), grid=(experts, hidden...]
    ppermute x28 -> x0, starting transfers between devices: 29.2 us -> none  [over_exp(): pieces.append(lax.ppermute(array[step], 'exp', pairs))]
    unnamed x125 -> x63, local copies, waits for them, and re-layouts: 30.8 us -> 13.2 us
    pallas_call x1, Pallas kernels: 51.1 us -> 64.5 us  [attention_back(): pl.pallas_call(attention_back_kernel, grid=(pairs, seqs), in_specs=[lines...]
    psum x1, waiting for transfers between devices: 9.77 us -> 23 us  [per_device(): lax.psum(tuple((part.astype(BF) for part in (query_part, key_part, value_...]
    pallas_call x1, Pallas kernels: 67.5 us -> 57.8 us  [weight_grads(): pl.pallas_call(functools.partial(weights_kernel, 3, sources, capacity, pa...]
  transfers between devices with their start and end apart: 38 -> 10, of which waited for: 13 -> 2; matrix products, arithmetic and copies ran while one was open for 5% -> 3% of each run, Pallas kernels for 30% -> 49%
where the time goes in v2:
time: 627 us; the launch traced here: 620 us
  Pallas kernels  368 us (59%)
  blocking collectives  155 us (25%)
  waiting for transfers between devices  32.7 us (5%)
  local copies, waits for them, and re-layouts  20.4 us (3%)
  other arithmetic  17.4 us (3%)
  between operations  14.6 us (2%)
  starting transfers between devices  11 us (2%)
    psum x1, blocking collectives, per_device(): lax.psum((norm_attn_part, norm_ffn_part, table_part, router_part), axes)  155 us
    pallas_call x1, Pallas kernels, expert_pass(): pl.pallas_call(functools.partial(expert_kernel, 3), grid=(experts, hidden...  109 us
    pallas_call x1, Pallas kernels, attention_back(): pl.pallas_call(attention_back_kernel, grid=(pairs, seqs), in_specs=[lines...  64.5 us
    pallas_call x1, Pallas kernels, weight_grads(): pl.pallas_call(functools.partial(weights_kernel, 3, sources, capacity, pa...  57.8 us
    pallas_call x1, Pallas kernels, attention(): pl.pallas_call(attention_kernel, grid=(pairs, seqs), in_specs=[pl.BlockSp...  41.3 us
    pallas_call x1, Pallas kernels, combine(): pl.pallas_call(combine_kernel, grid=(tokens // size,), in_specs=[rows(1),...  32.9 us
    psum x1, waiting for transfers between devices, per_device(): lax.psum(tuple((part.astype(BF) for part in (query_part, key_part, value_...  23 us
    pallas_call x1, Pallas kernels, last(): pl.pallas_call(last_kernel, grid=(tokens // size,), in_specs=[rows] * 5 +...  18.3 us
  transfers between devices with their start and end apart: 10, of which 2 were waited for; matrix products, arithmetic and copies ran while one was open for 3% of the time, Pallas kernels for 49%

profile of v2, /device:TPU:0, one launch (start us, length us, event | category | flops | bytes accessed | tf_op | source)
XLA Modules:
  0.0 620.1 jit_solution(621582114436571726)
XLA Ops:
  9.8 2.0 convert_reduce_fusion
  12.6 1.7 copy-done.4
  14.3 7.0 %shard_map.229 = bf16[2048,768]{1,0:T(8,128)(2,1)} custom-call(s32[1,1536]{1,0:T(1,128)S(1)} %compare_select_fusion.slot_ref, bf16[1536,768]{1,0:T(8,128)(2,1)S(1)} %copy-done.4), custom_call_target="tpu_custom_call" | custom-call | flops 4831838208 | bytes 5505024 | tf_op jit(solution)/shard_map/pallas_call | solution.py:107
  21.3 8.5 %shard_map.230 = (bf16[1536,768]{1,0:T(8,128)(2,1)}, bf16[1536,768]{1,0:T(8,128)(2,1)}, bf16[1536,768]{1,0:T(8,128)(2,1)}) custom-call(bf16[1536,768]{1,0:T(8,128)(2,1)} %x_ref.5, f32[1,768]{1,0:T(1,128)S(1)} %broadcast_in_dim.14.gain_ref, bf16[768,768]{1,0:T(8,128)(2,1)S(1)} %copy-done.6, bf16[768,768]{1,0:T(8,128)(2,1)S(1)} %copy-done.8, ...), custom_call_target="tpu_custom_call" | custom-call | flops 5435817984 | bytes 9437184 | tf_op jit(solution)/shard_map/pallas_call | solution.py:134
  29.8 41.3 %shard_map.231 = (bf16[1536,768]{1,0:T(8,128)(2,1)S(1)}, f32[6,3,2,512]{3,2,1,0:T(2,128)S(1)}, bf16[4,8,64,768]{3,2,1,0:T(8,128)(2,1)}) custom-call(f32[12,8,128]{2,1,0:T(8,128)S(1)} %concatenate.21.lines_ref, bf16[8,4,64,768]{3,2,1,0:T(8,128)(2,1)} %bitcast.37, bf16[1536,768]{1,0:T(8,128)(2,1)} %get-tuple-element.52.q_ref, ...), custom_call_target="tpu_custom_call" | custom-call | flops 9663676416 | bytes 9437184 | tf_op jit(solution)/shard_map/pallas_call | solution.py:258
  71.2 4.7 constant_dynamic-slice_fusion.2
  75.9 3.6 collective-permute-start.2
  80.8 14.5 %shard_map.232 = (f32[1536,768]{1,0:T(8,128)}, bf16[1536,768]{1,0:T(8,128)(2,1)}, f32[1536,32]{1,0:T(8,128)S(1)}, f32[1536,1]{1,0:T(8,128)S(1)}, f32[1,1536]{1,0:T(1,128)S(1)}) custom-call(bf16[1536,768]{1,0:T(8,128)(2,1)} %copy-done.2, bf16[1536,768]{1,0:T(8,128)(2,1)} %x_ref.5, bf16[768,768]{1,0:T(8,128)(2,1)S(1)} %copy-done.3, ...), custom_call_target="tpu_custom_call" | custom-call | flops 1811939328 | bytes 11796480 | tf_op jit(solution)/shard_map/pallas_call | solution.py:419
  97.1 1.7 copy-done.5
  98.7 9.2 %shard_map.233 = bf16[2048,768]{1,0:T(8,128)(2,1)} custom-call(s32[1,1536]{1,0:T(1,128)S(1)} %compare_select_fusion.slot_ref, f32[1,1536]{1,0:T(1,128)S(1)} %get-tuple-element.59.gate_ref, bf16[1536,768]{1,0:T(8,128)(2,1)S(1)} %copy-done.5), custom_call_target="tpu_custom_call" | custom-call | flops 4831838208 | bytes 5505024 | tf_op jit(solution)/shard_map/pallas_call | solution.py:111
  107.9 109.3 %shard_map.234 = (bf16[4,8,64,768]{3,2,1,0:T(8,128)(2,1)S(1)}, bf16[8,4,64,768]{3,2,1,0:T(8,128)(2,1)}, bf16[8,4,64,768]{3,2,1,0:T(8,128)(2,1)}) custom-call(bf16[8,4,64,768]{3,2,1,0:T(8,128)(2,1)} %bitcast.38, bf16[4,512,768]{2,1,0:T(8,128)(2,1)} %bitcast.32, bf16[4,768,3072]{2,1,0:T(8,128)(2,1)} %refs_8_.1, bf16[4,3072,768]{2,1,0:T(8,128)(2,1)} %refs_9_.1), custom_call_target="tpu_custom_call" | custom-call | flops 38654705664 | bytes 50331648 | tf_op jit(solution)/shard_map/pallas_call | solution.py:552
  218.7 3.6 collective-permute-start.5
  226.8 32.9 %shard_map.235 = (bf16[1536,768]{1,0:T(8,128)(2,1)}, f32[1536,768]{1,0:T(8,128)}, bf16[1536,768]{1,0:T(8,128)(2,1)}, f32[768,768]{1,0:T(8,128)}, f32[768,32]{1,0:T(8,128)}, /*index=5*/f32[1,768]{1,0:T(1,128)S(1)}) custom-call(s32[1536,1]{1,0:T(8,128)S(1)} %fusion.slot_ref, s32[1536,1]{1,0:T(8,128)S(1)} %copy.55.expert_ref, f32[1536,1]{1,0:T(8,128)S(1)} %copy-done.15, ...), custom_call_target="tpu_custom_call" | custom-call | flops 13287555072 | bytes 25165824 | tf_op jit(solution)/shard_map/pallas_call | solution.py:756
  259.8 64.5 %shard_map.236 = (bf16[1536,768]{1,0:T(8,128)(2,1)S(1)}, bf16[1536,768]{1,0:T(8,128)(2,1)}, bf16[1536,768]{1,0:T(8,128)(2,1)}, f32[12,8,128]{2,1,0:T(8,128)S(1)}) custom-call(f32[12,8,128]{2,1,0:T(8,128)S(1)} %concatenate.21.lines_ref, bf16[1536,768]{1,0:T(8,128)(2,1)} %get-tuple-element.52.q_ref, bf16[1536,768]{1,0:T(8,128)(2,1)} %get-tuple-element.53.k_ref, ...), custom_call_target="tpu_custom_call" | custom-call | flops 24159191040 | bytes 16515072 | tf_op jit(solution)/shard_map/pallas_call | solution.py:368
  325.8 18.3 %shard_map.237 = (f32[1536,768]{1,0:T(8,128)}, f32[768,768]{1,0:T(8,128)}, f32[768,768]{1,0:T(8,128)}, f32[768,768]{1,0:T(8,128)}, f32[1,768]{1,0:T(1,128)S(1)}) custom-call(bf16[1536,768]{1,0:T(8,128)(2,1)} %x_ref.5, f32[1536,768]{1,0:T(8,128)} %get-tuple-element.66.dh_ref, bf16[1536,768]{1,0:T(8,128)(2,1)} %copy-done.16, ...), custom_call_target="tpu_custom_call" | custom-call | flops 10871635968 | bytes 18874368 | tf_op jit(solution)/shard_map/pallas_call | solution.py:820
  350.5 9.7 %collective-permute-done.4.refs_2_ = bf16[2,512,768]{2,1,0:T(8,128)(2,1)} collective-permute-done((bf16[2,512,768]{2,1,0:T(8,128)(2,1)S(1)}, bf16[2,512,768]{2,1,0:T(8,128)(2,1)}, u32[]{:S(2)}, u32[]{:S(2)}) %collective-permute-start.4) | collective-permute-done | bytes 1572896 | tf_op jit(solution)/shard_map/ppermute | solution.py:878
  360.2 57.8 %shard_map.238 = (f32[4,768,768]{2,1,0:T(8,128)}, f32[4,768,768]{2,1,0:T(8,128)}, bf16[2,768,768]{2,1,0:T(8,128)(2,1)}, bf16[2,768,768]{2,1,0:T(8,128)(2,1)}) custom-call(s32[3]{0:T(128)S(1)} %pad_add_fusion.1.place_ref, bf16[2,512,768]{2,1,0:T(8,128)(2,1)S(1)} %get-tuple-element.136.refs_0_, bf16[2,512,768]{2,1,0:T(8,128)(2,1)} %collective-permute-done.3.refs_1_, ...), custom_call_target="tpu_custom_call" | custom-call | flops 38654705664 | bytes 40894464 | tf_op jit(solution)/shard_map/pallas_call | solution.py:633
  418.1 2.0 collective-permute-start.7
  420.5 154.8 %all-reduce.1 = (f32[768]{0:T(1024)}, f32[768]{0:T(1024)}, f32[32,12]{0,1:T(8,128)}) all-reduce(f32[768]{0:T(1024)S(1)} %reduce.2, f32[768]{0:T(1024)S(1)} %reduce.3, f32[32,12]{0,1:T(8,128)S(1)} %fusion.9), channel_id=1, replica_groups=mesh['exp'=8,'dp'=4] {'exp','dp'}, use_global_device_ids=true, to_apply=%region_5.6 | all-reduce | flops 1920 | bytes 15360 | tf_op jit(solution)/shard_map/psum | solution.py:929
  575.3 1.8 copy.67
  577.1 23.0 %all-reduce.8.cloned.1.call-done = (bf16[768,768]{1,0:T(8,128)(2,1)}, bf16[768,768]{1,0:T(8,128)(2,1)}, bf16[768,768]{1,0:T(8,128)(2,1)}, bf16[768,768]{1,0:T(8,128)(2,1)}) async-done(((bf16[768,768]{1,0:T(8,128)(2,1)}, bf16[768,768]{1,0:T(8,128)(2,1)}, bf16[768,768]{1,0:T(8,128)(2,1)}, bf16[768,768]{1,0:T(8,128)(2,1)}), (bf16[768,768]{1,0:T(8,128)(2,1)}, bf16[768,768]{1,0:T(8,128)(2,1)}, ...) | async-done | bytes 4718608 | tf_op jit(solution)/shard_map/psum | solution.py:926
  600.1 2.9 convert_element_type.94
  603.1 1.6 convert_element_type.96
  607.9 5.2 shard_map.239
  (104 shorter events, 23.9 us)
Async XLA Ops:
  7.2 568.1 %all-reduce.6.cloned.1.call-start = ((), (), s32[]{:S(2)}) async-start(), calls=%async_computation | async-start | bytes 786432 | tf_op jit(solution)/shard_map/psum | solution.py:929
  9.5 11.8 %copy-start.27 = (s32[512]{0:T(512)}, s32[512]{0:T(512)S(1)}, u32[]{:S(2)}) copy-start(s32[512]{0:T(512)S(1)} %fusion.15) | copy-start | bytes 6148
  14.3 7.0 %copy-start.6 = (bf16[768,768]{1,0:T(8,128)(2,1)S(1)}, bf16[768,768]{1,0:T(8,128)(2,1)}, u32[]{:S(2)}) copy-start(bf16[768,768]{1,0:T(8,128)(2,1)} %wq_ref.3) | copy-start | bytes 3538948
  14.3 7.0 %copy-start.8 = (bf16[768,768]{1,0:T(8,128)(2,1)S(1)}, bf16[768,768]{1,0:T(8,128)(2,1)}, u32[]{:S(2)}) copy-start(bf16[768,768]{1,0:T(8,128)(2,1)} %wk_ref.3) | copy-start | bytes 3538948
  14.3 7.0 %copy-start.10 = (bf16[768,768]{1,0:T(8,128)(2,1)S(1)}, bf16[768,768]{1,0:T(8,128)(2,1)}, u32[]{:S(2)}) copy-start(bf16[768,768]{1,0:T(8,128)(2,1)} %wv_ref.3) | copy-start | bytes 3538948
  71.2 9.1 %copy-start.24 = (s32[1536,1]{0,1:T(1,128)S(1)}, s32[1536,1]{0,1:T(1,128)}, u32[]{:S(2)}) copy-start(s32[1536,1]{0,1:T(1,128)} %param.25) | copy-start | bytes 18436
  71.2 9.4 %copy-start.26 = (f32[768]{0:T(1024)S(1)}, f32[768]{0:T(1024)}, u32[]{:S(2)}) copy-start(f32[768]{0:T(1024)} %param.20) | copy-start | bytes 9220
  71.2 9.4 %copy-start.25 = (f32[768,32]{0,1:T(8,128)S(1)}, f32[768,32]{0,1:T(8,128)}, u32[]{:S(2)}) copy-start(f32[768,32]{0,1:T(8,128)} %param.22) | copy-start | bytes 294916
  71.2 9.6 %copy-start.3 = (bf16[768,768]{1,0:T(8,128)(2,1)S(1)}, bf16[768,768]{1,0:T(8,128)(2,1)}, u32[]{:S(2)}) copy-start(bf16[768,768]{1,0:T(8,128)(2,1)} %wo_ref.3) | copy-start | bytes 3538948
  75.9 147.8 %collective-permute-start.2 = (bf16[2,512,768]{2,1,0:T(8,128)(2,1)}, bf16[2,512,768]{2,1,0:T(8,128)(2,1)}, u32[]{:S(2)}, u32[]{:S(2)}) collective-permute-start(bf16[2,512,768]{2,1,0:T(8,128)(2,1)} %get-tuple-element.137), channel_id=1, source_target_pairs={{0,3},{1,2},{2,1},{3,0},{4,7},{5,6},{6,5},{7,4},{8,11},{9,10},{10,... | collective-permute-start | bytes 4718600 | tf_op jit(solution)/shard_map/ppermute | solution.py:878
  79.5 145.0 %collective-permute-start = (bf16[2,512,768]{2,1,0:T(8,128)(2,1)}, bf16[2,512,768]{2,1,0:T(8,128)(2,1)}, u32[]{:S(2)}, u32[]{:S(2)}) collective-permute-start(bf16[2,512,768]{2,1,0:T(8,128)(2,1)} %get-tuple-element.137), channel_id=1, source_target_pairs={{0,1},{1,0},{2,3},{3,2},{4,5},{5,4},{6,7},{7,6},{8,9},{9,8},{10,11... | collective-permute-start | bytes 4718600 | tf_op jit(solution)/shard_map/ppermute | solution.py:878
  79.5 145.0 %collective-permute-start.1 = (bf16[2,512,768]{2,1,0:T(8,128)(2,1)}, bf16[2,512,768]{2,1,0:T(8,128)(2,1)}, u32[]{:S(2)}, u32[]{:S(2)}) collective-permute-start(bf16[2,512,768]{2,1,0:T(8,128)(2,1)} %get-tuple-element.82.refs_4_), channel_id=1, source_target_pairs={{0,2},{1,3},{2,0},{3,1},{4,6},{5,7},{6,4},{7,5},{8,10},{9,11},{10,... | collective-permute-start | bytes 4718600 | tf_op jit(solution)/shard_map/ppermute | solution.py:878
  218.7 131.8 %collective-permute-start.5 = (bf16[2,512,768]{2,1,0:T(8,128)(2,1)}, bf16[2,512,768]{2,1,0:T(8,128)(2,1)}, u32[]{:S(2)}, u32[]{:S(2)}) collective-permute-start(bf16[2,512,768]{2,1,0:T(8,128)(2,1)} %get-tuple-element.135), channel_id=1, source_target_pairs={{0,3},{1,2},{2,1},{3,0},{4,7},{5,6},{6,5},{7,4},{8,11},{9,10},{10,... | collective-permute-start | bytes 4718600 | tf_op jit(solution)/shard_map/ppermute | solution.py:878
  222.3 128.2 %collective-permute-start.3 = (bf16[2,512,768]{2,1,0:T(8,128)(2,1)}, bf16[2,512,768]{2,1,0:T(8,128)(2,1)}, u32[]{:S(2)}, u32[]{:S(2)}) collective-permute-start(bf16[2,512,768]{2,1,0:T(8,128)(2,1)} %get-tuple-element.135), channel_id=1, source_target_pairs={{0,1},{1,0},{2,3},{3,2},{4,5},{5,4},{6,7},{7,6},{8,9},{9,8},{10,11... | collective-permute-start | bytes 4718600 | tf_op jit(solution)/shard_map/ppermute | solution.py:878
  223.7 136.6 %collective-permute-start.4 = (bf16[2,512,768]{2,1,0:T(8,128)(2,1)S(1)}, bf16[2,512,768]{2,1,0:T(8,128)(2,1)}, u32[]{:S(2)}, u32[]{:S(2)}) collective-permute-start(bf16[2,512,768]{2,1,0:T(8,128)(2,1)S(1)} %get-tuple-element.136.refs_0_), channel_id=1, source_target_pairs={{0,2},{1,3},{2,0},{3,1},{4,6},{5,7},{6,4},{7,5},{8,10},{9,11},{10,... | collective-permute-start | bytes 4718600 | tf_op jit(solution)/shard_map/ppermute | solution.py:878
  259.7 340.4 %all-reduce.8.cloned.1.call-start = ((), (), s32[]{:S(2)}) async-start(), calls=%async_computation.1 | async-start | bytes 9437184 | tf_op jit(solution)/shard_map/psum | solution.py:926
  259.8 66.0 %copy-start.7 = (bf16[768,768]{1,0:T(8,128)(2,1)S(1)}, bf16[768,768]{1,0:T(8,128)(2,1)}, u32[]{:S(2)}) copy-start(bf16[768,768]{1,0:T(8,128)(2,1)} %wq_ref.3) | copy-start | bytes 3538948
  259.8 66.0 %copy-start.9 = (bf16[768,768]{1,0:T(8,128)(2,1)S(1)}, bf16[768,768]{1,0:T(8,128)(2,1)}, u32[]{:S(2)}) copy-start(bf16[768,768]{1,0:T(8,128)(2,1)} %wk_ref.3) | copy-start | bytes 3538948
  259.8 65.9 %copy-start.11 = (bf16[768,768]{1,0:T(8,128)(2,1)S(1)}, bf16[768,768]{1,0:T(8,128)(2,1)}, u32[]{:S(2)}) copy-start(bf16[768,768]{1,0:T(8,128)(2,1)} %wv_ref.3) | copy-start | bytes 3538948
  325.8 18.3 %copy-start.17 = (f32[768,768]{1,0:T(8,128)S(1)}, f32[768,768]{1,0:T(8,128)}, u32[]{:S(2)}) copy-start(f32[768,768]{1,0:T(8,128)} %get-tuple-element.76) | copy-start | bytes 7077892
  350.5 69.7 %copy-start.28 = (s32[512]{0:T(512)S(1)}, s32[512]{0:T(512)}, u32[]{:S(2)}) copy-start(s32[512]{0:T(512)} %copy-done.27) | copy-start | bytes 6148
  418.0 189.8 %collective-permute-start.6 = (bf16[2,768,768]{2,1,0:T(8,128)(2,1)}, bf16[2,768,768]{2,1,0:T(8,128)(2,1)S(1)}, u32[]{:S(2)}, u32[]{:S(2)}) collective-permute-start(bf16[2,768,768]{2,1,0:T(8,128)(2,1)} %get-tuple-element.88), channel_id=1, source_target_pairs={{0,1},{1,0},{2,3},{3,2},{4,5},{5,4},{6,7},{7,6},{8,9},{9,8},{10,11... | collective-permute-start | bytes 7077896 | tf_op jit(solution)/shard_map/ppermute | solution.py:921
  418.1 189.8 %collective-permute-start.7 = (bf16[2,768,768]{2,1,0:T(8,128)(2,1)}, bf16[2,768,768]{2,1,0:T(8,128)(2,1)}, u32[]{:S(2)}, u32[]{:S(2)}) collective-permute-start(bf16[2,768,768]{2,1,0:T(8,128)(2,1)} %get-tuple-element.89), channel_id=1, source_target_pairs={{0,1},{1,0},{2,3},{3,2},{4,5},{5,4},{6,7},{7,6},{8,9},{9,8},{10,11... | collective-permute-start | bytes 7077896 | tf_op jit(solution)/shard_map/ppermute | solution.py:921
  607.9 5.2 copy-start.1
  (15 other events, 28.4 us)
Sparse Core Ops, SparseCore 0:
  259.9 167.9 all-reduce.5
  435.6 164.4 all-reduce.7

commit v3 on v2

--- a/solution.py
+++ b/solution.py
@@ -585,116 +585,436 @@
     )(sent, c, w_in, w_out)
 
 
-def weights_kernel(parts, sources, capacity, padded, place_ref, *refs):
-    u_refs, c_refs = refs[:sources], refs[sources : 2 * sources]
-    first_ref, second_ref, own_in, own_out, far_in, far_out, in_sum, out_sum = refs[2 * sources :]
-    width, size = first_ref.shape[1:]
-    rows = u_refs[0].shape[1]
+def finish_kernel(steps, place_ref, *refs):
+    ins, outs, (a_out, b_out) = refs[:steps], refs[steps : 2 * steps], refs[2 * steps :]
+    for step in range(steps):
+
+        @pl.when(pl.program_id(0) == step)
+        def _(step=step):
+            a_out[0] = ins[step][...].astype(F32)
+            b_out[0] = outs[step][...].astype(F32)
+
+
+def finish(places, ins, outs):
+    steps = len(ins)
+    width, size = ins[0].shape
+
+    def whole(*shape):
+        return pl.BlockSpec(shape, lambda e, p: (0, 0))
+
+    def spec(*shape):
+        return pl.BlockSpec((1,) + shape, lambda e, p: (p[e], 0, 0))
+
+    return pl.pallas_call(
+        functools.partial(finish_kernel, steps),
+        grid_spec=pltpu.PrefetchScalarGridSpec(
+            num_scalar_prefetch=1,
+            grid=(steps,),
+            in_specs=[whole(width, size)] * steps + [whole(size, width)] * steps,
+            out_specs=[spec(width, size), spec(size, width)],
+        ),
+        out_shape=[
+            jax.ShapeDtypeStruct((steps, width, size), F32),
+            jax.ShapeDtypeStruct((steps, size, width), F32),
+        ],
+        compiler_params=params(),
+    )(places, *ins, *outs)
+
+
+def tail_kernel(parts, sources, experts, capacity, padded, *refs):
+    u_refs, refs = refs[:sources], refs[sources:]
+    c_refs, refs = refs[:sources], refs[sources:]
+    (
+        first_ref, second_ref, dense_o, dense_qkv, small_ref,
+        own_in_ref, own_out_ref, came_in_ref, came_out_ref, dense_ref, total_ref,
+        rows_u, rows_c, first_held, second_held, first_t, in_sum, out_sum, far_in, far_out, own_in, own_out,
+        dense, dense_came, dense_over_dp, small, small_came,
+        rows_sem, weight_sem, load_sem, far_send, far_recv, own_sem,
+        half_send, half_recv, over_send, over_recv, back_send, back_recv, small_send, small_recv, keep_sem,
+    ) = refs
+    rows, width = rows_u.shape[2:]
+    size = in_sum.shape[0]
     columns = size // parts
-    first_t = first_ref[0].T
-    for source in range(sources):
-        inputs, upstream = u_refs[source][0], c_refs[source][0]
+    exp_me, dp_me = lax.axis_index("exp"), lax.axis_index("dp")
+    exp_bits, dp_bits = half_send.shape[2], over_send.shape[0]
+    group, pair = dp_me % 2, dp_me // 2
+    mesh_id = pl.DeviceIdType.MESH
+
+    def exp_peer(bit):
+        return {"exp": flipped(exp_me, 1 << bit)}
+
+    def dp_peer(bit):
+        return {"dp": flipped(dp_me, 1 << bit)}
+
+    chain = dense.shape[0] // 2
+    bits = list(range(exp_bits))
+    split = 1 + (exp_bits - 1) // 2
+    orders = (bits, bits[:1] + bits[split:] + bits[1:split])
+
+    def region(which, depth):
+        start = which * chain
+        for level in range(depth):
+            start = start + (exp_me // (1 << orders[which][level])) % 2 * (chain >> (level + 1))
+        return pl.ds(pl.multiple_of(start, 16), chain >> depth)
+
+    def other_half(which, depth):
+        start = which * chain
+        for level in range(depth):
+            start = start + (exp_me // (1 << orders[which][level])) % 2 * (chain >> (level + 1))
+        start = start + (1 - (exp_me // (1 << orders[which][depth])) % 2) * (chain >> (depth + 1))
+        return pl.ds(pl.multiple_of(start, 16), chain >> (depth + 1))
+
+    def came(which, depth):
+        return pl.ds(which * chain + chain - (chain >> depth), chain >> (depth + 1))
+
+    def columns_of(side):
+        return pl.ds(side * (width // 2), width // 2)
+
+    def halving(side, which, depth):
+        return pltpu.make_async_remote_copy(
+            src_ref=dense.at[other_half(which, depth), columns_of(side)],
+            dst_ref=dense_came.at[came(which, depth), columns_of(side)],
+            send_sem=half_send.at[side, which, depth],
+            recv_sem=half_recv.at[side, which, depth],
+            device_id=exp_peer(orders[which][depth]),
+            device_id_type=mesh_id,
+        )
+
+    def over(side, which, bit):
+        mine = dense.at[region(which, exp_bits), columns_of(side)]
+        return pltpu.make_async_remote_copy(
+            src_ref=mine if bit == 0 else dense_over_dp.at[1, bit - 1, side, which],
+            dst_ref=dense_over_dp.at[0, bit, side, which],
+            send_sem=over_send.at[bit, side, which],
+            recv_sem=over_recv.at[bit, side, which],
+            device_id=dp_peer(dp_bits - 1 - bit),
+            device_id_type=mesh_id,
+        )
+
+    def keeping(side, which):
+        return pltpu.make_async_copy(
+            dense_over_dp.at[1, dp_bits - 1, side, which],
+            dense_ref.at[region(which, exp_bits), columns_of(side)],
+            keep_sem.at[side, which],
+        )
+
+    def returning(side, which, depth):
+        place = dense_ref.at[region(which, depth + 1), columns_of(side)]
+        return pltpu.make_async_remote_copy(
+            src_ref=place,
+            dst_ref=place,
+            send_sem=back_send.at[side, which, depth],
+            recv_sem=back_recv.at[side, which, depth],
+            device_id=exp_peer(orders[which][depth]),
+            device_id_type=mesh_id,
+        )
+
+    def small_copy(depth):
+        return pltpu.make_async_remote_copy(
+            src_ref=small.at[depth],
+            dst_ref=small_came.at[depth],
+            send_sem=small_send.at[depth],
+            recv_sem=small_recv.at[depth],
+            device_id=exp_peer(depth) if depth < exp_bits else dp_peer(depth - exp_bits),
+            device_id_type=mesh_id,
+        )
+
+    def loads():
+        return [
+            pltpu.make_async_copy(dense_o, dense.at[pl.ds(3 * width, width)], load_sem.at[0]),
+            pltpu.make_async_copy(dense_qkv, dense.at[pl.ds(0, 3 * width)], load_sem.at[1]),
+            pltpu.make_async_copy(small_ref, small.at[0], load_sem.at[2]),
+        ]
+
+    def add_small(depth):
+        small_copy(depth).wait_recv()
+        small[depth + 1] = small[depth] + small_came[depth]
+
+    def begin(side):
+        if side == 0:
+            for load in loads():
+                load.wait()
+            small_copy(0).start()
+        for which in range(2):
+            halving(side, which, 0).start()
+
+    def halve(depth):
+        def act(side):
+            for which in range(2):
+                halving(side, which, depth).wait_recv()
+                place, new, here = region(which, depth + 1), came(which, depth), columns_of(side)
+                dense[place, here] = (
+                    dense[place, here].astype(F32) + dense_came[new, here].astype(F32)
+                ).astype(BF)
+                if depth + 1 < exp_bits:
+                    halving(side, which, depth + 1).start()
+                else:
+                    over(side, which, 0).start()
+            if side == 0:
+                add_small(depth)
+                small_copy(depth + 1).start()
+
+        return act
+
+    def sum_over(bit):
+        def act(side):
+            for which in range(2):
+                over(side, which, bit).wait_recv()
+                if bit == 0:
+                    mine = dense[region(which, exp_bits), columns_of(side)]
+                else:
+                    mine = dense_over_dp[1, bit - 1, side, which]
+                dense_over_dp[1, bit, side, which] = (
+                    mine.astype(F32) + dense_over_dp[0, bit, side, which].astype(F32)
+                ).astype(BF)
+                if bit + 1 < dp_bits:
+                    over(side, which, bit + 1).start()
+                else:
+                    keeping(side, which).start()
+            if side == 0:
+                add_small(exp_bits + bit)
+                if bit + 1 < dp_bits:
+                    small_copy(exp_bits + bit + 1).start()
+            if bit + 1 == dp_bits:
+                for which in range(2):
+                    keeping(side, which).wait()
+                    returning(side, which, exp_bits - 1).start()
+
+        return act
+
+    def give_back(depth):
+        def act(side):
+            for which in range(2):
+                returning(side, which, depth).wait_recv()
+                if depth > 0:
+                    returning(side, which, depth - 1).start()
+
+        return act
+
+    stages = [begin] + [halve(depth) for depth in range(exp_bits)]
+    stages += [sum_over(bit) for bit in range(dp_bits)]
+    stages += [give_back(depth) for depth in reversed(range(exp_bits))]
+    stages = [functools.partial(stage, side) for stage in stages for side in range(2)]
+
+    steps, turns = 2 * experts, 2 * experts * sources
+
+    def rows_copy(source, expert):
+        return [
+            pltpu.make_async_copy(
+                u_refs[source].at[expert],
+                rows_u.at[source, expert],
+                rows_sem.at[0, source, expert],
+            ),
+            pltpu.make_async_copy(
+                c_refs[source].at[expert], rows_c.at[source, expert], rows_sem.at[1, source, expert]
+            ),
+        ]
+
+    def weight_copy(step):
+        far = step < experts
+        expert = group * experts + step % experts
+        place = (pair * 2 + jnp.where(far, 1 - group, group)) * size
+        place = pl.ds(pl.multiple_of(place, 128), size)
+        slot = step % 2
+        return [
+            pltpu.make_async_copy(
+                first_ref.at[expert, :, place], first_held.at[slot], weight_sem.at[0, slot]
+            ),
+            pltpu.make_async_copy(
+                second_ref.at[expert, place, :], second_held.at[slot], weight_sem.at[1, slot]
+            ),
+        ]
+
+    far_parts = far_send.shape[2]
+
+    def far_copy(index):
+        expert, kind, part = index // (2 * far_parts), index % 2, index // 2 % far_parts
+        held, target = ((far_in, came_in_ref), (far_out, came_out_ref))[kind]
+        lines = held.shape[1] // far_parts
+        place = pl.ds(part * lines, lines)
+        return pltpu.make_async_remote_copy(
+            src_ref=held.at[expert, place],
+            dst_ref=target.at[expert, place],
+            send_sem=far_send.at[expert, kind, part],
+            recv_sem=far_recv.at[expert, kind, part],
+            device_id=dp_peer(0),
+            device_id_type=mesh_id,
+        )
+
+    def own_copy(expert):
+        return [
+            pltpu.make_async_copy(held.at[expert], target.at[expert], own_sem.at[kind, expert])
+            for kind, (held, target) in enumerate(((own_in, own_in_ref), (own_out, own_out_ref)))
+        ]
+
+    for load in loads():
+        load.start()
+    for copy in weight_copy(0):
+        copy.start()
+    for expert in reversed(range(experts)):
+        for source in range(sources):
+            for copy in rows_copy(source, expert):
+                copy.start()
+    barrier = pltpu.get_barrier_semaphore()
+    for bit in range(exp_bits):
+        pl.semaphore_signal(barrier, inc=1, device_id=exp_peer(bit), device_id_type=mesh_id)
+    for bit in range(dp_bits):
+        pl.semaphore_signal(barrier, inc=1, device_id=dp_peer(bit), device_id_type=mesh_id)
+    pl.semaphore_wait(barrier, exp_bits + dp_bits)
+
+    places = [0, 0] + [2 + index + 2 * max(0, index // 2 - 2) for index in range(len(stages) - 2)]
+    places = [place for place in places if place < turns]
+    starts = {5: 2, 8: 3, 9: 4, 12: 5, 13: 6, 15: 7}
+    starts = {place: index for place, index in starts.items() if place < turns}
+    pieces = 2 * far_parts * experts
+
+    def turn(at, carry):
+        step, source = at // sources, at % sources
+        expert, slot = step % experts, step % 2
+        for place, stage in zip(places, stages):
+            pl.when(at == place)(stage)
+        for place, index in starts.items():
+            pl.when(at == place)(far_copy(index).start)
+
+        @pl.when(source == 0)
+        def _():
+            for copy in weight_copy(step):
+                copy.wait()
+
+            @pl.when(step + 1 < steps)
+            def _():
+                for copy in weight_copy(step + 1):
+                    copy.start()
+
+            first_t[...] = first_held[slot].T
+
+        for each_expert in range(experts):
+            for each in range(sources):
+
+                @pl.when(at == each_expert * sources + each)
+                def _(each=each, each_expert=each_expert):
+                    for copy in rows_copy(each, each_expert):
+                        copy.wait()
+
+        inputs, upstream = rows_u[source, expert], rows_c[source, expert]
         gate = jnp.zeros((1, rows), F32)
         for block in range(rows // padded):
             place = block * padded + capacity
             gate = gate + inputs[place : place + 1, :rows].astype(F32)
         for part in range(parts):
-            places = slice(part * columns, (part + 1) * columns)
-            value, slope = gelu_and_slope(mm_nt(first_t[places, :], inputs))
-            inner = (mm_nt(second_ref[0, places, :], upstream) * (slope * gate)).astype(BF)
+            here = slice(part * columns, (part + 1) * columns)
+            value, slope = gelu_and_slope(mm_nt(first_t[here, :], inputs))
+            inner = (mm_nt(second_held[slot, here, :], upstream) * (slope * gate)).astype(BF)
             in_term = mm(inner, inputs)
             out_term = mm((value * gate).astype(BF), upstream)
-            if source == 0:
-                in_sum[places, :] = in_term
-                out_sum[places, :] = out_term
-            else:
-                in_sum[places, :] += in_term
-                out_sum[places, :] += out_term
-    mine = pl.program_id(1) == place_ref[2]
-
-    @pl.when(mine)
-    def _():
-        own_in[0] = in_sum[...].T
-        own_out[0] = out_sum[...]
-
-    @pl.when(jnp.logical_not(mine))
-    def _():
-        far_in[0] = in_sum[...].T.astype(BF)
-        far_out[0] = out_sum[...].astype(BF)
-
-
-def weight_grads(place, us, cs, w_in, w_out, size, capacity, padded):
+            fresh = source == 0
+            in_sum[here, :] = jnp.where(fresh, 0.0, in_sum[here, :]) + in_term
+            out_sum[here, :] = jnp.where(fresh, 0.0, out_sum[here, :]) + out_term
+
+        for each in range(experts):
+
+            @pl.when((source == sources - 1) & (step == each))
+            def _(each=each):
+                far_in[each] = in_sum[...].T.astype(BF)
+                far_out[each] = out_sum[...].astype(BF)
+                if each == 0:
+                    for index in range(2):
+                        far_copy(index).start()
+
+            @pl.when((source == sources - 1) & (step == experts + each))
+            def _(each=each):
+                own_in[each] = in_sum[...].T.astype(BF)
+                own_out[each] = out_sum[...].astype(BF)
+                for copy in own_copy(each):
+                    copy.start()
+
+        return carry
+
+    lax.fori_loop(0, turns, turn, 0)
+    for index in range(2 + len(starts), pieces):
+        far_copy(index).start()
+    for stage in stages[len(places) :]:
+        stage()
+    total_ref[...] = small[exp_bits + dp_bits]
+    for index in range(pieces):
+        far_copy(index).wait()
+    for expert in range(experts):
+        for copy in own_copy(expert):
+            copy.wait()
+    for side in range(2):
+        for which in range(2):
+            for depth in range(exp_bits):
+                halving(side, which, depth).wait_send()
+                returning(side, which, depth).wait_send()
+            for bit in range(dp_bits):
+                over(side, which, bit).wait_send()
+    for depth in range(exp_bits + dp_bits):
+        small_copy(depth).wait_send()
+
+
+def tail(us, cs, w_in, w_out, size, dense_o, dense_qkv, small, capacity, padded, exp_n):
     sources = len(us)
     experts, rows, width = us[0].shape
-    local = w_in.shape[0]
-    block = pl.BlockSpec((1, rows, width), lambda e, f, p: (e, 0, 0))
-    tile = pl.BlockSpec((1, width, size), lambda e, f, p: (e, 0, 0))
-    turned = pl.BlockSpec((1, size, width), lambda e, f, p: (e, 0, 0))
+    far_parts = 4
+    exp_bits, dp_bits = exp_n.bit_length() - 1, sources.bit_length() - 1
+    lines = 4 * width
+    anywhere = pl.BlockSpec(memory_space=pl.ANY)
+    dma = pltpu.SemaphoreType.DMA
     return pl.pallas_call(
-        functools.partial(weights_kernel, 3, sources, capacity, padded),
-        grid_spec=pltpu.PrefetchScalarGridSpec(
-            num_scalar_prefetch=1,
-            grid=(experts, 2),
-            in_specs=[block] * (2 * sources)
-            + [
-                pl.BlockSpec((1, width, size), lambda e, f, p: (p[0] + e, 0, p[1] + f)),
-                pl.BlockSpec((1, size, width), lambda e, f, p: (p[0] + e, p[1] + f, 0)),
-            ],
-            out_specs=[
-                pl.BlockSpec((1, width, size), lambda e, f, p: (p[0] + e, 0, 0)),
-                pl.BlockSpec((1, size, width), lambda e, f, p: (p[0] + e, 0, 0)),
-                tile,
-                turned,
-            ],
-            scratch_shapes=[pltpu.VMEM((size, width), F32)] * 2,
-        ),
+        functools.partial(tail_kernel, 3, sources, experts, capacity, padded),
+        in_specs=[anywhere] * (2 * sources + 5),
+        out_specs=[anywhere] * 5 + [pl.BlockSpec(memory_space=pltpu.VMEM)],
         out_shape=[
-            jax.ShapeDtypeStruct((local, width, size), F32),
-            jax.ShapeDtypeStruct((local, size, width), F32),
             jax.ShapeDtypeStruct((experts, width, size), BF),
             jax.ShapeDtypeStruct((experts, size, width), BF),
+            jax.ShapeDtypeStruct((experts, width, size), BF),
+            jax.ShapeDtypeStruct((experts, size, width), BF),
+            jax.ShapeDtypeStruct((lines, width), BF),
+            jax.ShapeDtypeStruct(small.shape, F32),
         ],
-        compiler_params=params(),
-        cost_estimate=pl.CostEstimate(
-            flops=16 * sources * experts * rows * width * size,
-            bytes_accessed=4 * experts * (sources * rows * width + 6 * size * width),
-            transcendentals=2 * sources * experts * rows * size,
+        scratch_shapes=[
+            pltpu.VMEM((sources, experts, rows, width), BF),
+            pltpu.VMEM((sources, experts, rows, width), BF),
+            pltpu.VMEM((2, width, size), BF),
+            pltpu.VMEM((2, size, width), BF),
+            pltpu.VMEM((size, width), BF),
+            pltpu.VMEM((size, width), F32),
+            pltpu.VMEM((size, width), F32),
+            pltpu.VMEM((experts, width, size), BF),
+            pltpu.VMEM((experts, size, width), BF),
+            pltpu.VMEM((experts, width, size), BF),
+            pltpu.VMEM((experts, size, width), BF),
+            pltpu.VMEM((lines, width), BF),
+            pltpu.VMEM((lines, width), BF),
+            pltpu.VMEM((2, dp_bits, 2, 2, lines // 2 >> exp_bits, width // 2), BF),
+            pltpu.VMEM((exp_bits + dp_bits + 1,) + small.shape, F32),
+            pltpu.VMEM((exp_bits + dp_bits,) + small.shape, F32),
+            dma((2, sources, experts)),
+            dma((2, 2)),
+            dma((3,)),
+            dma((experts, 2, far_parts)),
+            dma((experts, 2, far_parts)),
+            dma((2, experts)),
+            dma((2, 2, exp_bits)),
+            dma((2, 2, exp_bits)),
+            dma((dp_bits, 2, 2)),
+            dma((dp_bits, 2, 2)),
+            dma((2, 2, exp_bits)),
+            dma((2, 2, exp_bits)),
+            dma((exp_bits + dp_bits,)),
+            dma((exp_bits + dp_bits,)),
+            dma((2, 2)),
+        ],
+        compiler_params=pltpu.CompilerParams(
+            vmem_limit_bytes=58 * 2**20, collective_id=2, has_side_effects=True
         ),
-    )(place, *us, *cs, w_in, w_out)
-
-
-def finish_kernel(place_ref, a_ref, b_ref, x_ref, y_ref, a_out, b_out):
-    a_out[...] = x_ref[...].astype(F32)
-    b_out[...] = y_ref[...].astype(F32)
-
-
-def finish(place, own_in, own_out, came_in, came_out):
-    experts, width, size = came_in.shape
-
-    def spec(shape, moved):
-        return pl.BlockSpec((1,) + shape, lambda e, p: ((p[0] if moved else 0) + e, 0, 0))
-
-    return pl.pallas_call(
-        finish_kernel,
-        grid_spec=pltpu.PrefetchScalarGridSpec(
-            num_scalar_prefetch=1,
-            grid=(experts,),
-            in_specs=[pl.BlockSpec(memory_space=pl.ANY)] * 2
-            + [spec((width, size), False), spec((size, width), False)],
-            out_specs=[spec((width, size), True), spec((size, width), True)],
-        ),
-        out_shape=[
-            jax.ShapeDtypeStruct(own_in.shape, F32),
-            jax.ShapeDtypeStruct(own_out.shape, F32),
-        ],
-        input_output_aliases={1: 0, 2: 1},
-        compiler_params=params(),
-    )(place, own_in, own_out, came_in, came_out)
+        cost_estimate=pl.CostEstimate(flops=0, bytes_accessed=2**16, transcendentals=0),
+    )(*us, *cs, w_in, w_out, dense_o, dense_qkv, small)
 
 
 def combine_kernel(
     slot_ref, expert_ref, gate_ref, probs_ref, h_ref, c_ref, o_ref, e_ref, d_ref, wo_ref, wr_ref, gain_ref,
-    mixed_ref, dh_ref, do_ref, wo_sum, wr_sum, gain_sum,
+    mixed_ref, dh_ref, do_ref, wo_ref_out, wr_sum, gain_sum, wo_sum,
 ):
     step = pl.program_id(0)
     tokens, slots = slot_ref.shape[0], e_ref.shape[0]
@@ -737,9 +1057,13 @@
 
     wo_sum[...] += mm(o_ref[...].T, low)
     wr_sum[...] += jnp.dot(
-        (unit * gain).T, logit_grad, precision=FULL_PRECISION, preferred_element_type=F32
+        logit_grad.T, unit * gain, precision=FULL_PRECISION, preferred_element_type=F32
     )
     gain_sum[...] += jnp.sum(normed_grad * unit, axis=0, keepdims=True)
+
+    @pl.when(step == pl.num_programs(0) - 1)
+    def _():
+        wo_ref_out[...] = wo_sum[...].astype(BF)
 
 
 def combine(slot, expert, gate, probs, h, c, o, e_out, du, wo, wr, gain):
@@ -759,16 +1083,17 @@
         in_specs=[rows(1), rows(1), rows(1), rows(experts), rows(width), rows(width), rows(width)]
         + [whole(slots, width), whole(slots, width), whole(width, width), whole(width, experts)]
         + [whole(1, width)],
-        out_specs=[rows(width), rows(width), rows(width), whole(width, width), whole(width, experts)]
+        out_specs=[rows(width), rows(width), rows(width), whole(width, width), whole(experts, width)]
         + [whole(1, width)],
         out_shape=[
             jax.ShapeDtypeStruct((tokens, width), BF),
             jax.ShapeDtypeStruct((tokens, width), F32),
             jax.ShapeDtypeStruct((tokens, width), BF),
-            jax.ShapeDtypeStruct((width, width), F32),
-            jax.ShapeDtypeStruct((width, experts), F32),
+            jax.ShapeDtypeStruct((width, width), BF),
+            jax.ShapeDtypeStruct((experts, width), F32),
             jax.ShapeDtypeStruct((1, width), F32),
         ],
+        scratch_shapes=[pltpu.VMEM((width, width), F32)],
         compiler_params=params(),
         cost_estimate=pl.CostEstimate(
             flops=4 * tokens * width * (slots + width),
@@ -780,9 +1105,10 @@
 
 def last_kernel(
     x_ref, dh_ref, dq_ref, dk_ref, dv_ref, wq_ref, wk_ref, wv_ref, gain_ref,
-    grad_ref, q_sum, k_sum, v_sum, gain_sum,
+    grad_ref, sums_ref, gain_sum, q_sum, k_sum, v_sum,
 ):
     step = pl.program_id(0)
+    width = x_ref.shape[1]
 
     @pl.when(step == 0)
     def _():
@@ -810,6 +1136,11 @@
     )
     gain_sum[...] += jnp.sum(normed_grad * unit, axis=0, keepdims=True)
 
+    @pl.when(step == pl.num_programs(0) - 1)
+    def _():
+        for which, total in enumerate((q_sum, k_sum, v_sum)):
+            sums_ref[which * width : (which + 1) * width, :] = total[...].astype(BF)
+
 
 def last(x, dh, dq, dk, dv, wq, wk, wv, gain):
     tokens, width = x.shape
@@ -821,10 +1152,13 @@
         last_kernel,
         grid=(tokens // size,),
         in_specs=[rows] * 5 + [square] * 3 + [one],
-        out_specs=[rows, square, square, square, one],
-        out_shape=[jax.ShapeDtypeStruct((tokens, width), F32)]
-        + [jax.ShapeDtypeStruct((width, width), F32)] * 3
-        + [jax.ShapeDtypeStruct((1, width), F32)],
+        out_specs=[rows, pl.BlockSpec((3 * width, width), lambda t: (0, 0)), one],
+        out_shape=[
+            jax.ShapeDtypeStruct((tokens, width), F32),
+            jax.ShapeDtypeStruct((3 * width, width), BF),
+            jax.ShapeDtypeStruct((1, width), F32),
+        ],
+        scratch_shapes=[pltpu.VMEM((width, width), F32)] * 3,
         compiler_params=params(),
         cost_estimate=pl.CostEstimate(
             flops=12 * tokens * width * width, bytes_accessed=16 * tokens * width, transcendentals=0
@@ -869,14 +1203,18 @@
     half = local // 2
     group = dp_me % 2
 
-    def over_dp(rows):
-        mine = lax.dynamic_slice_in_dim(rows, group * half, half, 0)
-        other = lax.dynamic_slice_in_dim(rows, (1 - group) * half, half, 0)
+    def over_dp(mine, other):
         pieces = [mine]
         for step in range(1, dp_n):
             pairs = [(i, i ^ step) for i in range(dp_n)]
             pieces.append(lax.ppermute(other if step % 2 else mine, "dp", pairs))
         return pieces
+
+    def groups(rows, start, count):
+        return (
+            lax.dynamic_slice_in_dim(rows, group * half + start, count, 0),
+            lax.dynamic_slice_in_dim(rows, (1 - group) * half + start, count, 0),
+        )
 
     lines = jnp.dot(
         relative_bias_table.T, diagonal_onehot(buckets).T, precision=FULL_PRECISION
@@ -887,7 +1225,7 @@
     c_sent = dispatch(slot_row, cotangent, exp_n, block).reshape(exp_n, local, padded, width)
     context, lse, c_rows = attention(lines, c_sent, q, k, v)
     c_rows = c_rows.reshape(local, exp_n * padded, width)
-    c_all = over_dp(c_rows)
+    c_all = over_dp(*groups(c_rows, 0, half))
     mixed, u, probs, gate, gate_row = router(
         context, tokens, w_output, gain_ffn, w_router, expert_index
     )
@@ -897,44 +1235,47 @@
     )
     e_back, *c_all = lax.optimization_barrier((e_back, *c_all))
     e_back, d_back = e_back.reshape(exp_n * block, width), d_back.reshape(exp_n * block, width)
-    u_all = over_dp(u_rows.reshape(local, exp_n * padded, width))
+    u_rows = u_rows.reshape(local, exp_n * padded, width)
+    u_all = over_dp(*groups(u_rows, 0, half))
     mixed_out, mixed_grad, context_grad, output_part, router_part, norm_ffn_part = combine(
         slot_column, expert_index, gate, probs, mixed, cotangent, context,
         e_back, d_back, w_output, w_router, gain_ffn,
     )
     query_grad, key_grad, value_grad, sums = attention_back(lines, q, k, v, context_grad, lse)
+    size = w_in.shape[2] // dp_n
     table_part = jnp.dot(
         diagonal_onehot(buckets).T,
         sums[:, :4].reshape(HEADS, 4 * TILE).T,
         precision=FULL_PRECISION,
     )
-    grad_tokens, query_part, key_part, value_part, norm_attn_part = last(
+    grad_tokens, qkv_part, norm_attn_part = last(
         tokens, mixed_grad, query_grad, key_grad, value_grad, w_query, w_key, w_value, gain_attn
     )
 
-    size = w_in.shape[2] // dp_n
-    where = jnp.stack([group * half, (dp_me // 2) * 2, group]).astype(jnp.int32)
-    own_in, own_out, far_in, far_out = weight_grads(
-        where, u_all, c_all, w_in, w_out, size, capacity, padded
-    )
-    swap = [(i, i ^ 1) for i in range(dp_n)]
-    came_in, came_out = lax.ppermute(far_in, "dp", swap), lax.ppermute(far_out, "dp", swap)
-    there = ((1 - group) * half).astype(jnp.int32)[None]
-    grad_in, grad_out = finish(there, own_in, own_out, came_in, came_out)
-
-    axes = ("exp", "dp")
-    big = lax.psum(
-        tuple(part.astype(BF) for part in (query_part, key_part, value_part, output_part)), axes
-    )
-    small = lax.psum((norm_attn_part, norm_ffn_part, table_part, router_part), axes)
+    table_line = jnp.pad(table_part.reshape(1, -1), ((0, 0), (0, width - table_part.size)))
+    small = jnp.concatenate([router_part, norm_attn_part, norm_ffn_part, table_line], axis=0)
+    small = jnp.pad(small, ((0, -small.shape[0] % 8), (0, 0)))
+    own_in, own_out, came_in, came_out, dense, total = tail(
+        u_all, c_all, w_in, w_out, size, output_part, qkv_part, small, capacity, padded, exp_n
+    )
+    experts = jnp.arange(local, dtype=jnp.int32)
+    grad_in, grad_out = finish(
+        jnp.where(group == 0, experts, (experts + half) % local),
+        list(own_in) + list(came_in),
+        list(own_out) + list(came_out),
+    )
+    dense = dense.reshape(4, width, width).astype(F32)
     return (
         mixed_out,
         grad_tokens,
-        *(part.astype(F32) for part in big),
-        small[0][0],
-        small[1][0],
-        small[2],
-        small[3],
+        dense[0],
+        dense[1],
+        dense[2],
+        dense[3],
+        total[all_experts],
+        total[all_experts + 1],
+        total[all_experts + 2, : table_part.size].reshape(table_part.shape),
+        total[:all_experts].T,
         grad_in,
         grad_out,
     )

time: 627 us -> 535 us (0.85); the launches traced: 620 us -> 535 us
  blocking collectives: 155 us -> 0 us
  Pallas kernels: 368 us -> 458 us
  local copies, waits for them, and re-layouts: 20.4 us -> 34.5 us
  between operations: 14.6 us -> 1.02 us
  other arithmetic: 17.4 us -> 5.13 us
    psum x1 -> x0, blocking collectives: 155 us -> none  [per_device(): lax.psum((norm_attn_part, norm_ffn_part, table_part, router_part), axes)]
    pallas_call x2, Pallas kernels: 63 us -> 166 us  [the longest x1 156 us: tail(): pl.pallas_call(functools.partial(tail_kernel, 3, sources, experts, capaci...]
    psum x2 -> x0, waiting for transfers between devices: 23 us -> none  [the longest x1 23 us: per_device(): lax.psum(tuple((part.astype(BF) for part in (query_part, key_part, value_...]
    ppermute x6, waiting for transfers between devices: 9.72 us -> 26.8 us  [over_dp(): pieces.append(lax.ppermute(other if step % 2 else mine, 'dp', pairs))]
    pallas_call x1, Pallas kernels: 64.5 us -> 51.3 us  [attention_back(): pl.pallas_call(attention_back_kernel, grid=(pairs, seqs), in_specs=[lines...]
    convert_element_type x8 -> x0, other arithmetic: 12.2 us -> none  [the longest x4 7.67 us: per_device(): part.astype(F32)]
    another operation x0 -> x5, local copies, waits for them, and re-layouts: none -> 6.95 us  [the longest x1 3.3 us: per_device(): list(came_out)]
    unnamed x63 -> x51, local copies, waits for them, and re-layouts: 13.2 us -> 11.5 us
  transfers between devices with their start and end apart: 10 -> 6, of which waited for: 2 -> 1; matrix products, arithmetic and copies ran while one was open for 3% -> 1% of each run, Pallas kernels for 49% -> 44%
where the time goes in v3:
time: 535 us
  Pallas kernels  458 us (86%)
  local copies, waits for them, and re-layouts  34.5 us (6%)
  waiting for transfers between devices  26.8 us (5%)
  starting transfers between devices  8.53 us (2%)
    pallas_call x1, Pallas kernels, tail(): pl.pallas_call(functools.partial(tail_kernel, 3, sources, experts, capaci...  156 us
    pallas_call x1, Pallas kernels, expert_pass(): pl.pallas_call(functools.partial(expert_kernel, 3), grid=(experts, hidden...  109 us
    pallas_call x1, Pallas kernels, attention_back(): pl.pallas_call(attention_back_kernel, grid=(pairs, seqs), in_specs=[lines...  51.3 us
    pallas_call x1, Pallas kernels, attention(): pl.pallas_call(attention_kernel, grid=(pairs, seqs), in_specs=[pl.BlockSp...  41.4 us
    pallas_call x1, Pallas kernels, combine(): pl.pallas_call(combine_kernel, grid=(tokens // size,), in_specs=[rows(1),...  31.6 us
    ppermute x6, waiting for transfers between devices, over_dp(): pieces.append(lax.ppermute(other if step % 2 else mine, 'dp', pairs))  26.8 us
    pallas_call x1, Pallas kernels, last(): pl.pallas_call(last_kernel, grid=(tokens // size,), in_specs=[rows] * 5 +...  19.3 us
    pallas_call x1, Pallas kernels, router(): pl.pallas_call(router_kernel, grid=(tokens // size,), in_specs=[rows(widt...  14.5 us
  transfers between devices with their start and end apart: 6, of which 1 were waited for; matrix products, arithmetic and copies ran while one was open for 1% of the time, Pallas kernels for 44%

profile of v3, /device:TPU:0, one launch (start us, length us, event | category | flops | bytes accessed | tf_op | source)
XLA Modules:
  0.0 534.7 jit_solution(17910981964867764677)
XLA Ops:
  3.2 2.0 convert_reduce_fusion
  6.0 1.7 copy-done.4
  7.7 7.1 %shard_map.229 = bf16[2048,768]{1,0:T(8,128)(2,1)} custom-call(s32[1,1536]{1,0:T(1,128)S(1)} %compare_select_fusion.slot_ref, bf16[1536,768]{1,0:T(8,128)(2,1)S(1)} %copy-done.4), custom_call_target="tpu_custom_call" | custom-call | flops 4831838208 | bytes 5505024 | tf_op jit(solution)/shard_map/pallas_call | solution.py:107
  14.8 8.5 %shard_map.230 = (bf16[1536,768]{1,0:T(8,128)(2,1)}, bf16[1536,768]{1,0:T(8,128)(2,1)}, bf16[1536,768]{1,0:T(8,128)(2,1)}) custom-call(bf16[1536,768]{1,0:T(8,128)(2,1)} %x_ref.5, f32[1,768]{1,0:T(1,128)S(1)} %broadcast_in_dim.12.gain_ref, bf16[768,768]{1,0:T(8,128)(2,1)S(1)} %copy-done.6, bf16[768,768]{1,0:T(8,128)(2,1)S(1)} %copy-done.8, ...), custom_call_target="tpu_custom_call" | custom-call | flops 5435817984 | bytes 9437184 | tf_op jit(solution)/shard_map/pallas_call | solution.py:134
  23.4 41.4 %shard_map.231 = (bf16[1536,768]{1,0:T(8,128)(2,1)S(1)}, f32[6,3,2,512]{3,2,1,0:T(2,128)S(1)}, bf16[4,8,64,768]{3,2,1,0:T(8,128)(2,1)}) custom-call(f32[12,8,128]{2,1,0:T(8,128)S(1)} %concatenate.24.lines_ref, bf16[8,4,64,768]{3,2,1,0:T(8,128)(2,1)} %bitcast.53, bf16[1536,768]{1,0:T(8,128)(2,1)} %get-tuple-element.52.q_ref, ...), custom_call_target="tpu_custom_call" | custom-call | flops 9663676416 | bytes 9437184 | tf_op jit(solution)/shard_map/pallas_call | solution.py:258
  64.8 4.7 constant_dynamic-slice_fusion.2
  69.5 1.6 collective-permute-start
  71.1 2.5 collective-permute-start.2
  74.2 14.5 %shard_map.232 = (f32[1536,768]{1,0:T(8,128)}, bf16[1536,768]{1,0:T(8,128)(2,1)}, f32[1536,32]{1,0:T(8,128)S(1)}, f32[1536,1]{1,0:T(8,128)S(1)}, f32[1,1536]{1,0:T(1,128)S(1)}) custom-call(bf16[1536,768]{1,0:T(8,128)(2,1)} %copy-done.2, bf16[1536,768]{1,0:T(8,128)(2,1)} %x_ref.5, bf16[768,768]{1,0:T(8,128)(2,1)S(1)} %copy-done.3, ...), custom_call_target="tpu_custom_call" | custom-call | flops 1811939328 | bytes 11796480 | tf_op jit(solution)/shard_map/pallas_call | solution.py:419
  89.6 1.7 copy-done.5
  91.3 9.2 %shard_map.233 = bf16[2048,768]{1,0:T(8,128)(2,1)} custom-call(s32[1,1536]{1,0:T(1,128)S(1)} %compare_select_fusion.slot_ref, f32[1,1536]{1,0:T(1,128)S(1)} %get-tuple-element.59.gate_ref, bf16[1536,768]{1,0:T(8,128)(2,1)S(1)} %copy-done.5), custom_call_target="tpu_custom_call" | custom-call | flops 4831838208 | bytes 5505024 | tf_op jit(solution)/shard_map/pallas_call | solution.py:111
  100.5 109.1 %shard_map.234 = (bf16[4,8,64,768]{3,2,1,0:T(8,128)(2,1)S(1)}, bf16[8,4,64,768]{3,2,1,0:T(8,128)(2,1)}, bf16[8,4,64,768]{3,2,1,0:T(8,128)(2,1)}) custom-call(bf16[8,4,64,768]{3,2,1,0:T(8,128)(2,1)} %bitcast.54, bf16[4,512,768]{2,1,0:T(8,128)(2,1)} %bitcast.48, bf16[4,768,3072]{2,1,0:T(8,128)(2,1)} %refs_8_.1, bf16[4,3072,768]{2,1,0:T(8,128)(2,1)} %refs_9_.1), custom_call_target="tpu_custom_call" | custom-call | flops 38654705664 | bytes 50331648 | tf_op jit(solution)/shard_map/pallas_call | solution.py:552
  209.6 1.9 constant_dynamic-slice_fusion
  211.5 1.8 collective-permute-start.3
  213.3 2.5 collective-permute-start.5
  217.2 31.6 %shard_map.235 = (bf16[1536,768]{1,0:T(8,128)(2,1)}, f32[1536,768]{1,0:T(8,128)}, bf16[1536,768]{1,0:T(8,128)(2,1)}, bf16[768,768]{1,0:T(8,128)(2,1)}, f32[32,768]{1,0:T(8,128)S(1)}, /*index=5*/f32[1,768]{1,0:T(1,128)S(1)}) custom-call(s32[1536,1]{1,0:T(8,128)S(1)} %fusion.slot_ref, s32[1536,1]{1,0:T(8,128)S(1)} %copy.55.expert_ref, ...), custom_call_target="tpu_custom_call" | custom-call | flops 13287555072 | bytes 25165824 | tf_op jit(solution)/shard_map/pallas_call | solution.py:1080
  248.9 51.3 %shard_map.236 = (bf16[1536,768]{1,0:T(8,128)(2,1)S(1)}, bf16[1536,768]{1,0:T(8,128)(2,1)}, bf16[1536,768]{1,0:T(8,128)(2,1)}, f32[12,8,128]{2,1,0:T(8,128)S(1)}) custom-call(f32[12,8,128]{2,1,0:T(8,128)S(1)} %concatenate.24.lines_ref, bf16[1536,768]{1,0:T(8,128)(2,1)} %get-tuple-element.52.q_ref, bf16[1536,768]{1,0:T(8,128)(2,1)} %get-tuple-element.53.k_ref, ...), custom_call_target="tpu_custom_call" | custom-call | flops 24159191040 | bytes 16515072 | tf_op jit(solution)/shard_map/pallas_call | solution.py:368
  304.6 19.3 %shard_map.237 = (f32[1536,768]{1,0:T(8,128)}, bf16[2304,768]{1,0:T(8,128)(2,1)}, f32[1,768]{1,0:T(1,128)S(1)}) custom-call(bf16[1536,768]{1,0:T(8,128)(2,1)} %x_ref.5, f32[1536,768]{1,0:T(8,128)} %get-tuple-element.66.dh_ref, bf16[1536,768]{1,0:T(8,128)(2,1)} %copy-done.14, bf16[1536,768]{1,0:T(8,128)(2,1)} %get-tuple-element.70.dk_ref, ...), custom_call_target="tpu_custom_call" | custom-call | flops 10871635968 | bytes 18874368 | tf_op jit(solution)/shard_map/pallas_call | solution.py:1151
  324.6 26.8 %collective-permute-done.4.refs_2_ = bf16[2,512,768]{2,1,0:T(8,128)(2,1)} collective-permute-done((bf16[2,512,768]{2,1,0:T(8,128)(2,1)}, bf16[2,512,768]{2,1,0:T(8,128)(2,1)}, u32[]{:S(2)}, u32[]{:S(2)}) %collective-permute-start.4) | collective-permute-done | bytes 1572896 | tf_op jit(solution)/shard_map/ppermute | solution.py:1210
  351.3 155.9 %shard_map.238 = (bf16[2,768,768]{2,1,0:T(8,128)(2,1)}, bf16[2,768,768]{2,1,0:T(8,128)(2,1)}, bf16[2,768,768]{2,1,0:T(8,128)(2,1)}, bf16[2,768,768]{2,1,0:T(8,12...) custom-call(bf16[2,512,768]{2,1,0:T(8,128)(2,1)} %get-tuple-element.135.refs_0_, ...), custom_call_target="tpu_custom_call" | custom-call | bytes 65536 | tf_op jit(solution)/shard_map/pallas_call | solution.py:963
  507.3 1.5 slice_bitcast_fusion.8
  511.0 3.3 slice_bitcast_fusion
  518.7 3.8 fusion.19
  524.6 10.1 %shard_map.239 = (f32[4,768,768]{2,1,0:T(8,128)}, f32[4,768,768]{2,1,0:T(8,128)}) custom-call(s32[4]{0:T(128)S(1)} %broadcast_select_fusion.place_ref, bf16[768,768]{1,0:T(8,128)(2,1)S(1)} %get-tuple-element.145.refs_0_, bf16[768,768]{1,0:T(8,128)(2,1)S(1)} %get-tuple-element.144.refs_1_, bf16[768,768]{1,0:T(8,128)(2,1)S(1)} %get-tuple-element.143.refs_2_, ...), custom_call_target="tpu_custom_call" | custom-call | tf_op jit(solution)/shard_map/pallas_call | solution.py:608
  (84 shorter events, 19.9 us)
Async XLA Ops:
  0.6 2.2 copy-start
  6.0 1.7 copy-start.4
  7.6 7.2 %copy-start.6 = (bf16[768,768]{1,0:T(8,128)(2,1)S(1)}, bf16[768,768]{1,0:T(8,128)(2,1)}, u32[]{:S(2)}) copy-start(bf16[768,768]{1,0:T(8,128)(2,1)} %wq_ref.3) | copy-start | bytes 3538948
  7.7 7.2 %copy-start.8 = (bf16[768,768]{1,0:T(8,128)(2,1)S(1)}, bf16[768,768]{1,0:T(8,128)(2,1)}, u32[]{:S(2)}) copy-start(bf16[768,768]{1,0:T(8,128)(2,1)} %wk_ref.3) | copy-start | bytes 3538948
  7.7 7.2 %copy-start.10 = (bf16[768,768]{1,0:T(8,128)(2,1)S(1)}, bf16[768,768]{1,0:T(8,128)(2,1)}, u32[]{:S(2)}) copy-start(bf16[768,768]{1,0:T(8,128)(2,1)} %wv_ref.3) | copy-start | bytes 3538948
  64.8 4.8 copy-start.2
  64.8 8.9 %copy-start.18 = (s32[1536,1]{0,1:T(1,128)S(1)}, s32[1536,1]{0,1:T(1,128)}, u32[]{:S(2)}) copy-start(s32[1536,1]{0,1:T(1,128)} %param.25) | copy-start | bytes 18436
  64.8 9.2 %copy-start.19 = (f32[768,32]{0,1:T(8,128)S(1)}, f32[768,32]{0,1:T(8,128)}, u32[]{:S(2)}) copy-start(f32[768,32]{0,1:T(8,128)} %param.22) | copy-start | bytes 294916
  64.8 9.4 %copy-start.20 = (f32[768]{0:T(1024)S(1)}, f32[768]{0:T(1024)}, u32[]{:S(2)}) copy-start(f32[768]{0:T(1024)} %param.20) | copy-start | bytes 9220
  64.8 9.4 %copy-start.3 = (bf16[768,768]{1,0:T(8,128)(2,1)S(1)}, bf16[768,768]{1,0:T(8,128)(2,1)}, u32[]{:S(2)}) copy-start(bf16[768,768]{1,0:T(8,128)(2,1)} %wo_ref.3) | copy-start | bytes 3538948
  69.5 147.6 %collective-permute-start = (bf16[2,512,768]{2,1,0:T(8,128)(2,1)}, bf16[2,512,768]{2,1,0:T(8,128)(2,1)}, u32[]{:S(2)}, u32[]{:S(2)}) collective-permute-start(bf16[2,512,768]{2,1,0:T(8,128)(2,1)} %get-tuple-element.136), channel_id=1, source_target_pairs={{0,1},{1,0},{2,3},{3,2},{4,5},{5,4},{6,7},{7,6},{8,9},{9,8},{10,11... | collective-permute-start | bytes 4718600 | tf_op jit(solution)/shard_map/ppermute | solution.py:1210
  71.1 146.1 %collective-permute-start.2 = (bf16[2,512,768]{2,1,0:T(8,128)(2,1)}, bf16[2,512,768]{2,1,0:T(8,128)(2,1)}, u32[]{:S(2)}, u32[]{:S(2)}) collective-permute-start(bf16[2,512,768]{2,1,0:T(8,128)(2,1)} %get-tuple-element.136), channel_id=1, source_target_pairs={{0,3},{1,2},{2,1},{3,0},{4,7},{5,6},{6,5},{7,4},{8,11},{9,10},{10,... | collective-permute-start | bytes 4718600 | tf_op jit(solution)/shard_map/ppermute | solution.py:1210
  73.6 143.6 %collective-permute-start.1 = (bf16[2,512,768]{2,1,0:T(8,128)(2,1)}, bf16[2,512,768]{2,1,0:T(8,128)(2,1)}, u32[]{:S(2)}, u32[]{:S(2)}) collective-permute-start(bf16[2,512,768]{2,1,0:T(8,128)(2,1)} %get-tuple-element.74.refs_4_), channel_id=1, source_target_pairs={{0,2},{1,3},{2,0},{3,1},{4,6},{5,7},{6,4},{7,5},{8,10},{9,11},{10,... | collective-permute-start | bytes 4718600 | tf_op jit(solution)/shard_map/ppermute | solution.py:1210
  209.6 7.6 %copy-start.13 = (f32[1536,1]{1,0:T(8,128)S(1)}, f32[1536,1]{1,0:T(8,128)}, u32[]{:S(2)}) copy-start(f32[1536,1]{1,0:T(8,128)} %copy-done.12) | copy-start | bytes 18436
  211.5 113.1 %collective-permute-start.3 = (bf16[2,512,768]{2,1,0:T(8,128)(2,1)}, bf16[2,512,768]{2,1,0:T(8,128)(2,1)}, u32[]{:S(2)}, u32[]{:S(2)}) collective-permute-start(bf16[2,512,768]{2,1,0:T(8,128)(2,1)} %get-tuple-element.134), channel_id=1, source_target_pairs={{0,1},{1,0},{2,3},{3,2},{4,5},{5,4},{6,7},{7,6},{8,9},{9,8},{10,11... | collective-permute-start | bytes 4718600 | tf_op jit(solution)/shard_map/ppermute | solution.py:1210
  213.3 138.0 %collective-permute-start.5 = (bf16[2,512,768]{2,1,0:T(8,128)(2,1)}, bf16[2,512,768]{2,1,0:T(8,128)(2,1)}, u32[]{:S(2)}, u32[]{:S(2)}) collective-permute-start(bf16[2,512,768]{2,1,0:T(8,128)(2,1)} %get-tuple-element.134), channel_id=1, source_target_pairs={{0,3},{1,2},{2,1},{3,0},{4,7},{5,6},{6,5},{7,4},{8,11},{9,10},{10,... | collective-permute-start | bytes 4718600 | tf_op jit(solution)/shard_map/ppermute | solution.py:1210
  217.1 134.2 %collective-permute-start.4 = (bf16[2,512,768]{2,1,0:T(8,128)(2,1)}, bf16[2,512,768]{2,1,0:T(8,128)(2,1)}, u32[]{:S(2)}, u32[]{:S(2)}) collective-permute-start(bf16[2,512,768]{2,1,0:T(8,128)(2,1)} %get-tuple-element.135.refs_0_), channel_id=1, source_target_pairs={{0,2},{1,3},{2,0},{3,1},{4,6},{5,7},{6,4},{7,5},{8,10},{9,11},{10,... | collective-permute-start | bytes 4718600 | tf_op jit(solution)/shard_map/ppermute | solution.py:1210
  248.9 53.2 %copy-start.7 = (bf16[768,768]{1,0:T(8,128)(2,1)S(1)}, bf16[768,768]{1,0:T(8,128)(2,1)}, u32[]{:S(2)}) copy-start(bf16[768,768]{1,0:T(8,128)(2,1)} %wq_ref.3) | copy-start | bytes 3538948
  511.0 3.3 copy-start.17
  511.0 4.8 copy-start.16
  514.3 4.3 slice-start
  515.8 2.6 copy-start.15
  515.8 2.8 slice-start.1
  524.6 10.1 %copy-start.1 = (f32[32,12]{0,1:T(8,128)S(1)}, f32[32,12]{0,1:T(8,128)}, u32[]{:S(2)}) copy-start(f32[32,12]{0,1:T(8,128)} %param.21) | copy-start | bytes 4612
  (5 other events, 6.5 us)

commit v4 on v3

--- a/solution.py
+++ b/solution.py
@@ -20,7 +20,8 @@
 CHUNK = 256
 GELU_A = 0.7978845608028654
 GELU_B = 0.044715 * GELU_A
-VMEM_MIB = 50
+VMEM_MIB = 58
+NO_COST = pl.CostEstimate(flops=0, bytes_accessed=2**16, transcendentals=0)
 
 
 def params(**more):
@@ -42,6 +43,49 @@
             index = index + bit * (1 - 2 * ((index // bit) % 2))
         bit *= 2
     return index
+
+
+def greet(me, blocks, others=()):
+    barrier = pltpu.get_barrier_semaphore()
+    devices = [{"exp": flipped(me, block)} for block in range(1, blocks)] + list(others)
+    for device in devices:
+        pl.semaphore_signal(barrier, inc=1, device_id=device, device_id_type=pl.DeviceIdType.MESH)
+    pl.semaphore_wait(barrier, len(devices))
+
+
+def spread(me, sent, expert, came, sems, index):
+    local_sem, send_sem, recv_sem = sems
+    copies = [pltpu.make_async_copy(sent.at[0, expert], came.at[0], local_sem.at[index])]
+    for block in range(1, came.shape[0]):
+        copies.append(
+            pltpu.make_async_remote_copy(
+                src_ref=sent.at[block, expert],
+                dst_ref=came.at[block],
+                send_sem=send_sem.at[index, block],
+                recv_sem=recv_sem.at[index, block],
+                device_id={"exp": flipped(me, block)},
+                device_id_type=pl.DeviceIdType.MESH,
+            )
+        )
+    return copies
+
+
+def spread_sems(count, blocks):
+    dma = pltpu.SemaphoreType.DMA
+    return [dma((count,)), dma((count, blocks)), dma((count, blocks))]
+
+
+def halves(array):
+    high = array.astype(BF)
+    return high, (array - high.astype(F32)).astype(BF)
+
+
+def as_column(line):
+    size = line.shape[1]
+    diagonal = lax.broadcasted_iota(jnp.int32, (size, size), 0) == lax.broadcasted_iota(
+        jnp.int32, (size, size), 1
+    )
+    return jnp.sum(jnp.where(diagonal, line, 0.0), axis=1, keepdims=True)
 
 
 def bucket_of(offset):
@@ -98,11 +142,7 @@
     )
     line = pl.BlockSpec((1, tokens), lambda k: (0, 0))
     full = pl.BlockSpec((tokens, width), lambda k: (0, 0))
-    cost = pl.CostEstimate(
-        flops=2 * blocks * block * tokens * width,
-        bytes_accessed=2 * width * (tokens + blocks * block),
-        transcendentals=0,
-    )
+    cost = NO_COST
     if gate is None:
         return pl.pallas_call(
             dispatch_kernel, in_specs=[line, full], compiler_params=params(), cost_estimate=cost, **grid_spec
@@ -138,9 +178,7 @@
         out_specs=[rows] * 3,
         out_shape=[jax.ShapeDtypeStruct((tokens, width), BF)] * 3,
         compiler_params=params(),
-        cost_estimate=pl.CostEstimate(
-            flops=6 * tokens * width * width, bytes_accessed=8 * tokens * width, transcendentals=0
-        ),
+        cost_estimate=NO_COST,
     )(x, gain, wq, wk, wv)
 
 
@@ -274,18 +312,48 @@
             pltpu.SemaphoreType.DMA((blocks,)),
         ],
         compiler_params=params(collective_id=1, has_side_effects=True),
-        cost_estimate=pl.CostEstimate(
-            flops=16 * pairs * seqs * SEQ * SEQ * PAIR,
-            bytes_accessed=8 * tokens * width,
-            transcendentals=2 * pairs * seqs * SEQ * SEQ,
-        ),
+        cost_estimate=NO_COST,
     )(lines, sent, q, k, v)
 
 
-def attention_back_kernel(
-    lines_ref, q_ref, k_ref, v_ref, do_ref, lse_ref, dq_ref, dk_ref, dv_ref, sums_ref, bias_ref, diag_ref
-):
-    seq = pl.program_id(1)
+def attention_back_kernel(parts, swaps, lines_ref, q_ref, k_ref, v_ref, do_ref, lse_ref, *refs):
+    sent_refs, swap_refs, refs = refs[:parts], refs[parts : parts + swaps], refs[parts + swaps :]
+    dq_ref, dk_ref, dv_ref, sums_ref = refs[:4]
+    came_refs, got_refs, refs = refs[4 : 4 + parts], refs[4 + parts : 4 + parts + swaps], refs[4 + parts + swaps :]
+    bias_ref, diag_ref, *sems = refs
+    sems, swap_send, swap_recv = sems[:3], sems[3], sems[4]
+    pair, seq = pl.program_id(0), pl.program_id(1)
+    blocks, expert = came_refs[0].shape[0], sent_refs[0].shape[1] - 1
+    me = lax.axis_index("exp")
+    partner = {"dp": flipped(lax.axis_index("dp"), 1)}
+
+    def transfers():
+        copies = []
+        for index in range(swaps):
+            copies.append(
+                pltpu.make_async_remote_copy(
+                    src_ref=swap_refs[index],
+                    dst_ref=got_refs[index],
+                    send_sem=swap_send.at[index],
+                    recv_sem=swap_recv.at[index],
+                    device_id=partner,
+                    device_id_type=pl.DeviceIdType.MESH,
+                )
+            )
+        for part in range(parts):
+            copies += spread(me, sent_refs[part], expert, came_refs[part], sems, part)
+        return copies
+
+    @pl.when((pair == 0) & (seq == 0))
+    def _():
+        greet(me, blocks, [partner])
+        for copy in transfers():
+            copy.start()
+
+    @pl.when((pair == pl.num_programs(0) - 1) & (seq == pl.num_programs(1) - 1))
+    def _():
+        for copy in transfers():
+            copy.wait()
 
     @pl.when(seq == 0)
     def _():
@@ -360,27 +428,35 @@
             )
 
 
-def attention_back(lines, q, k, v, do, lse):
+def attention_back(lines, q, k, v, do, lse, sent, swapped):
+    parts, swaps = len(sent), len(swapped)
+    blocks, _, padded, _ = sent[0].shape
+    anywhere = pl.BlockSpec(memory_space=pl.ANY)
     tokens, width = q.shape
     seqs, pairs = tokens // SEQ, width // PAIR
     block = pl.BlockSpec((SEQ, PAIR), lambda h, s: (s, h))
     lines_spec = pl.BlockSpec((2, 8, TILE), lambda h, s: (h, 0, 0))
     return pl.pallas_call(
-        attention_back_kernel,
+        functools.partial(attention_back_kernel, parts, swaps),
         grid=(pairs, seqs),
         in_specs=[lines_spec, block, block, block, block]
-        + [pl.BlockSpec((1, 1, 2, SEQ), lambda h, s: (h, s, 0, 0))],
-        out_specs=[block, block, block, lines_spec],
+        + [pl.BlockSpec((1, 1, 2, SEQ), lambda h, s: (h, s, 0, 0))]
+        + [anywhere] * (parts + swaps),
+        out_specs=[block, block, block, lines_spec] + [anywhere] * (parts + swaps),
         out_shape=[jax.ShapeDtypeStruct((tokens, width), BF)] * 3
-        + [jax.ShapeDtypeStruct((2 * pairs, 8, TILE), F32)],
-        scratch_shapes=[pltpu.VMEM((2, SEQ, SEQ), F32), pltpu.VMEM((2, 5, TILE, TILE), F32)],
-        compiler_params=params(),
-        cost_estimate=pl.CostEstimate(
-            flops=40 * pairs * seqs * SEQ * SEQ * PAIR,
-            bytes_accessed=14 * tokens * width,
-            transcendentals=2 * pairs * seqs * SEQ * SEQ,
-        ),
-    )(lines, q, k, v, do, lse)
+        + [jax.ShapeDtypeStruct((2 * pairs, 8, TILE), F32)]
+        + [jax.ShapeDtypeStruct((blocks, padded, width), BF)] * parts
+        + [jax.ShapeDtypeStruct(array.shape, BF) for array in swapped],
+        scratch_shapes=[
+            pltpu.VMEM((2, SEQ, SEQ), F32),
+            pltpu.VMEM((2, 5, TILE, TILE), F32),
+            *spread_sems(parts, blocks),
+            pltpu.SemaphoreType.DMA((swaps,)),
+            pltpu.SemaphoreType.DMA((swaps,)),
+        ],
+        compiler_params=params(collective_id=4, has_side_effects=True),
+        cost_estimate=NO_COST,
+    )(lines, q, k, v, do, lse, *sent, *swapped)
 
 
 def router_kernel(
@@ -391,7 +467,9 @@
     inv = lax.rsqrt(jnp.mean(mixed * mixed, axis=-1, keepdims=True) + EPSILON)
     normed = mixed * inv * gain_ref[...]
     u_ref[...] = normed.astype(BF)
-    logits = jnp.dot(normed, wr_ref[...], precision=FULL_PRECISION, preferred_element_type=F32)
+    high, low = halves(normed)
+    wr_high, wr_low = halves(wr_ref[...])
+    logits = mm(high, wr_high) + (mm(high, wr_low) + mm(low, wr_high))
     spread = jnp.exp(logits - jnp.max(logits, axis=-1, keepdims=True))
     probs = spread / jnp.sum(spread, axis=-1, keepdims=True)
     probs_ref[...] = probs
@@ -431,9 +509,7 @@
             jax.ShapeDtypeStruct((1, tokens), F32),
         ],
         compiler_params=params(),
-        cost_estimate=pl.CostEstimate(
-            flops=2 * tokens * width * width, bytes_accessed=10 * tokens * width, transcendentals=0
-        ),
+        cost_estimate=NO_COST,
     )(o, x, wo, gain, wr, expert)
 
 
@@ -445,75 +521,25 @@
     return value, slope
 
 
-def expert_kernel(
-    parts, sent_ref, c_ref, first_ref, second_ref, u_ref, e_ref, d_ref,
-    rows_ref, e_sum, d_sum, e_held, d_held, local_sem, send_sem, recv_sem, back_send, back_recv,
-):
-    expert, step = pl.program_id(0), pl.program_id(1)
-    experts, last_step = pl.num_programs(0), pl.num_programs(1) - 1
-    blocks, padded, width = rows_ref.shape[1:]
-    me = lax.axis_index("exp")
+def send_back(me, held, target, which, place, sems, kind):
+    send_sem, recv_sem, local_sem = sems
+    copies = [pltpu.make_async_copy(held.at[0], target.at[0, which], local_sem.at[kind, place])]
+    for block in range(1, held.shape[0]):
+        copies.append(
+            pltpu.make_async_remote_copy(
+                src_ref=held.at[block],
+                dst_ref=target.at[block, which],
+                send_sem=send_sem.at[kind, place, block],
+                recv_sem=recv_sem.at[kind, place, block],
+                device_id={"exp": flipped(me, block)},
+                device_id_type=pl.DeviceIdType.MESH,
+            )
+        )
+    return copies
+
+
+def expert_step(parts, rows, upstream, first_ref, second_ref, e_sum, d_sum):
     columns = first_ref.shape[2] // parts
-
-    def there(block):
-        return {"exp": flipped(me, block)}
-
-    def outgoing(which, block):
-        return pltpu.make_async_remote_copy(
-            src_ref=sent_ref.at[block, which],
-            dst_ref=rows_ref.at[which, block],
-            send_sem=send_sem.at[which, block],
-            recv_sem=recv_sem.at[which, block],
-            device_id=there(block),
-            device_id_type=pl.DeviceIdType.MESH,
-        )
-
-    def returning(kind, which, block):
-        held, target = (e_held, e_ref) if kind == 0 else (d_held, d_ref)
-        return pltpu.make_async_remote_copy(
-            src_ref=held.at[which, block],
-            dst_ref=target.at[block, which],
-            send_sem=back_send.at[kind, which, block],
-            recv_sem=back_recv.at[kind, which, block],
-            device_id=there(block),
-            device_id_type=pl.DeviceIdType.MESH,
-        )
-
-    def own_in(which):
-        return pltpu.make_async_copy(sent_ref.at[0, which], rows_ref.at[which, 0], local_sem.at[0, which])
-
-    def own_back(kind, which):
-        held, target = (e_held, e_ref) if kind == 0 else (d_held, d_ref)
-        return pltpu.make_async_copy(
-            held.at[which, 0], target.at[0, which], local_sem.at[1 + kind, which]
-        )
-
-    def keep(which):
-        return pltpu.make_async_copy(rows_ref.at[which], u_ref.at[which], local_sem.at[3, which])
-
-    @pl.when((expert == 0) & (step == 0))
-    def _():
-        barrier = pltpu.get_barrier_semaphore()
-        for block in range(1, blocks):
-            pl.semaphore_signal(
-                barrier, inc=1, device_id=there(block), device_id_type=pl.DeviceIdType.MESH
-            )
-        pl.semaphore_wait(barrier, blocks - 1)
-        for which in range(rows_ref.shape[0]):
-            own_in(which).start()
-            for block in range(1, blocks):
-                outgoing(which, block).start()
-
-    @pl.when(step == 0)
-    def _():
-        own_in(expert).wait()
-        for block in range(1, blocks):
-            outgoing(expert, block).wait_recv()
-        keep(expert).start()
-        e_sum[...] = jnp.zeros_like(e_sum)
-        d_sum[...] = jnp.zeros_like(d_sum)
-
-    rows, upstream = rows_ref[expert].reshape(blocks * padded, width), c_ref[0]
     for part in range(parts):
         places = slice(part * columns, (part + 1) * columns)
         first, second = first_ref[0, :, places], second_ref[0, places, :]
@@ -522,25 +548,150 @@
         e_sum[...] += mm(value.astype(BF), second)
         d_sum[...] += mm_nt(inner, first)
 
+
+def expert_kernel(
+    parts, sent_ref, c_ref, first_ref, second_ref, *refs
+):
+    expert, step = pl.program_id(0), pl.program_id(1)
+    count, last_step = pl.num_programs(0), pl.num_programs(1) - 1
+    all_experts = count + 1
+    u_refs, u_last, refs = refs[:all_experts], refs[all_experts], refs[all_experts + 1 :]
+    e_kept, d_kept, e_ref, d_ref, rows_ref, e_sum, d_sum, e_held, d_held = refs[:9]
+    local_sem, send_sem, recv_sem, back_send, back_recv, back_local = refs[9:]
+    _, blocks, padded, width = rows_ref.shape
+    me = lax.axis_index("exp")
+    group, half = lax.axis_index("dp") % 2, all_experts // 2
+    sems = (back_send, back_recv, back_local)
+
+    def outgoing(which, block):
+        return pltpu.make_async_remote_copy(
+            src_ref=sent_ref.at[block, which],
+            dst_ref=rows_ref.at[which, block],
+            send_sem=send_sem.at[which, block],
+            recv_sem=recv_sem.at[which, block],
+            device_id={"exp": flipped(me, block)},
+            device_id_type=pl.DeviceIdType.MESH,
+        )
+
+    def own_in(which):
+        return pltpu.make_async_copy(sent_ref.at[0, which], rows_ref.at[which, 0], local_sem.at[0, which])
+
+    def keep(which, act):
+        for each in range(2):
+            target = u_refs[(which // half + each) % 2 * half + which % half]
+
+            @pl.when(group == each)
+            def _(target=target):
+                act(pltpu.make_async_copy(rows_ref.at[which], target, local_sem.at[1, which]))
+
+        if which == all_experts - 1:
+            act(pltpu.make_async_copy(rows_ref.at[which], u_last, local_sem.at[2, 0]))
+
+    def arrive(which):
+        own_in(which).wait()
+        for block in range(1, blocks):
+            outgoing(which, block).wait_recv()
+        keep(which, lambda copy: copy.start())
+
+    def keep_result(which):
+        return [
+            pltpu.make_async_copy(e_held.at[which], e_kept.at[which - 1], local_sem.at[2, which]),
+            pltpu.make_async_copy(d_held.at[which], d_kept.at[which - 1], local_sem.at[3, which]),
+        ]
+
+    def back():
+        return send_back(me, e_held.at[0], e_ref, 0, 0, sems, 0) + send_back(
+            me, d_held.at[0], d_ref, 0, 0, sems, 1
+        )
+
+    @pl.when((expert == 0) & (step == 0))
+    def _():
+        greet(me, blocks)
+        for which in range(all_experts):
+            own_in(which).start()
+            for block in range(1, blocks):
+                outgoing(which, block).start()
+
+    @pl.when(step == 0)
+    def _():
+        for which in range(all_experts - 1):
+
+            @pl.when(expert == which)
+            def _(which=which):
+                arrive(which)
+
+        e_sum[...] = jnp.zeros_like(e_sum)
+        d_sum[...] = jnp.zeros_like(d_sum)
+
+    rows = rows_ref[expert].reshape(blocks * padded, width)
+    expert_step(parts, rows, c_ref[0], first_ref, second_ref, e_sum, d_sum)
+
     @pl.when(step == last_step)
     def _():
         e_held[expert] = e_sum[...].astype(BF).reshape(blocks, padded, width)
         d_held[expert] = d_sum[...].astype(BF).reshape(blocks, padded, width)
-        for kind in range(2):
-            own_back(kind, expert).start()
-            for block in range(1, blocks):
-                returning(kind, expert, block).start()
-
-    @pl.when((step == last_step) & (expert == experts - 1))
-    def _():
-        for which in range(rows_ref.shape[0]):
-            keep(which).wait()
+
+        @pl.when(expert == 0)
+        def _():
+            for copy in back():
+                copy.start()
+
+        for which in range(1, all_experts - 1):
+
+            @pl.when(expert == which)
+            def _(which=which):
+                for copy in keep_result(which):
+                    copy.start()
+
+    @pl.when((step == last_step) & (expert == count - 1))
+    def _():
+        arrive(all_experts - 1)
+        for which in range(all_experts):
+            keep(which, lambda copy: copy.wait())
             for block in range(1, blocks):
                 outgoing(which, block).wait_send()
-            for kind in range(2):
-                own_back(kind, which).wait()
-                for block in range(1, blocks):
-                    returning(kind, which, block).wait()
+        for which in range(1, all_experts - 1):
+            for copy in keep_result(which):
+                copy.wait()
+        for copy in back():
+            copy.wait()
+
+
+def expert_rest_kernel(
+    parts, kept, u_ref, c_ref, first_ref, second_ref, e_kept, d_kept, e_ref, d_ref,
+    e_sum, d_sum, e_held, d_held, back_send, back_recv, back_local,
+):
+    step, last_step = pl.program_id(0), pl.num_programs(0) - 1
+    blocks, padded, width = e_held.shape
+    me = lax.axis_index("exp")
+    sems = (back_send, back_recv, back_local)
+
+    def back(which):
+        e_from, d_from = (e_kept.at[which], d_kept.at[which]) if which < kept else (e_held, d_held)
+        return send_back(me, e_from, e_ref, which, which, sems, 0) + send_back(
+            me, d_from, d_ref, which, which, sems, 1
+        )
+
+    @pl.when(step == 0)
+    def _():
+        greet(me, blocks)
+        for which in range(kept):
+            for copy in back(which):
+                copy.start()
+        e_sum[...] = jnp.zeros_like(e_sum)
+        d_sum[...] = jnp.zeros_like(d_sum)
+
+    expert_step(parts, u_ref[...], c_ref[0], first_ref, second_ref, e_sum, d_sum)
+
+    @pl.when(step == last_step)
+    def _():
+        e_held[...] = e_sum[...].astype(BF).reshape(blocks, padded, width)
+        d_held[...] = d_sum[...].astype(BF).reshape(blocks, padded, width)
+        for copy in back(kept):
+            copy.start()
+        for which in range(kept + 1):
+            for copy in back(which):
+                copy.wait()
 
 
 def expert_pass(sent, c, w_in, w_out):
@@ -548,82 +699,181 @@
     hidden = w_in.shape[2]
     size = 768
     rows = blocks * padded
+    kept = experts - 2
     anywhere = pl.BlockSpec(memory_space=pl.ANY)
-    return pl.pallas_call(
+    dma = pltpu.SemaphoreType.DMA
+    *u_rows, u_last, e_kept, d_kept, e_first, d_first = pl.pallas_call(
         functools.partial(expert_kernel, 3),
-        grid=(experts, hidden // size),
+        grid=(experts - 1, hidden // size),
         in_specs=[
             anywhere,
             pl.BlockSpec((1, rows, width), lambda e, f: (e, 0, 0)),
             pl.BlockSpec((1, width, size), lambda e, f: (e, 0, f)),
             pl.BlockSpec((1, size, width), lambda e, f: (e, f, 0)),
         ],
-        out_specs=[anywhere] * 3,
-        out_shape=[
-            jax.ShapeDtypeStruct((experts, blocks, padded, width), BF),
-            jax.ShapeDtypeStruct(sent.shape, BF),
-            jax.ShapeDtypeStruct(sent.shape, BF),
+        out_specs=[anywhere] * (experts + 5),
+        out_shape=[jax.ShapeDtypeStruct((blocks, padded, width), BF)] * (experts + 1)
+        + [
+            jax.ShapeDtypeStruct((kept, blocks, padded, width), BF),
+            jax.ShapeDtypeStruct((kept, blocks, padded, width), BF),
+            jax.ShapeDtypeStruct((blocks, 1, padded, width), BF),
+            jax.ShapeDtypeStruct((blocks, 1, padded, width), BF),
         ],
         scratch_shapes=[
             pltpu.VMEM((experts, blocks, padded, width), BF),
             pltpu.VMEM((rows, width), F32),
             pltpu.VMEM((rows, width), F32),
-            pltpu.VMEM((experts, blocks, padded, width), BF),
-            pltpu.VMEM((experts, blocks, padded, width), BF),
-            pltpu.SemaphoreType.DMA((4, experts)),
-            pltpu.SemaphoreType.DMA((experts, blocks)),
-            pltpu.SemaphoreType.DMA((experts, blocks)),
-            pltpu.SemaphoreType.DMA((2, experts, blocks)),
-            pltpu.SemaphoreType.DMA((2, experts, blocks)),
+            pltpu.VMEM((experts - 1, blocks, padded, width), BF),
+            pltpu.VMEM((experts - 1, blocks, padded, width), BF),
+            dma((4, experts)),
+            dma((experts, blocks)),
+            dma((experts, blocks)),
+            dma((2, 1, blocks)),
+            dma((2, 1, blocks)),
+            dma((2, 1)),
         ],
         compiler_params=params(collective_id=0, has_side_effects=True),
+        cost_estimate=NO_COST,
+    )(sent, c, w_in, w_out)
+    u_rows = [part.reshape(rows, width) for part in u_rows]
+    last = experts - 1
+    e_rest, d_rest = pl.pallas_call(
+        functools.partial(expert_rest_kernel, 3, kept),
+        grid=(hidden // size,),
+        in_specs=[
+            pl.BlockSpec((rows, width), lambda f: (0, 0)),
+            pl.BlockSpec((1, rows, width), lambda f: (last, 0, 0)),
+            pl.BlockSpec((1, width, size), lambda f: (last, 0, f)),
+            pl.BlockSpec((1, size, width), lambda f: (last, f, 0)),
+            anywhere,
+            anywhere,
+        ],
+        out_specs=[anywhere] * 2,
+        out_shape=[jax.ShapeDtypeStruct((blocks, kept + 1, padded, width), BF)] * 2,
+        scratch_shapes=[
+            pltpu.VMEM((rows, width), F32),
+            pltpu.VMEM((rows, width), F32),
+            pltpu.VMEM((blocks, padded, width), BF),
+            pltpu.VMEM((blocks, padded, width), BF),
+            dma((2, kept + 1, blocks)),
+            dma((2, kept + 1, blocks)),
+            dma((2, kept + 1)),
+        ],
+        compiler_params=params(collective_id=3, has_side_effects=True),
         cost_estimate=pl.CostEstimate(
-            flops=8 * experts * rows * width * hidden,
-            bytes_accessed=4 * experts * width * (hidden + 2 * rows),
-            transcendentals=experts * rows * hidden,
+            flops=32 * rows * width * hidden, bytes_accessed=4 * width * hidden, transcendentals=0
         ),
-    )(sent, c, w_in, w_out)
-
-
-def finish_kernel(steps, place_ref, *refs):
-    ins, outs, (a_out, b_out) = refs[:steps], refs[steps : 2 * steps], refs[2 * steps :]
-    for step in range(steps):
+    )(u_last.reshape(rows, width), c, w_in, w_out, e_kept, d_kept)
+    return u_rows, (e_first, e_rest), (d_first, d_rest)
+
+
+def weights_kernel(parts, sources, capacity, padded, place_ref, *refs):
+    u_refs, c_refs = refs[:sources], refs[sources : 2 * sources]
+    first_ref, second_ref, far_in, far_out, in_sum, out_sum = refs[2 * sources :]
+    size = first_ref.shape[2]
+    rows = u_refs[0].shape[0]
+    columns = size // parts
+    first_t = first_ref[0].T
+    for source in range(sources):
+        inputs, upstream = u_refs[source][...], c_refs[source][...].reshape(u_refs[source].shape)
+        gate = jnp.zeros((1, rows), F32)
+        for block in range(rows // padded):
+            place = block * padded + capacity
+            gate = gate + inputs[place : place + 1, :rows].astype(F32)
+        for part in range(parts):
+            places = slice(part * columns, (part + 1) * columns)
+            value, slope = gelu_and_slope(mm_nt(first_t[places, :], inputs))
+            inner = (mm_nt(second_ref[0, places, :], upstream) * (slope * gate)).astype(BF)
+            in_term = mm(inner, inputs)
+            out_term = mm((value * gate).astype(BF), upstream)
+            if source == 0:
+                in_sum[places, :] = in_term
+                out_sum[places, :] = out_term
+            else:
+                in_sum[places, :] += in_term
+                out_sum[places, :] += out_term
+    far_in[...] = in_sum[...].T.astype(BF)
+    far_out[...] = out_sum[...].astype(BF)
+
+
+def weight_grads(place, us, c_rows, c_far, w_in, w_out, size, capacity, padded):
+    sources = len(us)
+    rows, width = us[0].shape
+    block = pl.BlockSpec((rows, width), lambda f, p: (0, 0))
+    return pl.pallas_call(
+        functools.partial(weights_kernel, 3, sources, capacity, padded),
+        grid_spec=pltpu.PrefetchScalarGridSpec(
+            num_scalar_prefetch=1,
+            grid=(1,),
+            in_specs=[block] * sources
+            + [pl.BlockSpec((1, rows, width), lambda f, p: (p[0], 0, 0))]
+            + [block] * (sources - 1)
+            + [
+                pl.BlockSpec((1, width, size), lambda f, p: (p[0], 0, p[1])),
+                pl.BlockSpec((1, size, width), lambda f, p: (p[0], p[1], 0)),
+            ],
+            out_specs=[
+                pl.BlockSpec((width, size), lambda f, p: (0, 0)),
+                pl.BlockSpec((size, width), lambda f, p: (0, 0)),
+            ],
+            scratch_shapes=[pltpu.VMEM((size, width), F32)] * 2,
+        ),
+        out_shape=[
+            jax.ShapeDtypeStruct((width, size), BF),
+            jax.ShapeDtypeStruct((size, width), BF),
+        ],
+        compiler_params=params(),
+        cost_estimate=NO_COST,
+    )(place, *us, c_rows, *c_far, w_in, w_out)
+
+
+def finish_kernel(half, place_ref, *refs):
+    own_in, own_out, refs = refs[0], refs[1], refs[2:]
+    came_in, came_out, dense_ref = refs[:half], refs[half : 2 * half], refs[2 * half]
+    a_out, b_out, *dense_outs = refs[2 * half + 1 :]
+    width = dense_ref.shape[1]
+    for step in range(2 * half):
 
         @pl.when(pl.program_id(0) == step)
         def _(step=step):
-            a_out[0] = ins[step][...].astype(F32)
-            b_out[0] = outs[step][...].astype(F32)
-
-
-def finish(places, ins, outs):
-    steps = len(ins)
-    width, size = ins[0].shape
+            a_out[0] = (own_in[step] if step < half else came_in[step - half][...]).astype(F32)
+            b_out[0] = (own_out[step] if step < half else came_out[step - half][...]).astype(F32)
+            for which in range(step, 4, 2 * half):
+                dense_outs[which][...] = dense_ref[which * width : (which + 1) * width, :].astype(F32)
+
+
+def finish(places, own_in, own_out, came_in, came_out, dense):
+    half, width, size = own_in.shape
 
     def whole(*shape):
-        return pl.BlockSpec(shape, lambda e, p: (0, 0))
+        return pl.BlockSpec(shape, lambda e, p: (0,) * len(shape))
 
     def spec(*shape):
         return pl.BlockSpec((1,) + shape, lambda e, p: (p[e], 0, 0))
 
     return pl.pallas_call(
-        functools.partial(finish_kernel, steps),
+        functools.partial(finish_kernel, half),
         grid_spec=pltpu.PrefetchScalarGridSpec(
             num_scalar_prefetch=1,
-            grid=(steps,),
-            in_specs=[whole(width, size)] * steps + [whole(size, width)] * steps,
-            out_specs=[spec(width, size), spec(size, width)],
+            grid=(2 * half,),
+            in_specs=[whole(half, width, size), whole(half, size, width)]
+            + [whole(width, size)] * half
+            + [whole(size, width)] * half
+            + [whole(4 * width, width)],
+            out_specs=[spec(width, size), spec(size, width)] + [whole(width, width)] * 4,
         ),
         out_shape=[
-            jax.ShapeDtypeStruct((steps, width, size), F32),
-            jax.ShapeDtypeStruct((steps, size, width), F32),
-        ],
+            jax.ShapeDtypeStruct((2 * half, width, size), F32),
+            jax.ShapeDtypeStruct((2 * half, size, width), F32),
+        ]
+        + [jax.ShapeDtypeStruct((width, width), F32)] * 4,
         compiler_params=params(),
-    )(places, *ins, *outs)
+    )(places, own_in, own_out, *came_in, *came_out, dense)
 
 
 def tail_kernel(parts, sources, experts, capacity, padded, *refs):
-    u_refs, refs = refs[:sources], refs[sources:]
-    c_refs, refs = refs[:sources], refs[sources:]
+    u_refs, refs = refs[: sources * experts], refs[sources * experts :]
+    c_own, c_far, refs = refs[0], refs[1 : 1 + (sources - 1) * experts], refs[1 + (sources - 1) * experts :]
     (
         first_ref, second_ref, dense_o, dense_qkv, small_ref,
         own_in_ref, own_out_ref, came_in_ref, came_out_ref, dense_ref, total_ref,
@@ -796,23 +1046,27 @@
     stages += [give_back(depth) for depth in reversed(range(exp_bits))]
     stages = [functools.partial(stage, side) for stage in stages for side in range(2)]
 
-    steps, turns = 2 * experts, 2 * experts * sources
+    steps, turns = 1 + experts, (1 + experts) * sources
 
     def rows_copy(source, expert):
+        if source == 0:
+            c_from = c_own.at[group * experts + expert]
+        else:
+            c_from = c_far[expert * (sources - 1) + source - 1]
         return [
             pltpu.make_async_copy(
-                u_refs[source].at[expert],
+                u_refs[expert * sources + source],
                 rows_u.at[source, expert],
                 rows_sem.at[0, source, expert],
             ),
             pltpu.make_async_copy(
-                c_refs[source].at[expert], rows_c.at[source, expert], rows_sem.at[1, source, expert]
+                c_from, rows_c.at[source, expert], rows_sem.at[1, source, expert]
             ),
         ]
 
     def weight_copy(step):
-        far = step < experts
-        expert = group * experts + step % experts
+        far = step == 0
+        expert = group * experts + jnp.where(far, experts - 1, step - 1)
         place = (pair * 2 + jnp.where(far, 1 - group, group)) * size
         place = pl.ds(pl.multiple_of(place, 128), size)
         slot = step % 2
@@ -825,18 +1079,18 @@
             ),
         ]
 
-    far_parts = far_send.shape[2]
+    far_parts = far_send.shape[1]
 
     def far_copy(index):
-        expert, kind, part = index // (2 * far_parts), index % 2, index // 2 % far_parts
+        kind, part = index % 2, index // 2
         held, target = ((far_in, came_in_ref), (far_out, came_out_ref))[kind]
-        lines = held.shape[1] // far_parts
+        lines = held.shape[0] // far_parts
         place = pl.ds(part * lines, lines)
         return pltpu.make_async_remote_copy(
-            src_ref=held.at[expert, place],
-            dst_ref=target.at[expert, place],
-            send_sem=far_send.at[expert, kind, part],
-            recv_sem=far_recv.at[expert, kind, part],
+            src_ref=held.at[place],
+            dst_ref=target.at[place],
+            send_sem=far_send.at[kind, part],
+            recv_sem=far_recv.at[kind, part],
             device_id=dp_peer(0),
             device_id_type=mesh_id,
         )
@@ -862,15 +1116,15 @@
         pl.semaphore_signal(barrier, inc=1, device_id=dp_peer(bit), device_id_type=mesh_id)
     pl.semaphore_wait(barrier, exp_bits + dp_bits)
 
-    places = [0, 0] + [2 + index + 2 * max(0, index // 2 - 2) for index in range(len(stages) - 2)]
-    places = [place for place in places if place < turns]
-    starts = {5: 2, 8: 3, 9: 4, 12: 5, 13: 6, 15: 7}
+    places = [0, 0, 1, 2, 3, 4, 5, 6]
+    places = [place for place in places if place < turns][: len(stages)]
+    starts = {7: 2, 9: 3}
     starts = {place: index for place, index in starts.items() if place < turns}
-    pieces = 2 * far_parts * experts
+    pieces = 2 * far_parts
 
     def turn(at, carry):
         step, source = at // sources, at % sources
-        expert, slot = step % experts, step % 2
+        expert, slot = jnp.where(step == 0, experts - 1, step - 1), step % 2
         for place, stage in zip(places, stages):
             pl.when(at == place)(stage)
         for place, index in starts.items():
@@ -890,8 +1144,9 @@
 
         for each_expert in range(experts):
             for each in range(sources):
-
-                @pl.when(at == each_expert * sources + each)
+                first_step = 0 if each_expert == experts - 1 else each_expert + 1
+
+                @pl.when(at == first_step * sources + each)
                 def _(each=each, each_expert=each_expert):
                     for copy in rows_copy(each, each_expert):
                         copy.wait()
@@ -911,29 +1166,30 @@
             in_sum[here, :] = jnp.where(fresh, 0.0, in_sum[here, :]) + in_term
             out_sum[here, :] = jnp.where(fresh, 0.0, out_sum[here, :]) + out_term
 
-        for each in range(experts):
-
-            @pl.when((source == sources - 1) & (step == each))
-            def _(each=each):
-                far_in[each] = in_sum[...].T.astype(BF)
-                far_out[each] = out_sum[...].astype(BF)
-                if each == 0:
-                    for index in range(2):
-                        far_copy(index).start()
-
-            @pl.when((source == sources - 1) & (step == experts + each))
-            def _(each=each):
-                own_in[each] = in_sum[...].T.astype(BF)
-                own_out[each] = out_sum[...].astype(BF)
-                for copy in own_copy(each):
+        @pl.when((source == sources - 1) & (step == 0))
+        def _():
+            far_in[...] = in_sum[...].T.astype(BF)
+            far_out[...] = out_sum[...].astype(BF)
+            for index in range(2):
+                far_copy(index).start()
+
+        for each_expert in range(experts):
+
+            @pl.when((source == sources - 1) & (step == each_expert + 1))
+            def _(each_expert=each_expert):
+                own_in[each_expert] = in_sum[...].T.astype(BF)
+                own_out[each_expert] = out_sum[...].astype(BF)
+                for copy in own_copy(each_expert):
                     copy.start()
 
         return carry
 
     lax.fori_loop(0, turns, turn, 0)
+    for stage in stages[len(places) : len(places) + 2]:
+        stage()
     for index in range(2 + len(starts), pieces):
         far_copy(index).start()
-    for stage in stages[len(places) :]:
+    for stage in stages[len(places) + 2 :]:
         stage()
     total_ref[...] = small[exp_bits + dp_bits]
     for index in range(pieces):
@@ -952,9 +1208,9 @@
         small_copy(depth).wait_send()
 
 
-def tail(us, cs, w_in, w_out, size, dense_o, dense_qkv, small, capacity, padded, exp_n):
-    sources = len(us)
-    experts, rows, width = us[0].shape
+def tail(us, c_rows, c_far, w_in, w_out, size, dense_o, dense_qkv, small, capacity, padded, exp_n):
+    sources, experts = len(us[0]), len(us)
+    rows, width = us[0][0].shape
     far_parts = 4
     exp_bits, dp_bits = exp_n.bit_length() - 1, sources.bit_length() - 1
     lines = 4 * width
@@ -962,13 +1218,13 @@
     dma = pltpu.SemaphoreType.DMA
     return pl.pallas_call(
         functools.partial(tail_kernel, 3, sources, experts, capacity, padded),
-        in_specs=[anywhere] * (2 * sources + 5),
+        in_specs=[anywhere] * (experts * (2 * sources - 1) + 6),
         out_specs=[anywhere] * 5 + [pl.BlockSpec(memory_space=pltpu.VMEM)],
         out_shape=[
             jax.ShapeDtypeStruct((experts, width, size), BF),
             jax.ShapeDtypeStruct((experts, size, width), BF),
-            jax.ShapeDtypeStruct((experts, width, size), BF),
-            jax.ShapeDtypeStruct((experts, size, width), BF),
+            jax.ShapeDtypeStruct((width, size), BF),
+            jax.ShapeDtypeStruct((size, width), BF),
             jax.ShapeDtypeStruct((lines, width), BF),
             jax.ShapeDtypeStruct(small.shape, F32),
         ],
@@ -980,8 +1236,8 @@
             pltpu.VMEM((size, width), BF),
             pltpu.VMEM((size, width), F32),
             pltpu.VMEM((size, width), F32),
-            pltpu.VMEM((experts, width, size), BF),
-            pltpu.VMEM((experts, size, width), BF),
+            pltpu.VMEM((width, size), BF),
+            pltpu.VMEM((size, width), BF),
             pltpu.VMEM((experts, width, size), BF),
             pltpu.VMEM((experts, size, width), BF),
             pltpu.VMEM((lines, width), BF),
@@ -992,8 +1248,8 @@
             dma((2, sources, experts)),
             dma((2, 2)),
             dma((3,)),
-            dma((experts, 2, far_parts)),
-            dma((experts, 2, far_parts)),
+            dma((2, far_parts)),
+            dma((2, far_parts)),
             dma((2, experts)),
             dma((2, 2, exp_bits)),
             dma((2, 2, exp_bits)),
@@ -1008,20 +1264,48 @@
         compiler_params=pltpu.CompilerParams(
             vmem_limit_bytes=58 * 2**20, collective_id=2, has_side_effects=True
         ),
-        cost_estimate=pl.CostEstimate(flops=0, bytes_accessed=2**16, transcendentals=0),
-    )(*us, *cs, w_in, w_out, dense_o, dense_qkv, small)
+        cost_estimate=NO_COST,
+    )(*sum(us, []), c_rows, *sum(c_far, []), w_in, w_out, dense_o, dense_qkv, small)
 
 
 def combine_kernel(
-    slot_ref, expert_ref, gate_ref, probs_ref, h_ref, c_ref, o_ref, e_ref, d_ref, wo_ref, wr_ref, gain_ref,
-    mixed_ref, dh_ref, do_ref, wo_ref_out, wr_sum, gain_sum, wo_sum,
+    parts, experts, slot_ref, expert_ref, gate_ref, probs_ref, h_ref, c_ref, o_ref,
+    e_first, e_rest, d_first, d_rest, wo_ref, wr_ref, gain_ref, *refs
 ):
+    sent_refs, refs = refs[:parts], refs[parts:]
+    mixed_ref, dh_ref, do_ref, wo_ref_out, wr_sum, gain_sum = refs[:6]
+    came_refs, refs = refs[6 : 6 + parts * experts], refs[6 + parts * experts :]
+    wo_sum, *sems = refs
     step = pl.program_id(0)
-    tokens, slots = slot_ref.shape[0], e_ref.shape[0]
+    me, blocks = lax.axis_index("exp"), sent_refs[0].shape[0]
+
+    def transfers():
+        copies = []
+        for expert in range(experts):
+            for part in range(parts):
+                index = expert * parts + part
+                copies += spread(me, sent_refs[part], expert, came_refs[index], sems, index)
+        return copies
+
+    @pl.when(step == 0)
+    def _():
+        greet(me, blocks)
+        for copy in transfers():
+            copy.start()
+
+    @pl.when(step == pl.num_programs(0) - 1)
+    def _():
+        for copy in transfers():
+            copy.wait()
+
+    tokens, early = slot_ref.shape[1], e_first.shape[0]
+    slots = early + e_rest.shape[0]
+    slot = as_column(slot_ref[...].astype(F32)).astype(jnp.int32)
     picks = jnp.where(
-        slot_ref[...] == lax.broadcasted_iota(jnp.int32, (tokens, slots), 1), 1.0, 0.0
+        slot == lax.broadcasted_iota(jnp.int32, (tokens, slots), 1), 1.0, 0.0
     ).astype(BF)
-    returned, arrived = mm(picks, e_ref[...]), mm(picks, d_ref[...])
+    returned = mm(picks[:, :early], e_first[...]) + mm(picks[:, early:], e_rest[...])
+    arrived = mm(picks[:, :early], d_first[...]) + mm(picks[:, early:], d_rest[...])
     gate, probs, mixed = gate_ref[...], probs_ref[...], h_ref[...]
     upstream = c_ref[...].astype(F32)
     mixed_ref[...] = (mixed + gate * returned).astype(BF)
@@ -1031,16 +1315,10 @@
     inv = lax.rsqrt(jnp.mean(mixed * mixed, axis=-1, keepdims=True) + EPSILON)
     unit = mixed * inv
     gain = gain_ref[...]
-    normed_grad = (
-        lax.dot_general(
-            logit_grad,
-            wr_ref[...],
-            (((1,), (1,)), ((), ())),
-            precision=FULL_PRECISION,
-            preferred_element_type=F32,
-        )
-        + gate * arrived
-    )
+    lg_high, lg_low = halves(logit_grad)
+    wr_high, wr_low = halves(wr_ref[...])
+    through_router = mm_nt(lg_high, wr_high) + (mm_nt(lg_low, wr_high) + mm_nt(lg_high, wr_low))
+    normed_grad = through_router + gate * arrived
     unit_grad = normed_grad * gain
     mixed_grad = upstream + inv * (
         unit_grad - unit * jnp.mean(unit_grad * unit, axis=-1, keepdims=True)
@@ -1056,9 +1334,9 @@
         gain_sum[...] = jnp.zeros_like(gain_sum)
 
     wo_sum[...] += mm(o_ref[...].T, low)
-    wr_sum[...] += jnp.dot(
-        logit_grad.T, unit * gain, precision=FULL_PRECISION, preferred_element_type=F32
-    )
+    n_high, n_low = halves(unit * gain)
+    lg_high, lg_low = lg_high.T, lg_low.T
+    wr_sum[...] += mm(lg_high, n_high) + (mm(lg_low, n_high) + mm(lg_high, n_low))
     gain_sum[...] += jnp.sum(normed_grad * unit, axis=0, keepdims=True)
 
     @pl.when(step == pl.num_programs(0) - 1)
@@ -1066,9 +1344,13 @@
         wo_ref_out[...] = wo_sum[...].astype(BF)
 
 
-def combine(slot, expert, gate, probs, h, c, o, e_out, du, wo, wr, gain):
+def combine(slot, expert, gate, probs, h, c, o, e_out, du, wo, wr, gain, sent):
+    parts, (blocks, local, padded, _) = len(sent), sent[0].shape
+    spreads = parts * (local - 1)
+    anywhere = pl.BlockSpec(memory_space=pl.ANY)
     tokens, width = h.shape
-    slots, experts = e_out.shape[0], wr.shape[1]
+    early, rest = (part.shape[0] for part in e_out)
+    slots, experts = early + rest, wr.shape[1]
     size = 256
 
     def rows(columns):
@@ -1078,13 +1360,16 @@
         return pl.BlockSpec(shape, lambda t: (0, 0))
 
     return pl.pallas_call(
-        combine_kernel,
+        functools.partial(combine_kernel, parts, local - 1),
         grid=(tokens // size,),
-        in_specs=[rows(1), rows(1), rows(1), rows(experts), rows(width), rows(width), rows(width)]
-        + [whole(slots, width), whole(slots, width), whole(width, width), whole(width, experts)]
-        + [whole(1, width)],
+        in_specs=[pl.BlockSpec((1, size), lambda t: (0, t)), rows(1), rows(1), rows(experts), rows(width), rows(width), rows(width)]
+        + [whole(early, width), whole(rest, width)] * 2
+        + [whole(width, width), whole(width, experts)]
+        + [whole(1, width)]
+        + [anywhere] * parts,
         out_specs=[rows(width), rows(width), rows(width), whole(width, width), whole(experts, width)]
-        + [whole(1, width)],
+        + [whole(1, width)]
+        + [anywhere] * spreads,
         out_shape=[
             jax.ShapeDtypeStruct((tokens, width), BF),
             jax.ShapeDtypeStruct((tokens, width), F32),
@@ -1092,15 +1377,12 @@
             jax.ShapeDtypeStruct((width, width), BF),
             jax.ShapeDtypeStruct((experts, width), F32),
             jax.ShapeDtypeStruct((1, width), F32),
-        ],
-        scratch_shapes=[pltpu.VMEM((width, width), F32)],
-        compiler_params=params(),
-        cost_estimate=pl.CostEstimate(
-            flops=4 * tokens * width * (slots + width),
-            bytes_accessed=16 * tokens * width + 4 * slots * width,
-            transcendentals=0,
-        ),
-    )(slot, expert, gate, probs, h, c, o, e_out, du, wo, wr, gain)
+        ]
+        + [jax.ShapeDtypeStruct((blocks, padded, width), BF)] * spreads,
+        scratch_shapes=[pltpu.VMEM((width, width), F32)] + spread_sems(spreads, blocks),
+        compiler_params=params(collective_id=5, has_side_effects=True),
+        cost_estimate=NO_COST,
+    )(slot, expert, gate, probs, h, c, o, *e_out, *du, wo, wr, gain, *sent)
 
 
 def last_kernel(
@@ -1160,9 +1442,7 @@
         ],
         scratch_shapes=[pltpu.VMEM((width, width), F32)] * 3,
         compiler_params=params(),
-        cost_estimate=pl.CostEstimate(
-            flops=12 * tokens * width * width, bytes_accessed=16 * tokens * width, transcendentals=0
-        ),
+        cost_estimate=NO_COST,
     )(x, dh, dq, dk, dv, wq, wk, wv, gain)
 
 
@@ -1198,7 +1478,11 @@
     rank = jnp.sum(ahead.astype(jnp.int32), axis=1)
     place = ((chosen // local) ^ exp_me) * block + (chosen % local) * padded + rank
     slots = jnp.where(rank < capacity, place, -1)
-    slot_row, slot_column = slots[None, :], slots[:, None]
+    chunk, inside = slots // block, slots % block
+    later = exp_n * padded + chunk * (block - padded) + inside - padded
+    returned_slots = jnp.where(inside < padded, chunk * padded + inside, later)
+    returned_slots = jnp.where(slots < 0, -1, returned_slots)
+    slot_row, returned_row = slots[None, :], returned_slots[None, :]
 
     half = local // 2
     group = dp_me % 2
@@ -1209,12 +1493,6 @@
             pairs = [(i, i ^ step) for i in range(dp_n)]
             pieces.append(lax.ppermute(other if step % 2 else mine, "dp", pairs))
         return pieces
-
-    def groups(rows, start, count):
-        return (
-            lax.dynamic_slice_in_dim(rows, group * half + start, count, 0),
-            lax.dynamic_slice_in_dim(rows, (1 - group) * half + start, count, 0),
-        )
 
     lines = jnp.dot(
         relative_bias_table.T, diagonal_onehot(buckets).T, precision=FULL_PRECISION
@@ -1223,9 +1501,12 @@
     gain_attn, gain_ffn = norm_attn[None, :], norm_ffn[None, :]
     q, k, v = qkv(tokens, gain_attn, w_query, w_key, w_value)
     c_sent = dispatch(slot_row, cotangent, exp_n, block).reshape(exp_n, local, padded, width)
+    c_far = over_dp(
+        lax.dynamic_slice_in_dim(c_sent, group * half, half, 1),
+        lax.dynamic_slice_in_dim(c_sent, (1 - group) * half, half, 1),
+    )[1:]
     context, lse, c_rows = attention(lines, c_sent, q, k, v)
     c_rows = c_rows.reshape(local, exp_n * padded, width)
-    c_all = over_dp(*groups(c_rows, 0, half))
     mixed, u, probs, gate, gate_row = router(
         context, tokens, w_output, gain_ffn, w_router, expert_index
     )
@@ -1233,16 +1514,35 @@
     u_rows, e_back, d_back = expert_pass(
         sent.reshape(exp_n, local, padded, width), c_rows, w_in, w_out
     )
-    e_back, *c_all = lax.optimization_barrier((e_back, *c_all))
-    e_back, d_back = e_back.reshape(exp_n * block, width), d_back.reshape(exp_n * block, width)
-    u_rows = u_rows.reshape(local, exp_n * padded, width)
-    u_all = over_dp(*groups(u_rows, 0, half))
-    mixed_out, mixed_grad, context_grad, output_part, router_part, norm_ffn_part = combine(
-        slot_column, expert_index, gate, probs, mixed, cotangent, context,
-        e_back, d_back, w_output, w_router, gain_ffn,
+    mine, other = u_rows[:half], u_rows[half:]
+    mine[0], *c_far = lax.optimization_barrier((mine[0], *c_far))
+    u_all = [over_dp(mine[0], other[0])]
+    for expert in range(1, half):
+        late, *u_all[-1], mine[expert], other[expert] = lax.optimization_barrier(
+            (e_back[1], *u_all[-1], mine[expert], other[expert])
+        )
+        e_back = (e_back[0], late)
+        u_all.append(over_dp(mine[expert], other[expert]))
+    e_back, d_back = ([part.reshape(-1, width) for part in parts] for parts in (e_back, d_back))
+    mixed_out, mixed_grad, context_grad, output_part, router_part, norm_ffn_part, *c_early = combine(
+        returned_row, expert_index, gate, probs, mixed, cotangent, context,
+        e_back, d_back, w_output, w_router, gain_ffn, c_far,
     )
-    query_grad, key_grad, value_grad, sums = attention_back(lines, q, k, v, context_grad, lse)
     size = w_in.shape[2] // dp_n
+    rows = exp_n * padded
+    c_early = [part.reshape(rows, width) for part in c_early]
+    c_spread = [c_early[at : at + dp_n - 1] for at in range(0, len(c_early), dp_n - 1)]
+    swapped = []
+    for expert in range(half - 1):
+        where = jnp.stack([group * half + expert, dp_me // 2 * 2 + 1 - group]).astype(jnp.int32)
+        swapped += weight_grads(
+            where, u_all[expert], c_rows, c_spread[expert], w_in, w_out, size, capacity, padded
+        )
+    query_grad, key_grad, value_grad, sums, *moved = attention_back(
+        lines, q, k, v, context_grad, lse, c_far, swapped
+    )
+    c_late, got = moved[: dp_n - 1], moved[dp_n - 1 :]
+    c_spread.append([part.reshape(rows, width) for part in c_late])
     table_part = jnp.dot(
         diagonal_onehot(buckets).T,
         sums[:, :4].reshape(HEADS, 4 * TILE).T,
@@ -1256,22 +1556,21 @@
     small = jnp.concatenate([router_part, norm_attn_part, norm_ffn_part, table_line], axis=0)
     small = jnp.pad(small, ((0, -small.shape[0] % 8), (0, 0)))
     own_in, own_out, came_in, came_out, dense, total = tail(
-        u_all, c_all, w_in, w_out, size, output_part, qkv_part, small, capacity, padded, exp_n
+        u_all, c_rows, c_spread, w_in, w_out, size, output_part, qkv_part, small, capacity, padded, exp_n
     )
     experts = jnp.arange(local, dtype=jnp.int32)
-    grad_in, grad_out = finish(
+    grad_in, grad_out, *dense_grads = finish(
         jnp.where(group == 0, experts, (experts + half) % local),
-        list(own_in) + list(came_in),
-        list(own_out) + list(came_out),
+        own_in,
+        own_out,
+        got[0::2] + [came_in],
+        got[1::2] + [came_out],
+        dense,
     )
-    dense = dense.reshape(4, width, width).astype(F32)
     return (
         mixed_out,
         grad_tokens,
-        dense[0],
-        dense[1],
-        dense[2],
-        dense[3],
+        *dense_grads,
         total[all_experts],
         total[all_experts + 1],
         total[all_experts + 2, : table_part.size].reshape(table_part.shape),

time: 535 us -> 518 us (0.968); the launches traced: 535 us -> 509 us
  waiting for transfers between devices: 26.8 us -> 8.34 us
  local copies, waits for them, and re-layouts: 34.5 us -> 19.4 us
    pallas_call x1, Pallas kernels: 156 us -> 109 us  [tail(): pl.pallas_call(functools.partial(tail_kernel, 3, sources, experts, capaci...]
    pallas_call x4 -> x6, Pallas kernels: 202 us -> 249 us  [the longest x1 59.8 us: attention_back(): pl.pallas_call(functools.partial(attention_back_kernel, parts, swaps), gr...]
    ppermute x6 -> x9, waiting for transfers between devices: 26.8 us -> 8.34 us  [over_dp(): pieces.append(lax.ppermute(other if step % 2 else mine, 'dp', pairs))]
    another operation x4 -> x0, local copies, waits for them, and re-layouts: 6.24 us -> none  [the longest x1 3.3 us: per_device(): list(came_out)]
    ppermute x6 -> x9, starting transfers between devices: 8.53 us -> 13.6 us  [over_dp(): pieces.append(lax.ppermute(other if step % 2 else mine, 'dp', pairs))]
    unnamed x51 -> x40, local copies, waits for them, and re-layouts: 11.5 us -> 8.29 us
  transfers between devices with their start and end apart: 6 -> 9, of which waited for: 1 -> 1; matrix products, arithmetic and copies ran while one was open for 1% -> 2% of each run, Pallas kernels for 44% -> 64%
where the time goes in v4:
time: 518 us; the launch traced here: 509 us
  Pallas kernels  459 us (89%)
  local copies, waits for them, and re-layouts  19.4 us (4%)
  starting transfers between devices  13.6 us (3%)
  waiting for transfers between devices  8.34 us (2%)
  other arithmetic  6.7 us (1%)
    pallas_call x1, Pallas kernels, tail(): pl.pallas_call(functools.partial(tail_kernel, 3, sources, experts, capaci...  109 us
    pallas_call x1, Pallas kernels, attention_back(): pl.pallas_call(functools.partial(attention_back_kernel, parts, swaps), gr...  59.8 us
    pallas_call x1, Pallas kernels, expert_pass(): pl.pallas_call(functools.partial(expert_kernel, 3), grid=(experts - 1, hi...  58.7 us
    pallas_call x1, Pallas kernels, expert_pass(): pl.pallas_call(functools.partial(expert_rest_kernel, 3, kept), grid=(hidd...  57.5 us
    pallas_call x1, Pallas kernels, attention(): pl.pallas_call(attention_kernel, grid=(pairs, seqs), in_specs=[pl.BlockSp...  40.6 us
    pallas_call x1, Pallas kernels, combine(): pl.pallas_call(functools.partial(combine_kernel, parts, local - 1), grid=...  39.6 us
    pallas_call x1, Pallas kernels, last(): pl.pallas_call(last_kernel, grid=(tokens // size,), in_specs=[rows] * 5 +...  20.2 us
    pallas_call x1, Pallas kernels, weight_grads(): pl.pallas_call(functools.partial(weights_kernel, 3, sources, capacity, pa...  17.7 us
  transfers between devices with their start and end apart: 9, of which 1 were waited for; matrix products, arithmetic and copies ran while one was open for 2% of the time, Pallas kernels for 64%

profile of v4, /device:TPU:0, one launch (start us, length us, event | category | flops | bytes accessed | tf_op | source)
XLA Modules:
  0.0 508.8 jit_solution(5908091598769606932)
XLA Ops:
  2.1 2.0 convert_reduce_fusion
  4.1 1.4 fusion.8
  5.5 8.8 %shard_map.229 = bf16[2048,768]{1,0:T(8,128)(2,1)} custom-call(s32[1,1536]{1,0:T(1,128)} %get-tuple-element.187.slot_ref, bf16[1536,768]{1,0:T(8,128)(2,1)} %c_ref.1), custom_call_target="tpu_custom_call" | custom-call | bytes 65536 | tf_op jit(solution)/shard_map/pallas_call | solution.py:147
  14.3 3.9 constant_dynamic-slice_fusion
  18.2 4.0 collective-permute-start.1
  22.3 1.4 collective-permute-start.2
  28.2 9.5 %shard_map.230 = (bf16[1536,768]{1,0:T(8,128)(2,1)}, bf16[1536,768]{1,0:T(8,128)(2,1)}, bf16[1536,768]{1,0:T(8,128)(2,1)}) custom-call(bf16[1536,768]{1,0:T(8,128)(2,1)} %x_ref.5, f32[1,768]{1,0:T(1,128)} %broadcast_in_dim.14.gain_ref, bf16[768,768]{1,0:T(8,128)(2,1)} %wq_ref.3, bf16[768,768]{1,0:T(8,128)(2,1)} %wk_ref.3, bf16[768,768]{1,0:T(8,128)(2,1)} %wv_ref.3), custom_call_target="tpu_custom_call" | custom-call | bytes 65536 | tf_op jit(solution)/shard_map/pallas_call | solution.py:174
  37.7 40.6 %shard_map.231 = (bf16[1536,768]{1,0:T(8,128)(2,1)}, f32[6,3,2,512]{3,2,1,0:T(2,128)}, bf16[4,8,64,768]{3,2,1,0:T(8,128)(2,1)}) custom-call(f32[12,8,128]{2,1,0:T(8,128)} %concatenate.24.lines_ref, bf16[8,4,64,768]{3,2,1,0:T(8,128)(2,1)} %bitcast.44, bf16[1536,768]{1,0:T(8,128)(2,1)} %get-tuple-element.80.q_ref, bf16[1536,768]{1,0:T(8,128)(2,1)} %get-tuple-element.81.k_ref, ...), custom_call_target="tpu_custom_call" | custom-call | bytes 65536 | tf_op jit(solution)/shard_map/pallas_call | solution.py:296
  78.3 11.2 %shard_map.232 = (f32[1536,768]{1,0:T(8,128)}, bf16[1536,768]{1,0:T(8,128)(2,1)}, f32[1536,32]{1,0:T(8,128)}, f32[1536,1]{1,0:T(8,128)}, f32[1,1536]{1,0:T(1,128)}) custom-call(bf16[1536,768]{1,0:T(8,128)(2,1)} %get-tuple-element.83.o_ref, bf16[1536,768]{1,0:T(8,128)(2,1)} %x_ref.5, bf16[768,768]{1,0:T(8,128)(2,1)} %wo_ref.3, ...), custom_call_target="tpu_custom_call" | custom-call | bytes 65536 | tf_op jit(solution)/shard_map/pallas_call | solution.py:497
  89.5 10.9 %shard_map.233 = bf16[2048,768]{1,0:T(8,128)(2,1)} custom-call(s32[1,1536]{1,0:T(1,128)} %get-tuple-element.187.slot_ref, f32[1,1536]{1,0:T(1,128)} %get-tuple-element.87.gate_ref, bf16[1536,768]{1,0:T(8,128)(2,1)} %get-tuple-element.88.rows_ref), custom_call_target="tpu_custom_call" | custom-call | bytes 65536 | tf_op jit(solution)/shard_map/pallas_call | solution.py:151
  100.4 58.7 %shard_map.234 = (bf16[8,64,768]{2,1,0:T(8,128)(2,1)}, bf16[8,64,768]{2,1,0:T(8,128)(2,1)}, bf16[8,64,768]{2,1,0:T(8,128)(2,1)}, bf16[8,64,768]{2,1,0:T(8,128)(2...) custom-call(bf16[8,4,64,768]{3,2,1,0:T(8,128)(2,1)} %bitcast.49, ...), custom_call_target="tpu_custom_call" | custom-call | bytes 65536 | tf_op jit(solution)/shard_map/pallas_call | solution.py:705
  159.1 3.0 collective-permute-start.5
  163.7 57.5 %shard_map.235 = (bf16[8,3,64,768]{3,2,1,0:T(8,128)(2,1)}, bf16[8,3,64,768]{3,2,1,0:T(8,128)(2,1)}) custom-call(bf16[512,768]{1,0:T(8,128)(2,1)} %bitcast.74, bf16[4,512,768]{2,1,0:T(8,128)(2,1)} %bitcast.46, bf16[4,768,3072]{2,1,0:T(8,128)(2,1)} %refs_15_.1, bf16[4,3072,768]{2,1,0:T(8,128)(2,1)} %refs_16_.1, ...), custom_call_target="tpu_custom_call" | custom-call | flops 38654705664 | bytes 9437184 | tf_op jit(solution)/shard_map/pallas_call | solution.py:740
  223.1 8.3 %collective-permute-done.4.refs_2_ = bf16[512,768]{1,0:T(8,128)(2,1)S(1)} collective-permute-done((bf16[512,768]{1,0:T(8,128)(2,1)}, bf16[512,768]{1,0:T(8,128)(2,1)S(1)}, u32[]{:S(2)}, u32[]{:S(2)}) %collective-permute-start.4) | collective-permute-done | bytes 786464 | tf_op jit(solution)/shard_map/ppermute | solution.py:1494
  232.3 2.5 collective-permute-start.8
  236.9 39.6 %shard_map.236 = (bf16[1536,768]{1,0:T(8,128)(2,1)}, f32[1536,768]{1,0:T(8,128)}, bf16[1536,768]{1,0:T(8,128)(2,1)}, bf16[768,768]{1,0:T(8,128)(2,1)}, f32[32,76...) custom-call(s32[1,1536]{1,0:T(1,128)} %get-tuple-element.186.slot_re, ...), custom_call_target="tpu_custom_call" | custom-call | bytes 65536 | tf_op jit(solution)/shard_map/pallas_call | solution.py:1362
  276.5 17.7 %shard_map.237 = (bf16[768,768]{1,0:T(8,128)(2,1)}, bf16[768,768]{1,0:T(8,128)(2,1)}) custom-call(s32[2]{0:T(128)} %pad_add_fusion.1.place_ref, bf16[512,768]{1,0:T(8,128)(2,1)} %bitcast.51, bf16[512,768]{1,0:T(8,128)(2,1)} %copy-done.5, bf16[512,768]{1,0:T(8,128)(2,1)} %copy-done.6, bf16[512,768]{1,0:T(8,128)(2,1)} %copy-done.4, ...), custom_call_target="tpu_custom_call" | custom-call | bytes 65536 | tf_op jit(solution)/shard_map/pallas_call | solution.py:803
  294.2 59.8 %shard_map.238 = (bf16[1536,768]{1,0:T(8,128)(2,1)}, bf16[1536,768]{1,0:T(8,128)(2,1)}, bf16[1536,768]{1,0:T(8,128)(2,1)}, f32[12,8,128]{2,1,0:T(8,128)}, bf16[8...) custom-call(f32[12,8,128]{2,1,0:T(8,128)} %concatenate.24.lines_ref,, ...), custom_call_target="tpu_custom_call" | custom-call | bytes 65536 | tf_op jit(solution)/shard_map/pallas_call | solution.py:439
  355.3 20.2 %shard_map.239 = (f32[1536,768]{1,0:T(8,128)}, bf16[2304,768]{1,0:T(8,128)(2,1)}, f32[1,768]{1,0:T(1,128)}) custom-call(bf16[1536,768]{1,0:T(8,128)(2,1)} %x_ref.5, f32[1536,768]{1,0:T(8,128)} %get-tuple-element.107.dh_ref, bf16[1536,768]{1,0:T(8,128)(2,1)} %get-tuple-element.119.dq_ref, bf16[1536,768]{1,0:T(8,128)(2,1)} %get-tuple-element.120.dk_ref, ...), custom_call_target="tpu_custom_call" | custom-call | bytes 65536 | tf_op jit(solution)/shard_map/pallas_call | solution.py:1433
  378.3 108.5 %shard_map.240 = (bf16[2,768,768]{2,1,0:T(8,128)(2,1)}, bf16[2,768,768]{2,1,0:T(8,128)(2,1)}, bf16[768,768]{1,0:T(8,128)(2,1)}, bf16[768,768]{1,0:T(8,128)(2,1)}...) custom-call(bf16[512,768]{1,0:T(8,128)(2,1)} %bitcast.52, bf16[512,768]{1,0:T(8,128)(2,1)} %copy-done.5, ...), custom_call_target="tpu_custom_call" | custom-call | bytes 65536 | tf_op jit(solution)/shard_map/pallas_call | solution.py:1219
  487.6 1.4 slice_reduce_fusion
  489.0 1.5 slice_bitcast_fusion
  491.3 15.8 %shard_map.241 = (f32[4,768,768]{2,1,0:T(8,128)}, f32[4,768,768]{2,1,0:T(8,128)}, f32[768,768]{1,0:T(8,128)}, f32[768,768]{1,0:T(8,128)}, f32[768,768]{1,0:T(8,128)}, /*index=5*/f32[768,768]{1,0:T(8,128)}) custom-call(s32[4]{0:T(128)} %broadcast_select_fusion.place_ref, bf16[2,768,768]{2,1,0:T(8,128)(2,1)} %get-tuple-element.134.refs_0_, ...), custom_call_target="tpu_custom_call" | custom-call | tf_op jit(solution)/shard_map/pallas_call | solution.py:854
  507.1 1.4 copy.47
  (72 shorter events, 17.8 us)
Async XLA Ops:
  0.6 25.6 %copy-start = (f32[32,12]{0,1:T(8,128)S(1)}, f32[32,12]{0,1:T(8,128)}, u32[]{:S(2)}) copy-start(f32[32,12]{0,1:T(8,128)} %param.21) | copy-start | bytes 4612
  14.3 9.6 %copy-start.13 = (s32[1536,1]{0,1:T(1,128)S(1)}, s32[1536,1]{0,1:T(1,128)}, u32[]{:S(2)}) copy-start(s32[1536,1]{0,1:T(1,128)} %param.25) | copy-start | bytes 18436
  14.3 10.8 %copy-start.14 = (f32[768]{0:T(1024)S(1)}, f32[768]{0:T(1024)}, u32[]{:S(2)}) copy-start(f32[768]{0:T(1024)} %param.19) | copy-start | bytes 9220
  14.3 11.3 %copy-start.15 = (f32[768]{0:T(1024)S(1)}, f32[768]{0:T(1024)}, u32[]{:S(2)}) copy-start(f32[768]{0:T(1024)} %param.20) | copy-start | bytes 9220
  14.3 12.3 %copy-start.12 = (f32[768,32]{0,1:T(8,128)S(1)}, f32[768,32]{0,1:T(8,128)}, u32[]{:S(2)}) copy-start(f32[768,32]{0,1:T(8,128)} %param.22) | copy-start | bytes 294916
  18.2 144.4 %collective-permute-start.1 = (bf16[8,2,64,768]{3,2,1,0:T(8,128)(2,1)}, bf16[8,2,64,768]{3,2,1,0:T(8,128)(2,1)S(1)}, u32[]{:S(2)}, u32[]{:S(2)}) collective-permute-start(bf16[8,2,64,768]{3,2,1,0:T(8,128)(2,1)} %get-tuple-element.188), channel_id=1, source_target_pairs={{0,2},{1,3},{2,0},{3,1},{4,6},{5,7},{6,4},{7,5},{8,10},{9,11},{10,... | collective-permute-start | bytes 4718600 | tf_op jit(solution)/shard_map/ppermute | solution.py:1494
  22.3 140.3 %collective-permute-start.2 = (bf16[8,2,64,768]{3,2,1,0:T(8,128)(2,1)}, bf16[8,2,64,768]{3,2,1,0:T(8,128)(2,1)S(1)}, u32[]{:S(2)}, u32[]{:S(2)}) collective-permute-start(bf16[8,2,64,768]{3,2,1,0:T(8,128)(2,1)} %get-tuple-element.189), channel_id=1, source_target_pairs={{0,3},{1,2},{2,1},{3,0},{4,7},{5,6},{6,5},{7,4},{8,11},{9,10},{10,... | collective-permute-start | bytes 4718600 | tf_op jit(solution)/shard_map/ppermute | solution.py:1494
  23.6 139.0 %collective-permute-start = (bf16[8,2,64,768]{3,2,1,0:T(8,128)(2,1)}, bf16[8,2,64,768]{3,2,1,0:T(8,128)(2,1)}, u32[]{:S(2)}, u32[]{:S(2)}) collective-permute-start(bf16[8,2,64,768]{3,2,1,0:T(8,128)(2,1)} %get-tuple-element.189), channel_id=1, source_target_pairs={{0,1},{1,0},{2,3},{3,2},{4,5},{5,4},{6,7},{7,6},{8,9},{9,8},{10,11... | collective-permute-start | bytes 4718600 | tf_op jit(solution)/shard_map/ppermute | solution.py:1494
  159.1 62.1 %collective-permute-start.5 = (bf16[512,768]{1,0:T(8,128)(2,1)}, bf16[512,768]{1,0:T(8,128)(2,1)S(1)}, u32[]{:S(2)}, u32[]{:S(2)}) collective-permute-start(bf16[512,768]{1,0:T(8,128)(2,1)} %bitcast.72), channel_id=1, source_target_pairs={{0,3},{1,2},{2,1},{3,0},{4,7},{5,6},{6,5},{7,4},{8,11},{9,10},{10,... | collective-permute-start | bytes 2359304 | tf_op jit(solution)/shard_map/ppermute | solution.py:1494
  162.1 60.0 %collective-permute-start.3 = (bf16[512,768]{1,0:T(8,128)(2,1)}, bf16[512,768]{1,0:T(8,128)(2,1)S(1)}, u32[]{:S(2)}, u32[]{:S(2)}) collective-permute-start(bf16[512,768]{1,0:T(8,128)(2,1)} %bitcast.73), channel_id=1, source_target_pairs={{0,1},{1,0},{2,3},{3,2},{4,5},{5,4},{6,7},{7,6},{8,9},{9,8},{10,11... | collective-permute-start | bytes 2359304 | tf_op jit(solution)/shard_map/ppermute | solution.py:1494
  162.6 58.7 %copy-start.2 = (bf16[8,2,64,768]{3,2,1,0:T(8,128)(2,1)}, bf16[8,2,64,768]{3,2,1,0:T(8,128)(2,1)S(1)}, u32[]{:S(2)}) copy-start(bf16[8,2,64,768]{3,2,1,0:T(8,128)(2,1)S(1)} %collective-permute-done.1.refs_1_) | copy-start | bytes 4718596
  162.6 58.7 %copy-start.3 = (bf16[8,2,64,768]{3,2,1,0:T(8,128)(2,1)}, bf16[8,2,64,768]{3,2,1,0:T(8,128)(2,1)S(1)}, u32[]{:S(2)}) copy-start(bf16[8,2,64,768]{3,2,1,0:T(8,128)(2,1)S(1)} %collective-permute-done.2.refs_2_) | copy-start | bytes 4718596
  162.6 68.8 %collective-permute-start.4 = (bf16[512,768]{1,0:T(8,128)(2,1)}, bf16[512,768]{1,0:T(8,128)(2,1)S(1)}, u32[]{:S(2)}, u32[]{:S(2)}) collective-permute-start(bf16[512,768]{1,0:T(8,128)(2,1)} %bitcast.50), channel_id=1, source_target_pairs={{0,2},{1,3},{2,0},{3,1},{4,6},{5,7},{6,4},{7,5},{8,10},{9,11},{10,... | collective-permute-start | bytes 2359304 | tf_op jit(solution)/shard_map/ppermute | solution.py:1494
  221.3 0.9 copy-start.4
  231.4 0.9 copy-start.6
  232.3 144.7 %collective-permute-start.7 = (bf16[512,768]{1,0:T(8,128)(2,1)}, bf16[512,768]{1,0:T(8,128)(2,1)S(1)}, u32[]{:S(2)}, u32[]{:S(2)}) collective-permute-start(bf16[512,768]{1,0:T(8,128)(2,1)} %bitcast.63), channel_id=1, source_target_pairs={{0,2},{1,3},{2,0},{3,1},{4,6},{5,7},{6,4},{7,5},{8,10},{9,11},{10,... | collective-permute-start | bytes 2359304 | tf_op jit(solution)/shard_map/ppermute | solution.py:1494
  232.3 144.7 %collective-permute-start.8 = (bf16[512,768]{1,0:T(8,128)(2,1)}, bf16[512,768]{1,0:T(8,128)(2,1)S(1)}, u32[]{:S(2)}, u32[]{:S(2)}) collective-permute-start(bf16[512,768]{1,0:T(8,128)(2,1)} %bitcast.70), channel_id=1, source_target_pairs={{0,3},{1,2},{2,1},{3,0},{4,7},{5,6},{6,5},{7,4},{8,11},{9,10},{10,... | collective-permute-start | bytes 2359304 | tf_op jit(solution)/shard_map/ppermute | solution.py:1494
  234.8 142.2 %collective-permute-start.6 = (bf16[512,768]{1,0:T(8,128)(2,1)}, bf16[512,768]{1,0:T(8,128)(2,1)S(1)}, u32[]{:S(2)}, u32[]{:S(2)}) collective-permute-start(bf16[512,768]{1,0:T(8,128)(2,1)} %bitcast.71), channel_id=1, source_target_pairs={{0,1},{1,0},{2,3},{3,2},{4,5},{5,4},{6,7},{7,6},{8,9},{9,8},{10,11... | collective-permute-start | bytes 2359304 | tf_op jit(solution)/shard_map/ppermute | solution.py:1494
  355.3 20.2 %copy-start.11 = (f32[32,768]{1,0:T(8,128)S(1)}, f32[32,768]{1,0:T(8,128)}, u32[]{:S(2)}) copy-start(f32[32,768]{1,0:T(8,128)} %get-tuple-element.130) | copy-start | bytes 294916
  355.3 20.2 %copy-start.16 = (f32[1,768]{1,0:T(1,128)S(1)}, f32[1,768]{1,0:T(1,128)}, u32[]{:S(2)}) copy-start(f32[1,768]{1,0:T(1,128)} %get-tuple-element.132) | copy-start | bytes 9220
  376.9 1.1 copy-start.9
  376.9 1.4 copy-start.10
  491.3 15.8 %copy-start.7 = (bf16[1536,768]{1,0:T(8,128)(2,1)S(1)}, bf16[1536,768]{1,0:T(8,128)(2,1)}, u32[]{:S(2)}) copy-start(bf16[1536,768]{1,0:T(8,128)(2,1)} %get-tuple-element.204) | copy-start | bytes 7077892
  507.1 1.4 copy-start.1
  (2 other events, 1.8 us)

commit v5 on v4

--- a/solution.py
+++ b/solution.py
@@ -100,13 +100,6 @@
     places = jnp.arange(TILE, dtype=jnp.int32)
     offsets = jnp.concatenate([-places, TILE - places, 0 * places - SEQ, 0 * places + SEQ])
     return (bucket_of(offsets)[:, None] == jnp.arange(count, dtype=jnp.int32)[None, :]).astype(F32)
-
-
-def dispatch_kernel(slot_ref, rows_ref, out_ref):
-    block, tokens = out_ref.shape[0], rows_ref.shape[0]
-    ids = lax.broadcasted_iota(jnp.int32, (block, tokens), 0) + pl.program_id(0) * block
-    picks = jnp.where(slot_ref[...] == ids, 1.0, 0.0).astype(BF)
-    out_ref[...] = mm(picks, rows_ref[...]).astype(BF)
 
 
 def dispatch_gate_kernel(experts, capacity, padded, slot_ref, gate_ref, rows_ref, out_ref):
@@ -133,7 +126,7 @@
     out_ref[:, lanes:] = out[:, lanes:].astype(BF)
 
 
-def dispatch(slot_row, rows, blocks, block, gate=None):
+def dispatch(slot_row, rows, blocks, block, gate):
     tokens, width = rows.shape
     grid_spec = dict(
         grid=(blocks,),
@@ -142,19 +135,52 @@
     )
     line = pl.BlockSpec((1, tokens), lambda k: (0, 0))
     full = pl.BlockSpec((tokens, width), lambda k: (0, 0))
-    cost = NO_COST
-    if gate is None:
-        return pl.pallas_call(
-            dispatch_kernel, in_specs=[line, full], compiler_params=params(), cost_estimate=cost, **grid_spec
-        )(slot_row, rows)
     values, experts, capacity, padded = gate
     return pl.pallas_call(
         functools.partial(dispatch_gate_kernel, experts, capacity, padded),
         in_specs=[line, line, full],
         compiler_params=params(),
-        cost_estimate=cost,
+        cost_estimate=NO_COST,
         **grid_spec,
     )(slot_row, values, rows)
+
+
+def dispatch_by_group_kernel(slot_ref, rows_ref, mine_ref, other_ref):
+    block, tokens = mine_ref.shape[0], rows_ref.shape[0]
+    step = pl.program_id(0)
+    ids = lax.broadcasted_iota(jnp.int32, (block, tokens), 0) + step * block
+    picks = jnp.where(slot_ref[...] == ids, 1.0, 0.0).astype(BF)
+    out = mm(picks, rows_ref[...]).astype(BF)
+    first = step < pl.num_programs(0) // 2
+
+    @pl.when(first)
+    def _():
+        mine_ref[...] = out
+
+    @pl.when(jnp.logical_not(first))
+    def _():
+        other_ref[...] = out
+
+
+def dispatch_by_group(slot_row, rows, slots):
+    tokens, width = rows.shape
+    block = 256
+    steps = slots // block
+    return pl.pallas_call(
+        dispatch_by_group_kernel,
+        grid=(2 * steps,),
+        in_specs=[
+            pl.BlockSpec((1, tokens), lambda k: (0, 0)),
+            pl.BlockSpec((tokens, width), lambda k: (0, 0)),
+        ],
+        out_specs=[
+            pl.BlockSpec((block, width), lambda k: (jnp.minimum(k, steps - 1), 0)),
+            pl.BlockSpec((block, width), lambda k: (jnp.maximum(k - steps, 0), 0)),
+        ],
+        out_shape=[jax.ShapeDtypeStruct((slots, width), BF)] * 2,
+        compiler_params=params(),
+        cost_estimate=NO_COST,
+    )(slot_row, rows)
 
 
 def qkv_kernel(x_ref, gain_ref, wq_ref, wk_ref, wv_ref, q_ref, k_ref, v_ref):
@@ -226,38 +252,38 @@
 
 
 def attention_kernel(
-    lines_ref, sent_ref, q_ref, k_ref, v_ref, o_ref, lse_ref, came_ref, bias_ref, local_sem, send_sem, recv_sem
+    lines_ref, mine_ref, other_ref, q_ref, k_ref, v_ref, o_ref, lse_ref, came_ref,
+    bias_ref, local_sem, send_sem, recv_sem
 ):
     pair, seq = pl.program_id(0), pl.program_id(1)
-    blocks = sent_ref.shape[0]
-    me = lax.axis_index("exp")
-
-    def there(block):
-        return {"exp": flipped(me, block)}
-
-    def outgoing(block):
-        return pltpu.make_async_remote_copy(
-            src_ref=sent_ref.at[block],
-            dst_ref=came_ref.at[:, block],
-            send_sem=send_sem.at[block],
-            recv_sem=recv_sem.at[block],
-            device_id=there(block),
-            device_id_type=pl.DeviceIdType.MESH,
-        )
-
-    own = pltpu.make_async_copy(sent_ref.at[0], came_ref.at[:, 0], local_sem)
+    blocks, half = mine_ref.shape[:2]
+    me, group = lax.axis_index("exp"), lax.axis_index("dp") % 2
+
+    def transfers():
+        copies = []
+        for kind, sent in enumerate((mine_ref, other_ref)):
+            experts = pl.ds((group + kind) % 2 * half, half)
+            copies.append(
+                pltpu.make_async_copy(sent.at[0], came_ref.at[experts, 0], local_sem.at[kind])
+            )
+            for block in range(1, blocks):
+                copies.append(
+                    pltpu.make_async_remote_copy(
+                        src_ref=sent.at[block],
+                        dst_ref=came_ref.at[experts, block],
+                        send_sem=send_sem.at[kind, block],
+                        recv_sem=recv_sem.at[kind, block],
+                        device_id={"exp": flipped(me, block)},
+                        device_id_type=pl.DeviceIdType.MESH,
+                    )
+                )
+        return copies
 
     @pl.when((pair == 0) & (seq == 0))
     def _():
-        barrier = pltpu.get_barrier_semaphore()
-        for block in range(1, blocks):
-            pl.semaphore_signal(
-                barrier, inc=1, device_id=there(block), device_id_type=pl.DeviceIdType.MESH
-            )
-        pl.semaphore_wait(barrier, blocks - 1)
-        own.start()
-        for block in range(1, blocks):
-            outgoing(block).start()
+        greet(me, blocks)
+        for copy in transfers():
+            copy.start()
 
     @pl.when(seq == 0)
     def _():
@@ -283,70 +309,52 @@
 
     @pl.when((pair == pl.num_programs(0) - 1) & (seq == pl.num_programs(1) - 1))
     def _():
-        own.wait()
-        for block in range(1, blocks):
-            outgoing(block).wait()
+        for copy in transfers():
+            copy.wait()
 
 
 def attention(lines, sent, q, k, v):
-    blocks, experts, padded, width = sent.shape
+    blocks, half, padded, width = sent[0].shape
     tokens, width = q.shape
     seqs, pairs = tokens // SEQ, width // PAIR
     block = pl.BlockSpec((SEQ, PAIR), lambda h, s: (s, h))
     return pl.pallas_call(
         attention_kernel,
         grid=(pairs, seqs),
-        in_specs=[pl.BlockSpec((2, 8, TILE), lambda h, s: (h, 0, 0)), pl.BlockSpec(memory_space=pl.ANY)]
+        in_specs=[pl.BlockSpec((2, 8, TILE), lambda h, s: (h, 0, 0))]
+        + [pl.BlockSpec(memory_space=pl.ANY)] * 2
         + [block, block, block],
         out_specs=[block, pl.BlockSpec((1, 1, 2, SEQ), lambda h, s: (h, s, 0, 0))]
         + [pl.BlockSpec(memory_space=pl.ANY)],
         out_shape=[
             jax.ShapeDtypeStruct((tokens, width), BF),
             jax.ShapeDtypeStruct((pairs, seqs, 2, SEQ), F32),
-            jax.ShapeDtypeStruct((experts, blocks, padded, width), BF),
+            jax.ShapeDtypeStruct((2 * half, blocks, padded, width), BF),
         ],
-        scratch_shapes=[
-            pltpu.VMEM((2, SEQ, SEQ), F32),
-            pltpu.SemaphoreType.DMA,
-            pltpu.SemaphoreType.DMA((blocks,)),
-            pltpu.SemaphoreType.DMA((blocks,)),
-        ],
+        scratch_shapes=[pltpu.VMEM((2, SEQ, SEQ), F32)] + spread_sems(2, blocks),
         compiler_params=params(collective_id=1, has_side_effects=True),
         cost_estimate=NO_COST,
-    )(lines, sent, q, k, v)
-
-
-def attention_back_kernel(parts, swaps, lines_ref, q_ref, k_ref, v_ref, do_ref, lse_ref, *refs):
-    sent_refs, swap_refs, refs = refs[:parts], refs[parts : parts + swaps], refs[parts + swaps :]
+    )(lines, *sent, q, k, v)
+
+
+def attention_back_kernel(parts, lines_ref, q_ref, k_ref, v_ref, do_ref, lse_ref, *refs):
+    sent_refs, refs = refs[:parts], refs[parts:]
     dq_ref, dk_ref, dv_ref, sums_ref = refs[:4]
-    came_refs, got_refs, refs = refs[4 : 4 + parts], refs[4 + parts : 4 + parts + swaps], refs[4 + parts + swaps :]
+    came_refs, refs = refs[4 : 4 + parts], refs[4 + parts :]
     bias_ref, diag_ref, *sems = refs
-    sems, swap_send, swap_recv = sems[:3], sems[3], sems[4]
     pair, seq = pl.program_id(0), pl.program_id(1)
     blocks, expert = came_refs[0].shape[0], sent_refs[0].shape[1] - 1
     me = lax.axis_index("exp")
-    partner = {"dp": flipped(lax.axis_index("dp"), 1)}
 
     def transfers():
         copies = []
-        for index in range(swaps):
-            copies.append(
-                pltpu.make_async_remote_copy(
-                    src_ref=swap_refs[index],
-                    dst_ref=got_refs[index],
-                    send_sem=swap_send.at[index],
-                    recv_sem=swap_recv.at[index],
-                    device_id=partner,
-                    device_id_type=pl.DeviceIdType.MESH,
-                )
-            )
         for part in range(parts):
             copies += spread(me, sent_refs[part], expert, came_refs[part], sems, part)
         return copies
 
     @pl.when((pair == 0) & (seq == 0))
     def _():
-        greet(me, blocks, [partner])
+        greet(me, blocks)
         for copy in transfers():
             copy.start()
 
@@ -428,8 +436,8 @@
             )
 
 
-def attention_back(lines, q, k, v, do, lse, sent, swapped):
-    parts, swaps = len(sent), len(swapped)
+def attention_back(lines, q, k, v, do, lse, sent):
+    parts = len(sent)
     blocks, _, padded, _ = sent[0].shape
     anywhere = pl.BlockSpec(memory_space=pl.ANY)
     tokens, width = q.shape
@@ -437,26 +445,27 @@
     block = pl.BlockSpec((SEQ, PAIR), lambda h, s: (s, h))
     lines_spec = pl.BlockSpec((2, 8, TILE), lambda h, s: (h, 0, 0))
     return pl.pallas_call(
-        functools.partial(attention_back_kernel, parts, swaps),
+        functools.partial(attention_back_kernel, parts),
         grid=(pairs, seqs),
         in_specs=[lines_spec, block, block, block, block]
         + [pl.BlockSpec((1, 1, 2, SEQ), lambda h, s: (h, s, 0, 0))]
-        + [anywhere] * (parts + swaps),
-        out_specs=[block, block, block, lines_spec] + [anywhere] * (parts + swaps),
+        + [anywhere] * parts,
+        out_specs=[block, block, block, lines_spec] + [anywhere] * parts,
         out_shape=[jax.ShapeDtypeStruct((tokens, width), BF)] * 3
         + [jax.ShapeDtypeStruct((2 * pairs, 8, TILE), F32)]
-        + [jax.ShapeDtypeStruct((blocks, padded, width), BF)] * parts
-        + [jax.ShapeDtypeStruct(array.shape, BF) for array in swapped],
+        + [jax.ShapeDtypeStruct((blocks, padded, width), BF)] * parts,
         scratch_shapes=[
             pltpu.VMEM((2, SEQ, SEQ), F32),
             pltpu.VMEM((2, 5, TILE, TILE), F32),
             *spread_sems(parts, blocks),
-            pltpu.SemaphoreType.DMA((swaps,)),
-            pltpu.SemaphoreType.DMA((swaps,)),
         ],
         compiler_params=params(collective_id=4, has_side_effects=True),
-        cost_estimate=NO_COST,
-    )(lines, q, k, v, do, lse, *sent, *swapped)
+        cost_estimate=pl.CostEstimate(
+            flops=40 * pairs * seqs * SEQ * SEQ * PAIR,
+            bytes_accessed=14 * tokens * width,
+            transcendentals=2 * pairs * seqs * SEQ * SEQ,
+        ),
+    )(lines, q, k, v, do, lse, *sent)
 
 
 def router_kernel(
@@ -549,19 +558,14 @@
         d_sum[...] += mm_nt(inner, first)
 
 
-def expert_kernel(
-    parts, sent_ref, c_ref, first_ref, second_ref, *refs
-):
+def expert_kernel(parts, all_experts, sent_ref, c_ref, first_ref, second_ref, *refs):
     expert, step = pl.program_id(0), pl.program_id(1)
     count, last_step = pl.num_programs(0), pl.num_programs(1) - 1
-    all_experts = count + 1
-    u_refs, u_last, refs = refs[:all_experts], refs[all_experts], refs[all_experts + 1 :]
-    e_kept, d_kept, e_ref, d_ref, rows_ref, e_sum, d_sum, e_held, d_held = refs[:9]
-    local_sem, send_sem, recv_sem, back_send, back_recv, back_local = refs[9:]
-    _, blocks, padded, width = rows_ref.shape
+    u_refs, u_late, refs = refs[:all_experts], refs[all_experts], refs[all_experts + 1 :]
+    e_kept, d_kept, rows_ref, e_sum, d_sum, e_held, d_held, local_sem, send_sem, recv_sem = refs
+    early, blocks, padded, width = e_held.shape
     me = lax.axis_index("exp")
     group, half = lax.axis_index("dp") % 2, all_experts // 2
-    sems = (back_send, back_recv, back_local)
 
     def outgoing(which, block):
         return pltpu.make_async_remote_copy(
@@ -584,8 +588,12 @@
             def _(target=target):
                 act(pltpu.make_async_copy(rows_ref.at[which], target, local_sem.at[1, which]))
 
-        if which == all_experts - 1:
-            act(pltpu.make_async_copy(rows_ref.at[which], u_last, local_sem.at[2, 0]))
+        if which >= early:
+            act(
+                pltpu.make_async_copy(
+                    rows_ref.at[which], u_late.at[which - early], local_sem.at[2, which - early]
+                )
+            )
 
     def arrive(which):
         own_in(which).wait()
@@ -595,14 +603,9 @@
 
     def keep_result(which):
         return [
-            pltpu.make_async_copy(e_held.at[which], e_kept.at[which - 1], local_sem.at[2, which]),
-            pltpu.make_async_copy(d_held.at[which], d_kept.at[which - 1], local_sem.at[3, which]),
+            pltpu.make_async_copy(e_held.at[which], e_kept.at[which], local_sem.at[3, which]),
+            pltpu.make_async_copy(d_held.at[which], d_kept.at[which], local_sem.at[4, which]),
         ]
-
-    def back():
-        return send_back(me, e_held.at[0], e_ref, 0, 0, sems, 0) + send_back(
-            me, d_held.at[0], d_ref, 0, 0, sems, 1
-        )
 
     @pl.when((expert == 0) & (step == 0))
     def _():
@@ -614,7 +617,7 @@
 
     @pl.when(step == 0)
     def _():
-        for which in range(all_experts - 1):
+        for which in range(early):
 
             @pl.when(expert == which)
             def _(which=which):
@@ -630,13 +633,7 @@
     def _():
         e_held[expert] = e_sum[...].astype(BF).reshape(blocks, padded, width)
         d_held[expert] = d_sum[...].astype(BF).reshape(blocks, padded, width)
-
-        @pl.when(expert == 0)
-        def _():
-            for copy in back():
-                copy.start()
-
-        for which in range(1, all_experts - 1):
+        for which in range(early):
 
             @pl.when(expert == which)
             def _(which=which):
@@ -645,51 +642,66 @@
 
     @pl.when((step == last_step) & (expert == count - 1))
     def _():
-        arrive(all_experts - 1)
+        for which in range(early, all_experts):
+            arrive(which)
         for which in range(all_experts):
             keep(which, lambda copy: copy.wait())
             for block in range(1, blocks):
                 outgoing(which, block).wait_send()
-        for which in range(1, all_experts - 1):
+        for which in range(early):
             for copy in keep_result(which):
                 copy.wait()
-        for copy in back():
-            copy.wait()
 
 
 def expert_rest_kernel(
-    parts, kept, u_ref, c_ref, first_ref, second_ref, e_kept, d_kept, e_ref, d_ref,
+    parts, u_ref, c_ref, first_ref, second_ref, e_kept, d_kept, e_ref, d_ref,
     e_sum, d_sum, e_held, d_held, back_send, back_recv, back_local,
 ):
-    step, last_step = pl.program_id(0), pl.num_programs(0) - 1
-    blocks, padded, width = e_held.shape
+    expert, step = pl.program_id(0), pl.program_id(1)
+    count, last_step = pl.num_programs(0), pl.num_programs(1) - 1
+    late, blocks, padded, width = e_held.shape
+    kept = e_kept.shape[0]
     me = lax.axis_index("exp")
     sems = (back_send, back_recv, back_local)
 
     def back(which):
-        e_from, d_from = (e_kept.at[which], d_kept.at[which]) if which < kept else (e_held, d_held)
+        if which < kept:
+            e_from, d_from = e_kept.at[which], d_kept.at[which]
+        else:
+            e_from, d_from = e_held.at[which - kept], d_held.at[which - kept]
         return send_back(me, e_from, e_ref, which, which, sems, 0) + send_back(
             me, d_from, d_ref, which, which, sems, 1
         )
 
-    @pl.when(step == 0)
+    @pl.when((expert == 0) & (step == 0))
     def _():
         greet(me, blocks)
         for which in range(kept):
             for copy in back(which):
                 copy.start()
+
+    @pl.when(step == 0)
+    def _():
         e_sum[...] = jnp.zeros_like(e_sum)
         d_sum[...] = jnp.zeros_like(d_sum)
 
-    expert_step(parts, u_ref[...], c_ref[0], first_ref, second_ref, e_sum, d_sum)
+    rows = u_ref[0].reshape(blocks * padded, width)
+    expert_step(parts, rows, c_ref[0], first_ref, second_ref, e_sum, d_sum)
 
     @pl.when(step == last_step)
     def _():
-        e_held[...] = e_sum[...].astype(BF).reshape(blocks, padded, width)
-        d_held[...] = d_sum[...].astype(BF).reshape(blocks, padded, width)
-        for copy in back(kept):
-            copy.start()
-        for which in range(kept + 1):
+        e_held[expert] = e_sum[...].astype(BF).reshape(blocks, padded, width)
+        d_held[expert] = d_sum[...].astype(BF).reshape(blocks, padded, width)
+        for which in range(late):
+
+            @pl.when(expert == which)
+            def _(which=which):
+                for copy in back(kept + which):
+                    copy.start()
+
+    @pl.when((step == last_step) & (expert == count - 1))
+    def _():
+        for which in range(kept + late):
             for copy in back(which):
                 copy.wait()
 
@@ -699,72 +711,65 @@
     hidden = w_in.shape[2]
     size = 768
     rows = blocks * padded
-    kept = experts - 2
+    early = experts // 2
+    late = experts - early
     anywhere = pl.BlockSpec(memory_space=pl.ANY)
     dma = pltpu.SemaphoreType.DMA
-    *u_rows, u_last, e_kept, d_kept, e_first, d_first = pl.pallas_call(
-        functools.partial(expert_kernel, 3),
-        grid=(experts - 1, hidden // size),
-        in_specs=[
-            anywhere,
-            pl.BlockSpec((1, rows, width), lambda e, f: (e, 0, 0)),
-            pl.BlockSpec((1, width, size), lambda e, f: (e, 0, f)),
-            pl.BlockSpec((1, size, width), lambda e, f: (e, f, 0)),
-        ],
-        out_specs=[anywhere] * (experts + 5),
-        out_shape=[jax.ShapeDtypeStruct((blocks, padded, width), BF)] * (experts + 1)
-        + [
-            jax.ShapeDtypeStruct((kept, blocks, padded, width), BF),
-            jax.ShapeDtypeStruct((kept, blocks, padded, width), BF),
-            jax.ShapeDtypeStruct((blocks, 1, padded, width), BF),
-            jax.ShapeDtypeStruct((blocks, 1, padded, width), BF),
-        ],
+
+    def results(count):
+        return jax.ShapeDtypeStruct((count, blocks, padded, width), BF)
+
+    def weights(first):
+        return [
+            pl.BlockSpec((1, rows, width), lambda e, f: (first + e, 0, 0)),
+            pl.BlockSpec((1, width, size), lambda e, f: (first + e, 0, f)),
+            pl.BlockSpec((1, size, width), lambda e, f: (first + e, f, 0)),
+        ]
+
+    *u_rows, u_late, e_kept, d_kept = pl.pallas_call(
+        functools.partial(expert_kernel, 3, experts),
+        grid=(early, hidden // size),
+        in_specs=[anywhere] + weights(0),
+        out_specs=[anywhere] * (experts + 3),
+        out_shape=[jax.ShapeDtypeStruct((blocks, padded, width), BF)] * experts
+        + [results(late), results(early), results(early)],
         scratch_shapes=[
             pltpu.VMEM((experts, blocks, padded, width), BF),
             pltpu.VMEM((rows, width), F32),
             pltpu.VMEM((rows, width), F32),
-            pltpu.VMEM((experts - 1, blocks, padded, width), BF),
-            pltpu.VMEM((experts - 1, blocks, padded, width), BF),
-            dma((4, experts)),
+            pltpu.VMEM((early, blocks, padded, width), BF),
+            pltpu.VMEM((early, blocks, padded, width), BF),
+            dma((5, experts)),
             dma((experts, blocks)),
             dma((experts, blocks)),
-            dma((2, 1, blocks)),
-            dma((2, 1, blocks)),
-            dma((2, 1)),
         ],
         compiler_params=params(collective_id=0, has_side_effects=True),
         cost_estimate=NO_COST,
     )(sent, c, w_in, w_out)
     u_rows = [part.reshape(rows, width) for part in u_rows]
-    last = experts - 1
-    e_rest, d_rest = pl.pallas_call(
-        functools.partial(expert_rest_kernel, 3, kept),
-        grid=(hidden // size,),
-        in_specs=[
-            pl.BlockSpec((rows, width), lambda f: (0, 0)),
-            pl.BlockSpec((1, rows, width), lambda f: (last, 0, 0)),
-            pl.BlockSpec((1, width, size), lambda f: (last, 0, f)),
-            pl.BlockSpec((1, size, width), lambda f: (last, f, 0)),
-            anywhere,
-            anywhere,
-        ],
+    e_back, d_back = pl.pallas_call(
+        functools.partial(expert_rest_kernel, 3),
+        grid=(late, hidden // size),
+        in_specs=[pl.BlockSpec((1, blocks, padded, width), lambda e, f: (e, 0, 0, 0))]
+        + weights(early)
+        + [anywhere] * 2,
         out_specs=[anywhere] * 2,
-        out_shape=[jax.ShapeDtypeStruct((blocks, kept + 1, padded, width), BF)] * 2,
+        out_shape=[jax.ShapeDtypeStruct((blocks, experts, padded, width), BF)] * 2,
         scratch_shapes=[
             pltpu.VMEM((rows, width), F32),
             pltpu.VMEM((rows, width), F32),
-            pltpu.VMEM((blocks, padded, width), BF),
-            pltpu.VMEM((blocks, padded, width), BF),
-            dma((2, kept + 1, blocks)),
-            dma((2, kept + 1, blocks)),
-            dma((2, kept + 1)),
+            pltpu.VMEM((late, blocks, padded, width), BF),
+            pltpu.VMEM((late, blocks, padded, width), BF),
+            dma((2, experts, blocks)),
+            dma((2, experts, blocks)),
+            dma((2, experts)),
         ],
         compiler_params=params(collective_id=3, has_side_effects=True),
         cost_estimate=pl.CostEstimate(
             flops=32 * rows * width * hidden, bytes_accessed=4 * width * hidden, transcendentals=0
         ),
-    )(u_last.reshape(rows, width), c, w_in, w_out, e_kept, d_kept)
-    return u_rows, (e_first, e_rest), (d_first, d_rest)
+    )(u_late, c, w_in, w_out, e_kept, d_kept)
+    return u_rows, e_back, d_back
 
 
 def weights_kernel(parts, sources, capacity, padded, place_ref, *refs):
@@ -875,9 +880,9 @@
     u_refs, refs = refs[: sources * experts], refs[sources * experts :]
     c_own, c_far, refs = refs[0], refs[1 : 1 + (sources - 1) * experts], refs[1 + (sources - 1) * experts :]
     (
-        first_ref, second_ref, dense_o, dense_qkv, small_ref,
+        first_ref, second_ref, far_in, far_out, dense_o, dense_qkv, small_ref,
         own_in_ref, own_out_ref, came_in_ref, came_out_ref, dense_ref, total_ref,
-        rows_u, rows_c, first_held, second_held, first_t, in_sum, out_sum, far_in, far_out, own_in, own_out,
+        rows_u, rows_c, first_held, second_held, first_t, in_sum, out_sum, own_in, own_out,
         dense, dense_came, dense_over_dp, small, small_came,
         rows_sem, weight_sem, load_sem, far_send, far_recv, own_sem,
         half_send, half_recv, over_send, over_recv, back_send, back_recv, small_send, small_recv, keep_sem,
@@ -1046,7 +1051,7 @@
     stages += [give_back(depth) for depth in reversed(range(exp_bits))]
     stages = [functools.partial(stage, side) for stage in stages for side in range(2)]
 
-    steps, turns = 1 + experts, (1 + experts) * sources
+    steps, turns = experts, experts * sources
 
     def rows_copy(source, expert):
         if source == 0:
@@ -1065,9 +1070,8 @@
         ]
 
     def weight_copy(step):
-        far = step == 0
-        expert = group * experts + jnp.where(far, experts - 1, step - 1)
-        place = (pair * 2 + jnp.where(far, 1 - group, group)) * size
+        expert = group * experts + step
+        place = (pair * 2 + group) * size
         place = pl.ds(pl.multiple_of(place, 128), size)
         slot = step % 2
         return [
@@ -1105,7 +1109,7 @@
         load.start()
     for copy in weight_copy(0):
         copy.start()
-    for expert in reversed(range(experts)):
+    for expert in range(experts):
         for source in range(sources):
             for copy in rows_copy(source, expert):
                 copy.start()
@@ -1118,13 +1122,13 @@
 
     places = [0, 0, 1, 2, 3, 4, 5, 6]
     places = [place for place in places if place < turns][: len(stages)]
-    starts = {7: 2, 9: 3}
+    starts = {4: 3}
     starts = {place: index for place, index in starts.items() if place < turns}
     pieces = 2 * far_parts
 
     def turn(at, carry):
         step, source = at // sources, at % sources
-        expert, slot = jnp.where(step == 0, experts - 1, step - 1), step % 2
+        expert, slot = step, step % 2
         for place, stage in zip(places, stages):
             pl.when(at == place)(stage)
         for place, index in starts.items():
@@ -1144,9 +1148,8 @@
 
         for each_expert in range(experts):
             for each in range(sources):
-                first_step = 0 if each_expert == experts - 1 else each_expert + 1
-
-                @pl.when(at == first_step * sources + each)
+
+                @pl.when(at == each_expert * sources + each)
                 def _(each=each, each_expert=each_expert):
                     for copy in rows_copy(each, each_expert):
                         copy.wait()
@@ -1166,16 +1169,9 @@
             in_sum[here, :] = jnp.where(fresh, 0.0, in_sum[here, :]) + in_term
             out_sum[here, :] = jnp.where(fresh, 0.0, out_sum[here, :]) + out_term
 
-        @pl.when((source == sources - 1) & (step == 0))
-        def _():
-            far_in[...] = in_sum[...].T.astype(BF)
-            far_out[...] = out_sum[...].astype(BF)
-            for index in range(2):
-                far_copy(index).start()
-
         for each_expert in range(experts):
 
-            @pl.when((source == sources - 1) & (step == each_expert + 1))
+            @pl.when((source == sources - 1) & (step == each_expert))
             def _(each_expert=each_expert):
                 own_in[each_expert] = in_sum[...].T.astype(BF)
                 own_out[each_expert] = out_sum[...].astype(BF)
@@ -1184,10 +1180,12 @@
 
         return carry
 
+    for index in range(3):
+        far_copy(index).start()
     lax.fori_loop(0, turns, turn, 0)
     for stage in stages[len(places) : len(places) + 2]:
         stage()
-    for index in range(2 + len(starts), pieces):
+    for index in range(3 + len(starts), pieces):
         far_copy(index).start()
     for stage in stages[len(places) + 2 :]:
         stage()
@@ -1208,7 +1206,7 @@
         small_copy(depth).wait_send()
 
 
-def tail(us, c_rows, c_far, w_in, w_out, size, dense_o, dense_qkv, small, capacity, padded, exp_n):
+def tail(us, c_rows, c_far, w_in, w_out, far_in, far_out, size, dense_o, dense_qkv, small, capacity, padded, exp_n):
     sources, experts = len(us[0]), len(us)
     rows, width = us[0][0].shape
     far_parts = 4
@@ -1218,7 +1216,7 @@
     dma = pltpu.SemaphoreType.DMA
     return pl.pallas_call(
         functools.partial(tail_kernel, 3, sources, experts, capacity, padded),
-        in_specs=[anywhere] * (experts * (2 * sources - 1) + 6),
+        in_specs=[anywhere] * (experts * (2 * sources - 1) + 8),
         out_specs=[anywhere] * 5 + [pl.BlockSpec(memory_space=pltpu.VMEM)],
         out_shape=[
             jax.ShapeDtypeStruct((experts, width, size), BF),
@@ -1236,8 +1234,6 @@
             pltpu.VMEM((size, width), BF),
             pltpu.VMEM((size, width), F32),
             pltpu.VMEM((size, width), F32),
-            pltpu.VMEM((width, size), BF),
-            pltpu.VMEM((size, width), BF),
             pltpu.VMEM((experts, width, size), BF),
             pltpu.VMEM((experts, size, width), BF),
             pltpu.VMEM((lines, width), BF),
@@ -1265,12 +1261,12 @@
             vmem_limit_bytes=58 * 2**20, collective_id=2, has_side_effects=True
         ),
         cost_estimate=NO_COST,
-    )(*sum(us, []), c_rows, *sum(c_far, []), w_in, w_out, dense_o, dense_qkv, small)
+    )(*sum(us, []), c_rows, *sum(c_far, []), w_in, w_out, far_in, far_out, dense_o, dense_qkv, small)
 
 
 def combine_kernel(
     parts, experts, slot_ref, expert_ref, gate_ref, probs_ref, h_ref, c_ref, o_ref,
-    e_first, e_rest, d_first, d_rest, wo_ref, wr_ref, gain_ref, *refs
+    e_ref, d_ref, wo_ref, wr_ref, gain_ref, *refs
 ):
     sent_refs, refs = refs[:parts], refs[parts:]
     mixed_ref, dh_ref, do_ref, wo_ref_out, wr_sum, gain_sum = refs[:6]
@@ -1298,14 +1294,12 @@
         for copy in transfers():
             copy.wait()
 
-    tokens, early = slot_ref.shape[1], e_first.shape[0]
-    slots = early + e_rest.shape[0]
+    tokens, slots = slot_ref.shape[1], e_ref.shape[0]
     slot = as_column(slot_ref[...].astype(F32)).astype(jnp.int32)
     picks = jnp.where(
         slot == lax.broadcasted_iota(jnp.int32, (tokens, slots), 1), 1.0, 0.0
     ).astype(BF)
-    returned = mm(picks[:, :early], e_first[...]) + mm(picks[:, early:], e_rest[...])
-    arrived = mm(picks[:, :early], d_first[...]) + mm(picks[:, early:], d_rest[...])
+    returned, arrived = mm(picks, e_ref[...]), mm(picks, d_ref[...])
     gate, probs, mixed = gate_ref[...], probs_ref[...], h_ref[...]
     upstream = c_ref[...].astype(F32)
     mixed_ref[...] = (mixed + gate * returned).astype(BF)
@@ -1349,8 +1343,7 @@
     spreads = parts * (local - 1)
     anywhere = pl.BlockSpec(memory_space=pl.ANY)
     tokens, width = h.shape
-    early, rest = (part.shape[0] for part in e_out)
-    slots, experts = early + rest, wr.shape[1]
+    slots, experts = e_out.shape[0], wr.shape[1]
     size = 256
 
     def rows(columns):
@@ -1363,7 +1356,7 @@
         functools.partial(combine_kernel, parts, local - 1),
         grid=(tokens // size,),
         in_specs=[pl.BlockSpec((1, size), lambda t: (0, t)), rows(1), rows(1), rows(experts), rows(width), rows(width), rows(width)]
-        + [whole(early, width), whole(rest, width)] * 2
+        + [whole(slots, width)] * 2
         + [whole(width, width), whole(width, experts)]
         + [whole(1, width)]
         + [anywhere] * parts,
@@ -1382,7 +1375,7 @@
         scratch_shapes=[pltpu.VMEM((width, width), F32)] + spread_sems(spreads, blocks),
         compiler_params=params(collective_id=5, has_side_effects=True),
         cost_estimate=NO_COST,
-    )(slot, expert, gate, probs, h, c, o, *e_out, *du, wo, wr, gain, *sent)
+    )(slot, expert, gate, probs, h, c, o, e_out, du, wo, wr, gain, *sent)
 
 
 def last_kernel(
@@ -1478,21 +1471,18 @@
     rank = jnp.sum(ahead.astype(jnp.int32), axis=1)
     place = ((chosen // local) ^ exp_me) * block + (chosen % local) * padded + rank
     slots = jnp.where(rank < capacity, place, -1)
-    chunk, inside = slots // block, slots % block
-    later = exp_n * padded + chunk * (block - padded) + inside - padded
-    returned_slots = jnp.where(inside < padded, chunk * padded + inside, later)
-    returned_slots = jnp.where(slots < 0, -1, returned_slots)
-    slot_row, returned_row = slots[None, :], returned_slots[None, :]
-
+    slot_row = slots[None, :]
     half = local // 2
     group = dp_me % 2
+    inside = chosen % local
+    grouped = ((inside // half + group) % 2 * exp_n + place // block) * half + inside % half
+    c_row = jnp.where(rank < capacity, grouped * padded + rank, -1)[None, :]
+
+    def to_dp(rows, step):
+        return lax.ppermute(rows, "dp", [(i, i ^ step) for i in range(dp_n)])
 
     def over_dp(mine, other):
-        pieces = [mine]
-        for step in range(1, dp_n):
-            pairs = [(i, i ^ step) for i in range(dp_n)]
-            pieces.append(lax.ppermute(other if step % 2 else mine, "dp", pairs))
-        return pieces
+        return [mine] + [to_dp(other if step % 2 else mine, step) for step in range(1, dp_n)]
 
     lines = jnp.dot(
         relative_bias_table.T, diagonal_onehot(buckets).T, precision=FULL_PRECISION
@@ -1500,11 +1490,11 @@
     lines = jnp.concatenate([lines, jnp.zeros_like(lines)], axis=1)
     gain_attn, gain_ffn = norm_attn[None, :], norm_ffn[None, :]
     q, k, v = qkv(tokens, gain_attn, w_query, w_key, w_value)
-    c_sent = dispatch(slot_row, cotangent, exp_n, block).reshape(exp_n, local, padded, width)
-    c_far = over_dp(
-        lax.dynamic_slice_in_dim(c_sent, group * half, half, 1),
-        lax.dynamic_slice_in_dim(c_sent, (1 - group) * half, half, 1),
-    )[1:]
+    c_sent = [
+        part.reshape(exp_n, half, padded, width)
+        for part in dispatch_by_group(c_row, cotangent, exp_n * half * padded)
+    ]
+    c_far = over_dp(*c_sent)[1:]
     context, lse, c_rows = attention(lines, c_sent, q, k, v)
     c_rows = c_rows.reshape(local, exp_n * padded, width)
     mixed, u, probs, gate, gate_row = router(
@@ -1515,34 +1505,45 @@
         sent.reshape(exp_n, local, padded, width), c_rows, w_in, w_out
     )
     mine, other = u_rows[:half], u_rows[half:]
-    mine[0], *c_far = lax.optimization_barrier((mine[0], *c_far))
+    mine[0], other[0], c_far[0] = lax.optimization_barrier((mine[0], other[0], c_far[0]))
     u_all = [over_dp(mine[0], other[0])]
     for expert in range(1, half):
-        late, *u_all[-1], mine[expert], other[expert] = lax.optimization_barrier(
-            (e_back[1], *u_all[-1], mine[expert], other[expert])
+        e_back, mine[expert], other[expert], *c_far[1:] = lax.optimization_barrier(
+            (e_back, mine[expert], other[expert], *c_far[1:])
         )
-        e_back = (e_back[0], late)
-        u_all.append(over_dp(mine[expert], other[expert]))
-    e_back, d_back = ([part.reshape(-1, width) for part in parts] for parts in (e_back, d_back))
+        u_all.append([mine[expert], None] + [
+            to_dp(other[expert] if step % 2 else mine[expert], step) for step in range(2, dp_n)
+        ])
+    e_back, d_back = e_back.reshape(-1, width), d_back.reshape(-1, width)
     mixed_out, mixed_grad, context_grad, output_part, router_part, norm_ffn_part, *c_early = combine(
-        returned_row, expert_index, gate, probs, mixed, cotangent, context,
+        slot_row, expert_index, gate, probs, mixed, cotangent, context,
         e_back, d_back, w_output, w_router, gain_ffn, c_far,
     )
+    for expert in range(1, half):
+        context_grad, *u_all[0], other[expert] = lax.optimization_barrier(
+            (context_grad, *u_all[0], other[expert])
+        )
+        u_all[expert][1] = to_dp(other[expert], 1)
     size = w_in.shape[2] // dp_n
     rows = exp_n * padded
     c_early = [part.reshape(rows, width) for part in c_early]
     c_spread = [c_early[at : at + dp_n - 1] for at in range(0, len(c_early), dp_n - 1)]
-    swapped = []
-    for expert in range(half - 1):
+
+    def for_partner(expert):
         where = jnp.stack([group * half + expert, dp_me // 2 * 2 + 1 - group]).astype(jnp.int32)
-        swapped += weight_grads(
+        return weight_grads(
             where, u_all[expert], c_rows, c_spread[expert], w_in, w_out, size, capacity, padded
         )
-    query_grad, key_grad, value_grad, sums, *moved = attention_back(
-        lines, q, k, v, context_grad, lse, c_far, swapped
+
+    got = []
+    for expert in range(half - 1):
+        context_grad, *far = lax.optimization_barrier((context_grad, *for_partner(expert)))
+        got += [to_dp(array, 1) for array in far]
+    query_grad, key_grad, value_grad, sums, *c_late = attention_back(
+        lines, q, k, v, context_grad, lse, c_far
     )
-    c_late, got = moved[: dp_n - 1], moved[dp_n - 1 :]
     c_spread.append([part.reshape(rows, width) for part in c_late])
+    query_grad, far_in, far_out = lax.optimization_barrier((query_grad, *for_partner(half - 1)))
     table_part = jnp.dot(
         diagonal_onehot(buckets).T,
         sums[:, :4].reshape(HEADS, 4 * TILE).T,
@@ -1556,7 +1557,7 @@
     small = jnp.concatenate([router_part, norm_attn_part, norm_ffn_part, table_line], axis=0)
     small = jnp.pad(small, ((0, -small.shape[0] % 8), (0, 0)))
     own_in, own_out, came_in, came_out, dense, total = tail(
-        u_all, c_rows, c_spread, w_in, w_out, size, output_part, qkv_part, small, capacity, padded, exp_n
+        u_all, c_rows, c_spread, w_in, w_out, far_in, far_out, size, output_part, qkv_part, small, capacity, padded, exp_n
     )
     experts = jnp.arange(local, dtype=jnp.int32)
     grad_in, grad_out, *dense_grads = finish(

time: 518 us -> 511 us (0.986)
  waiting for transfers between devices: 8.34 us -> 0.03 us
  local copies, waits for them, and re-layouts: 19.4 us -> 14 us
    pallas_call x1 -> x2, Pallas kernels: 17.7 us -> 35.3 us  [weight_grads(): pl.pallas_call(functools.partial(weights_kernel, 3, sources, capacity, pa...]
    pallas_call x1, Pallas kernels: 109 us -> 95.6 us  [tail(): pl.pallas_call(functools.partial(tail_kernel, 3, sources, experts, capaci...]
    ppermute x9 -> x11, waiting for transfers between devices: 8.34 us -> 0.03 us  [to_dp(): return lax.ppermute(rows, 'dp', [(i, i ^ step) for i in range(dp_n)])]
    ppermute x9 -> x11, starting transfers between devices: 13.6 us -> 16.5 us  [to_dp(): return lax.ppermute(rows, 'dp', [(i, i ^ step) for i in range(dp_n)])]
  transfers between devices with their start and end apart: 9 -> 11, of which waited for: 1 -> 0; matrix products, arithmetic and copies ran while one was open for 2% -> 3% of each run, Pallas kernels for 64% -> 87%
where the time goes in v5:
time: 511 us; the launch traced here: 502 us
  Pallas kernels  461 us (90%)
  starting transfers between devices  16.5 us (3%)
  local copies, waits for them, and re-layouts  14 us (3%)
  other arithmetic  7.96 us (2%)
    pallas_call x1, Pallas kernels, tail(): pl.pallas_call(functools.partial(tail_kernel, 3, sources, experts, capaci...  95.6 us
    pallas_call x1, Pallas kernels, expert_pass(): pl.pallas_call(functools.partial(expert_rest_kernel, 3), grid=(late, hidd...  74.8 us
    pallas_call x1, Pallas kernels, attention_back(): pl.pallas_call(functools.partial(attention_back_kernel, parts), grid=(pai...  53.9 us
    pallas_call x1, Pallas kernels, expert_pass(): pl.pallas_call(functools.partial(expert_kernel, 3, experts), grid=(early,...  43.7 us
    pallas_call x1, Pallas kernels, attention(): pl.pallas_call(attention_kernel, grid=(pairs, seqs), in_specs=[pl.BlockSp...  41 us
    pallas_call x1, Pallas kernels, combine(): pl.pallas_call(functools.partial(combine_kernel, parts, local - 1), grid=...  39.8 us
    pallas_call x2, Pallas kernels, weight_grads(): pl.pallas_call(functools.partial(weights_kernel, 3, sources, capacity, pa...  35.3 us
    pallas_call x1, Pallas kernels, last(): pl.pallas_call(last_kernel, grid=(tokens // size,), in_specs=[rows] * 5 +...  20.4 us
  transfers between devices with their start and end apart: 11, of which 0 were waited for; matrix products, arithmetic and copies ran while one was open for 3% of the time, Pallas kernels for 87%

profile of v5, /device:TPU:0, one launch (start us, length us, event | category | flops | bytes accessed | tf_op | source)
XLA Modules:
  0.0 501.8 jit_solution(1079692736948110870)
XLA Ops:
  2.2 2.0 convert_reduce_fusion
  4.2 1.5 compare_select_fusion.11
  5.6 9.3 %shard_map.229 = (bf16[1024,768]{1,0:T(8,128)(2,1)}, bf16[1024,768]{1,0:T(8,128)(2,1)}) custom-call(s32[1,1536]{1,0:T(1,128)} %get-tuple-element.204.slot_ref, bf16[1536,768]{1,0:T(8,128)(2,1)} %c_ref.1), custom_call_target="tpu_custom_call" | custom-call | bytes 65536 | tf_op jit(solution)/shard_map/pallas_call | solution.py:169
  14.9 3.0 collective-permute-start.2
  17.9 2.5 collective-permute-start.1
  24.8 9.5 %shard_map.230 = (bf16[1536,768]{1,0:T(8,128)(2,1)}, bf16[1536,768]{1,0:T(8,128)(2,1)}, bf16[1536,768]{1,0:T(8,128)(2,1)}) custom-call(bf16[1536,768]{1,0:T(8,128)(2,1)} %x_ref.5, f32[1,768]{1,0:T(1,128)} %broadcast_in_dim.13.gain_ref, bf16[768,768]{1,0:T(8,128)(2,1)} %wq_ref.3, bf16[768,768]{1,0:T(8,128)(2,1)} %wk_ref.3, bf16[768,768]{1,0:T(8,128)(2,1)} %wv_ref.3), custom_call_target="tpu_custom_call" | custom-call | bytes 65536 | tf_op jit(solution)/shard_map/pallas_call | solution.py:200
  34.4 41.0 %shard_map.231 = (bf16[1536,768]{1,0:T(8,128)(2,1)}, f32[6,3,2,512]{3,2,1,0:T(2,128)}, bf16[4,8,64,768]{3,2,1,0:T(8,128)(2,1)}) custom-call(f32[12,8,128]{2,1,0:T(8,128)} %concatenate.24.lines_ref, bf16[8,2,64,768]{3,2,1,0:T(8,128)(2,1)} %bitcast.76, bf16[8,2,64,768]{3,2,1,0:T(8,128)(2,1)} %bitcast.74, bf16[1536,768]{1,0:T(8,128)(2,1)} %get-tuple-element.91.q_ref, ...), custom_call_target="tpu_custom_call" | custom-call | bytes 65536 | tf_op jit(solution)/shard_map/pallas_call | solution.py:321
  75.4 11.2 %shard_map.232 = (f32[1536,768]{1,0:T(8,128)}, bf16[1536,768]{1,0:T(8,128)(2,1)}, f32[1536,32]{1,0:T(8,128)}, f32[1536,1]{1,0:T(8,128)}, f32[1,1536]{1,0:T(1,128)}) custom-call(bf16[1536,768]{1,0:T(8,128)(2,1)} %get-tuple-element.94.o_ref, bf16[1536,768]{1,0:T(8,128)(2,1)} %x_ref.5, bf16[768,768]{1,0:T(8,128)(2,1)} %wo_ref.3, ...), custom_call_target="tpu_custom_call" | custom-call | bytes 65536 | tf_op jit(solution)/shard_map/pallas_call | solution.py:506
  87.2 10.9 %shard_map.233 = bf16[2048,768]{1,0:T(8,128)(2,1)} custom-call(s32[1,1536]{1,0:T(1,128)} %compare_select_fusion.12.slot_ref, f32[1,1536]{1,0:T(1,128)} %get-tuple-element.98.gate_ref, bf16[1536,768]{1,0:T(8,128)(2,1)} %get-tuple-element.99.rows_ref), custom_call_target="tpu_custom_call" | custom-call | bytes 65536 | tf_op jit(solution)/shard_map/pallas_call | solution.py:139
  98.1 43.7 %shard_map.234 = (bf16[8,64,768]{2,1,0:T(8,128)(2,1)}, bf16[8,64,768]{2,1,0:T(8,128)(2,1)}, bf16[8,64,768]{2,1,0:T(8,128)(2,1)}, bf16[8,64,768]{2,1,0:T(8,128)(2...) custom-call(bf16[8,4,64,768]{3,2,1,0:T(8,128)(2,1)} %bitcast.51, ...), custom_call_target="tpu_custom_call" | custom-call | bytes 65536 | tf_op jit(solution)/shard_map/pallas_call | solution.py:729
  143.0 2.9 collective-permute-start.5
  147.3 74.8 %shard_map.235 = (bf16[8,4,64,768]{3,2,1,0:T(8,128)(2,1)}, bf16[8,4,64,768]{3,2,1,0:T(8,128)(2,1)}) custom-call(bf16[2,8,64,768]{3,2,1,0:T(8,128)(2,1)} %get-tuple-element.101.u_ref, bf16[4,512,768]{2,1,0:T(8,128)(2,1)} %bitcast.47, bf16[4,768,3072]{2,1,0:T(8,128)(2,1)} %refs_15_.1, bf16[4,3072,768]{2,1,0:T(8,128)(2,1)} %refs_16_.1, ...), custom_call_target="tpu_custom_call" | custom-call | flops 38654705664 | bytes 9437184 | tf_op jit(solution)/shard_map/pallas_call | solution.py:750
  223.9 39.8 %shard_map.236 = (bf16[1536,768]{1,0:T(8,128)(2,1)}, f32[1536,768]{1,0:T(8,128)}, bf16[1536,768]{1,0:T(8,128)(2,1)}, bf16[768,768]{1,0:T(8,128)(2,1)}, f32[32,76...) custom-call(s32[1,1536]{1,0:T(1,128)} %compare_select_fusion.12.slot, ...), custom_call_target="tpu_custom_call" | custom-call | bytes 65536 | tf_op jit(solution)/shard_map/pallas_call | solution.py:1355
  263.7 3.0 collective-permute-start.8
  266.8 1.5 collective-permute-start.6
  268.3 17.7 %shard_map.237 = (bf16[768,768]{1,0:T(8,128)(2,1)}, bf16[768,768]{1,0:T(8,128)(2,1)}) custom-call(s32[2]{0:T(128)} %pad_add_fusion.1.place_ref, bf16[512,768]{1,0:T(8,128)(2,1)} %bitcast.53, bf16[512,768]{1,0:T(8,128)(2,1)} %copy-done.4, bf16[512,768]{1,0:T(8,128)(2,1)} %copy-done.5, bf16[512,768]{1,0:T(8,128)(2,1)} %copy-done.3, ...), custom_call_target="tpu_custom_call" | custom-call | bytes 65536 | tf_op jit(solution)/shard_map/pallas_call | solution.py:808
  288.0 53.9 %shard_map.238 = (bf16[1536,768]{1,0:T(8,128)(2,1)}, bf16[1536,768]{1,0:T(8,128)(2,1)}, bf16[1536,768]{1,0:T(8,128)(2,1)}, f32[12,8,128]{2,1,0:T(8,128)}, bf16[8...) custom-call(f32[12,8,128]{2,1,0:T(8,128)} %concatenate.24.lines_ref, ...), custom_call_target="tpu_custom_call" | custom-call | flops 24159191040 | bytes 16515072 | tf_op jit(solution)/shard_map/pallas_call | solution.py:447
  343.3 17.7 %shard_map.239 = (bf16[768,768]{1,0:T(8,128)(2,1)}, bf16[768,768]{1,0:T(8,128)(2,1)}) custom-call(s32[2]{0:T(128)} %pad_add_fusion.2.place_ref, bf16[512,768]{1,0:T(8,128)(2,1)} %bitcast.55, bf16[512,768]{1,0:T(8,128)(2,1)} %collective-permute-done.6.refs_1_.refs_5_, bf16[512,768]{1,0:T(8,128)(2,1)} %collective-permute-done.7.refs_2_.refs_6_, ...), custom_call_target="tpu_custom_call" | custom-call | bytes 65536 | tf_op jit(solution)/shard_map/pallas_call | solution.py:808
  360.9 20.4 %shard_map.240 = (f32[1536,768]{1,0:T(8,128)}, bf16[2304,768]{1,0:T(8,128)(2,1)}, f32[1,768]{1,0:T(1,128)}) custom-call(bf16[1536,768]{1,0:T(8,128)(2,1)} %x_ref.5, f32[1536,768]{1,0:T(8,128)} %get-tuple-element.115.dh_ref, bf16[1536,768]{1,0:T(8,128)(2,1)} %get-tuple-element.140.dq_ref, bf16[1536,768]{1,0:T(8,128)(2,1)} %get-tuple-element.141.dk_ref, ...), custom_call_target="tpu_custom_call" | custom-call | bytes 65536 | tf_op jit(solution)/shard_map/pallas_call | solution.py:1426
  382.7 95.6 %shard_map.241 = (bf16[2,768,768]{2,1,0:T(8,128)(2,1)}, bf16[2,768,768]{2,1,0:T(8,128)(2,1)}, bf16[768,768]{1,0:T(8,128)(2,1)}, bf16[768,768]{1,0:T(8,128)(2,1)}...) custom-call(bf16[512,768]{1,0:T(8,128)(2,1)} %bitcast.54, bf16[512,768]{1,0:T(8,128)(2,1)} %copy-done.4, ...), custom_call_target="tpu_custom_call" | custom-call | bytes 65536 | tf_op jit(solution)/shard_map/pallas_call | solution.py:1217
  479.8 1.4 slice_reduce_fusion
  481.3 1.5 slice_bitcast_fusion
  484.2 15.8 %shard_map.242 = (f32[4,768,768]{2,1,0:T(8,128)}, f32[4,768,768]{2,1,0:T(8,128)}, f32[768,768]{1,0:T(8,128)}, f32[768,768]{1,0:T(8,128)}, f32[768,768]{1,0:T(8,128)}, /*index=5*/f32[768,768]{1,0:T(8,128)}) custom-call(s32[4]{0:T(128)} %broadcast_select_fusion.place_ref, bf16[2,768,768]{2,1,0:T(8,128)(2,1)} %get-tuple-element.152.refs_0_, ...), custom_call_target="tpu_custom_call" | custom-call | tf_op jit(solution)/shard_map/pallas_call | solution.py:859
  500.0 1.4 copy.47
  (76 shorter events, 18.5 us)
Async XLA Ops:
  0.6 22.3 %copy-start = (f32[32,12]{0,1:T(8,128)S(1)}, f32[32,12]{0,1:T(8,128)}, u32[]{:S(2)}) copy-start(f32[32,12]{0,1:T(8,128)} %param.21) | copy-start | bytes 4612
  0.7 19.9 %copy-start.12 = (s32[1536,1]{0,1:T(1,128)S(1)}, s32[1536,1]{0,1:T(1,128)}, u32[]{:S(2)}) copy-start(s32[1536,1]{0,1:T(1,128)} %param.25) | copy-start | bytes 18436
  0.7 21.0 %copy-start.13 = (f32[768]{0:T(1024)S(1)}, f32[768]{0:T(1024)}, u32[]{:S(2)}) copy-start(f32[768]{0:T(1024)} %param.19) | copy-start | bytes 9220
  0.7 21.6 %copy-start.14 = (f32[768]{0:T(1024)S(1)}, f32[768]{0:T(1024)}, u32[]{:S(2)}) copy-start(f32[768]{0:T(1024)} %param.20) | copy-start | bytes 9220
  0.7 22.6 %copy-start.11 = (f32[768,32]{0,1:T(8,128)S(1)}, f32[768,32]{0,1:T(8,128)}, u32[]{:S(2)}) copy-start(f32[768,32]{0,1:T(8,128)} %param.22) | copy-start | bytes 294916
  14.9 126.9 %collective-permute-start.2 = (bf16[8,2,64,768]{3,2,1,0:T(8,128)(2,1)}, bf16[8,2,64,768]{3,2,1,0:T(8,128)(2,1)S(1)}, u32[]{:S(2)}, u32[]{:S(2)}) collective-permute-start(bf16[8,2,64,768]{3,2,1,0:T(8,128)(2,1)} %bitcast.72), channel_id=1, source_target_pairs={{0,1},{1,0},{2,3},{3,2},{4,5},{5,4},{6,7},{7,6},{8,9},{9,8},{10,11... | collective-permute-start | bytes 4718600 | tf_op jit(solution)/shard_map/ppermute | solution.py:1482
  17.9 206.0 %collective-permute-start.1 = (bf16[8,2,64,768]{3,2,1,0:T(8,128)(2,1)}, bf16[8,2,64,768]{3,2,1,0:T(8,128)(2,1)}, u32[]{:S(2)}, u32[]{:S(2)}) collective-permute-start(bf16[8,2,64,768]{3,2,1,0:T(8,128)(2,1)} %bitcast.73), channel_id=1, source_target_pairs={{0,3},{1,2},{2,1},{3,0},{4,7},{5,6},{6,5},{7,4},{8,11},{9,10},{10,... | collective-permute-start | bytes 4718600 | tf_op jit(solution)/shard_map/ppermute | solution.py:1482
  20.4 203.5 %collective-permute-start = (bf16[8,2,64,768]{3,2,1,0:T(8,128)(2,1)}, bf16[8,2,64,768]{3,2,1,0:T(8,128)(2,1)}, u32[]{:S(2)}, u32[]{:S(2)}) collective-permute-start(bf16[8,2,64,768]{3,2,1,0:T(8,128)(2,1)} %bitcast.75), channel_id=1, source_target_pairs={{0,2},{1,3},{2,0},{3,1},{4,6},{5,7},{6,4},{7,5},{8,10},{9,11},{10,... | collective-permute-start | bytes 4718600 | tf_op jit(solution)/shard_map/ppermute | solution.py:1482
  143.0 123.8 %collective-permute-start.5 = (bf16[512,768]{1,0:T(8,128)(2,1)}, bf16[512,768]{1,0:T(8,128)(2,1)S(1)}, u32[]{:S(2)}, u32[]{:S(2)}) collective-permute-start(bf16[512,768]{1,0:T(8,128)(2,1)} %bitcast.79), channel_id=1, source_target_pairs={{0,3},{1,2},{2,1},{3,0},{4,7},{5,6},{6,5},{7,4},{8,11},{9,10},{10,... | collective-permute-start | bytes 2359304 | tf_op jit(solution)/shard_map/ppermute | solution.py:1482
  145.9 120.9 %collective-permute-start.3 = (bf16[512,768]{1,0:T(8,128)(2,1)}, bf16[512,768]{1,0:T(8,128)(2,1)S(1)}, u32[]{:S(2)}, u32[]{:S(2)}) collective-permute-start(bf16[512,768]{1,0:T(8,128)(2,1)} %bitcast.80), channel_id=1, source_target_pairs={{0,1},{1,0},{2,3},{3,2},{4,5},{5,4},{6,7},{7,6},{8,9},{9,8},{10,11... | collective-permute-start | bytes 2359304 | tf_op jit(solution)/shard_map/ppermute | solution.py:1482
  146.3 120.4 %collective-permute-start.4 = (bf16[512,768]{1,0:T(8,128)(2,1)}, bf16[512,768]{1,0:T(8,128)(2,1)S(1)}, u32[]{:S(2)}, u32[]{:S(2)}) collective-permute-start(bf16[512,768]{1,0:T(8,128)(2,1)} %bitcast.52), channel_id=1, source_target_pairs={{0,2},{1,3},{2,0},{3,1},{4,6},{5,7},{6,4},{7,5},{8,10},{9,11},{10,... | collective-permute-start | bytes 2359304 | tf_op jit(solution)/shard_map/ppermute | solution.py:1482
  223.9 42.8 %copy-start.2 = (bf16[8,64,768]{2,1,0:T(8,128)(2,1)S(1)}, bf16[8,64,768]{2,1,0:T(8,128)(2,1)}, u32[]{:S(2)}) copy-start(bf16[8,64,768]{2,1,0:T(8,128)(2,1)} %get-tuple-element.105) | copy-start | bytes 2359300
  263.7 79.5 %collective-permute-start.8 = (bf16[512,768]{1,0:T(8,128)(2,1)}, bf16[512,768]{1,0:T(8,128)(2,1)}, u32[]{:S(2)}, u32[]{:S(2)}) collective-permute-start(bf16[512,768]{1,0:T(8,128)(2,1)} %bitcast.7), channel_id=1, source_target_pairs={{0,3},{1,2},{2,1},{3,0},{4,7},{5,6},{6,5},{7,4},{8,11},{9,10},{10,... | collective-permute-start | bytes 2359304 | tf_op jit(solution)/shard_map/ppermute | solution.py:1482
  266.7 76.6 %collective-permute-start.7 = (bf16[512,768]{1,0:T(8,128)(2,1)S(1)}, bf16[512,768]{1,0:T(8,128)(2,1)}, u32[]{:S(2)}, u32[]{:S(2)}) collective-permute-start(bf16[512,768]{1,0:T(8,128)(2,1)S(1)} %bitcast.57), channel_id=1, source_target_pairs={{0,2},{1,3},{2,0},{3,1},{4,6},{5,7},{6,4},{7,5},{8,10},{9,11},{10,... | collective-permute-start | bytes 2359304 | tf_op jit(solution)/shard_map/ppermute | solution.py:1482
  266.7 1.6 copy-start.5
  266.7 1.6 copy-start.3
  266.7 1.5 copy-start.4
  266.8 76.5 %collective-permute-start.6 = (bf16[512,768]{1,0:T(8,128)(2,1)}, bf16[512,768]{1,0:T(8,128)(2,1)}, u32[]{:S(2)}, u32[]{:S(2)}) collective-permute-start(bf16[512,768]{1,0:T(8,128)(2,1)} %bitcast.7), channel_id=1, source_target_pairs={{0,1},{1,0},{2,3},{3,2},{4,5},{5,4},{6,7},{7,6},{8,9},{9,8},{10,11... | collective-permute-start | bytes 2359304 | tf_op jit(solution)/shard_map/ppermute | solution.py:1482
  285.9 196.8 %collective-permute-start.9 = (bf16[768,768]{1,0:T(8,128)(2,1)}, bf16[768,768]{1,0:T(8,128)(2,1)S(1)}, u32[]{:S(2)}, u32[]{:S(2)}) collective-permute-start(bf16[768,768]{1,0:T(8,128)(2,1)} %get-tuple-element.154), channel_id=1, source_target_pairs={{0,1},{1,0},{2,3},{3,2},{4,5},{5,4},{6,7},{7,6},{8,9},{9,8},{10,11... | collective-permute-start | bytes 3538952 | tf_op jit(solution)/shard_map/ppermute | solution.py:1482
  287.2 195.6 %collective-permute-start.10 = (bf16[768,768]{1,0:T(8,128)(2,1)}, bf16[768,768]{1,0:T(8,128)(2,1)S(1)}, u32[]{:S(2)}, u32[]{:S(2)}) collective-permute-start(bf16[768,768]{1,0:T(8,128)(2,1)} %get-tuple-element.156), channel_id=1, source_target_pairs={{0,1},{1,0},{2,3},{3,2},{4,5},{5,4},{6,7},{7,6},{8,9},{9,8},{10,11... | collective-permute-start | bytes 3538952 | tf_op jit(solution)/shard_map/ppermute | solution.py:1482
  360.9 20.4 %copy-start.10 = (f32[32,768]{1,0:T(8,128)S(1)}, f32[32,768]{1,0:T(8,128)}, u32[]{:S(2)}) copy-start(f32[32,768]{1,0:T(8,128)} %get-tuple-element.148) | copy-start | bytes 294916
  360.9 20.4 %copy-start.15 = (f32[1,768]{1,0:T(1,128)S(1)}, f32[1,768]{1,0:T(1,128)}, u32[]{:S(2)}) copy-start(f32[1,768]{1,0:T(1,128)} %get-tuple-element.150) | copy-start | bytes 9220
  484.2 15.8 %copy-start.6 = (bf16[1536,768]{1,0:T(8,128)(2,1)S(1)}, bf16[1536,768]{1,0:T(8,128)(2,1)}, u32[]{:S(2)}) copy-start(bf16[1536,768]{1,0:T(8,128)(2,1)} %get-tuple-element.220) | copy-start | bytes 7077892
  500.0 1.4 copy-start.1
  (3 other events, 3.6 us)

commit v6 on v5

--- a/solution.py
+++ b/solution.py
@@ -835,23 +835,42 @@
 def finish_kernel(half, place_ref, *refs):
     own_in, own_out, refs = refs[0], refs[1], refs[2:]
     came_in, came_out, dense_ref = refs[:half], refs[half : 2 * half], refs[2 * half]
-    a_out, b_out, *dense_outs = refs[2 * half + 1 :]
-    width = dense_ref.shape[1]
-    for step in range(2 * half):
-
-        @pl.when(pl.program_id(0) == step)
+    a_out, b_out, *dense_outs = refs[2 * half + 1 : 2 * half + 7]
+    held, sem = refs[2 * half + 7 :]
+    at, last_step = pl.program_id(0), pl.num_programs(0) - 1
+    dense = [
+        pltpu.make_async_copy(held.at[which], dense_outs[which], sem.at[which]) for which in range(4)
+    ]
+    held[at] = dense_ref[...].astype(F32)
+    for which in range(4):
+        pl.when(at == which)(dense[which].start)
+
+    @pl.when(at < half)
+    def _():
+        a_out[0] = own_in[0].astype(F32)
+        b_out[0] = own_out[0].astype(F32)
+
+    for step in range(half):
+
+        @pl.when(at == half + step)
         def _(step=step):
-            a_out[0] = (own_in[step] if step < half else came_in[step - half][...]).astype(F32)
-            b_out[0] = (own_out[step] if step < half else came_out[step - half][...]).astype(F32)
-            for which in range(step, 4, 2 * half):
-                dense_outs[which][...] = dense_ref[which * width : (which + 1) * width, :].astype(F32)
+            a_out[0] = came_in[step][...].astype(F32)
+            b_out[0] = came_out[step][...].astype(F32)
+
+    @pl.when(at == last_step)
+    def _():
+        for copy in dense:
+            copy.wait()
 
 
 def finish(places, own_in, own_out, came_in, came_out, dense):
     half, width, size = own_in.shape
 
     def whole(*shape):
-        return pl.BlockSpec(shape, lambda e, p: (0,) * len(shape))
+        return pl.BlockSpec(shape, lambda e, p: (0, 0))
+
+    def own(*shape):
+        return pl.BlockSpec((1,) + shape, lambda e, p: (jnp.minimum(e, half - 1), 0, 0))
 
     def spec(*shape):
         return pl.BlockSpec((1,) + shape, lambda e, p: (p[e], 0, 0))
@@ -861,11 +880,13 @@
         grid_spec=pltpu.PrefetchScalarGridSpec(
             num_scalar_prefetch=1,
             grid=(2 * half,),
-            in_specs=[whole(half, width, size), whole(half, size, width)]
+            in_specs=[own(width, size), own(size, width)]
             + [whole(width, size)] * half
             + [whole(size, width)] * half
-            + [whole(4 * width, width)],
-            out_specs=[spec(width, size), spec(size, width)] + [whole(width, width)] * 4,
+            + [pl.BlockSpec((width, width), lambda e, p: (e, 0))],
+            out_specs=[spec(width, size), spec(size, width)]
+            + [pl.BlockSpec(memory_space=pl.ANY)] * 4,
+            scratch_shapes=[pltpu.VMEM((4, width, width), F32), pltpu.SemaphoreType.DMA((4,))],
         ),
         out_shape=[
             jax.ShapeDtypeStruct((2 * half, width, size), F32),
@@ -1271,9 +1292,15 @@
     sent_refs, refs = refs[:parts], refs[parts:]
     mixed_ref, dh_ref, do_ref, wo_ref_out, wr_sum, gain_sum = refs[:6]
     came_refs, refs = refs[6 : 6 + parts * experts], refs[6 + parts * experts :]
-    wo_sum, *sems = refs
+    wo_sum, e_held, d_held, load_sem, *sems = refs
     step = pl.program_id(0)
     me, blocks = lax.axis_index("exp"), sent_refs[0].shape[0]
+
+    def loads():
+        return [
+            pltpu.make_async_copy(e_ref, e_held, load_sem.at[0]),
+            pltpu.make_async_copy(d_ref, d_held, load_sem.at[1]),
+        ]
 
     def transfers():
         copies = []
@@ -1285,9 +1312,13 @@
 
     @pl.when(step == 0)
     def _():
+        for copy in loads():
+            copy.start()
         greet(me, blocks)
         for copy in transfers():
             copy.start()
+        for copy in loads():
+            copy.wait()
 
     @pl.when(step == pl.num_programs(0) - 1)
     def _():
@@ -1299,7 +1330,7 @@
     picks = jnp.where(
         slot == lax.broadcasted_iota(jnp.int32, (tokens, slots), 1), 1.0, 0.0
     ).astype(BF)
-    returned, arrived = mm(picks, e_ref[...]), mm(picks, d_ref[...])
+    returned, arrived = mm(picks, e_held[...]), mm(picks, d_held[...])
     gate, probs, mixed = gate_ref[...], probs_ref[...], h_ref[...]
     upstream = c_ref[...].astype(F32)
     mixed_ref[...] = (mixed + gate * returned).astype(BF)
@@ -1356,7 +1387,7 @@
         functools.partial(combine_kernel, parts, local - 1),
         grid=(tokens // size,),
         in_specs=[pl.BlockSpec((1, size), lambda t: (0, t)), rows(1), rows(1), rows(experts), rows(width), rows(width), rows(width)]
-        + [whole(slots, width)] * 2
+        + [anywhere] * 2
         + [whole(width, width), whole(width, experts)]
         + [whole(1, width)]
         + [anywhere] * parts,
@@ -1372,7 +1403,13 @@
             jax.ShapeDtypeStruct((1, width), F32),
         ]
         + [jax.ShapeDtypeStruct((blocks, padded, width), BF)] * spreads,
-        scratch_shapes=[pltpu.VMEM((width, width), F32)] + spread_sems(spreads, blocks),
+        scratch_shapes=[
+            pltpu.VMEM((width, width), F32),
+            pltpu.VMEM((slots, width), BF),
+            pltpu.VMEM((slots, width), BF),
+            pltpu.SemaphoreType.DMA((2,)),
+            *spread_sems(spreads, blocks),
+        ],
         compiler_params=params(collective_id=5, has_side_effects=True),
         cost_estimate=NO_COST,
     )(slot, expert, gate, probs, h, c, o, e_out, du, wo, wr, gain, *sent)

time: 511 us -> 508 us (level)
  no operation moved by 1% of the time
where the time goes in v6:
time: 508 us; the launch traced here: 499 us
  Pallas kernels  459 us (90%)
  starting transfers between devices  16.5 us (3%)
  local copies, waits for them, and re-layouts  14 us (3%)
  other arithmetic  7.96 us (2%)
    pallas_call x1, Pallas kernels, tail(): pl.pallas_call(functools.partial(tail_kernel, 3, sources, experts, capaci...  95.6 us
    pallas_call x1, Pallas kernels, expert_pass(): pl.pallas_call(functools.partial(expert_rest_kernel, 3), grid=(late, hidd...  74.8 us
    pallas_call x1, Pallas kernels, attention_back(): pl.pallas_call(functools.partial(attention_back_kernel, parts), grid=(pai...  53.9 us
    pallas_call x1, Pallas kernels, expert_pass(): pl.pallas_call(functools.partial(expert_kernel, 3, experts), grid=(early,...  43.7 us
    pallas_call x1, Pallas kernels, attention(): pl.pallas_call(attention_kernel, grid=(pairs, seqs), in_specs=[pl.BlockSp...  41 us
    pallas_call x1, Pallas kernels, combine(): pl.pallas_call(functools.partial(combine_kernel, parts, local - 1), grid=...  37.9 us
    pallas_call x2, Pallas kernels, weight_grads(): pl.pallas_call(functools.partial(weights_kernel, 3, sources, capacity, pa...  35.3 us
    pallas_call x1, Pallas kernels, last(): pl.pallas_call(last_kernel, grid=(tokens // size,), in_specs=[rows] * 5 +...  20.4 us
  transfers between devices with their start and end apart: 11, of which 0 were waited for; matrix products, arithmetic and copies ran while one was open for 3% of the time, Pallas kernels for 87%

profile of v6, /device:TPU:0, one launch (start us, length us, event | category | flops | bytes accessed | tf_op | source)
XLA Modules:
  0.0 499.2 jit_solution(5379354451292882145)
XLA Ops:
  2.2 2.0 convert_reduce_fusion
  4.2 1.5 compare_select_fusion.11
  5.6 9.3 %shard_map.229 = (bf16[1024,768]{1,0:T(8,128)(2,1)}, bf16[1024,768]{1,0:T(8,128)(2,1)}) custom-call(s32[1,1536]{1,0:T(1,128)} %get-tuple-element.204.slot_ref, bf16[1536,768]{1,0:T(8,128)(2,1)} %c_ref.1), custom_call_target="tpu_custom_call" | custom-call | bytes 65536 | tf_op jit(solution)/shard_map/pallas_call | solution.py:169
  14.9 3.0 collective-permute-start.2
  17.9 2.5 collective-permute-start.1
  24.8 9.5 %shard_map.230 = (bf16[1536,768]{1,0:T(8,128)(2,1)}, bf16[1536,768]{1,0:T(8,128)(2,1)}, bf16[1536,768]{1,0:T(8,128)(2,1)}) custom-call(bf16[1536,768]{1,0:T(8,128)(2,1)} %x_ref.5, f32[1,768]{1,0:T(1,128)} %broadcast_in_dim.13.gain_ref, bf16[768,768]{1,0:T(8,128)(2,1)} %wq_ref.3, bf16[768,768]{1,0:T(8,128)(2,1)} %wk_ref.3, bf16[768,768]{1,0:T(8,128)(2,1)} %wv_ref.3), custom_call_target="tpu_custom_call" | custom-call | bytes 65536 | tf_op jit(solution)/shard_map/pallas_call | solution.py:200
  34.4 41.0 %shard_map.231 = (bf16[1536,768]{1,0:T(8,128)(2,1)}, f32[6,3,2,512]{3,2,1,0:T(2,128)}, bf16[4,8,64,768]{3,2,1,0:T(8,128)(2,1)}) custom-call(f32[12,8,128]{2,1,0:T(8,128)} %concatenate.24.lines_ref, bf16[8,2,64,768]{3,2,1,0:T(8,128)(2,1)} %bitcast.76, bf16[8,2,64,768]{3,2,1,0:T(8,128)(2,1)} %bitcast.74, bf16[1536,768]{1,0:T(8,128)(2,1)} %get-tuple-element.91.q_ref, ...), custom_call_target="tpu_custom_call" | custom-call | bytes 65536 | tf_op jit(solution)/shard_map/pallas_call | solution.py:321
  75.4 11.2 %shard_map.232 = (f32[1536,768]{1,0:T(8,128)}, bf16[1536,768]{1,0:T(8,128)(2,1)}, f32[1536,32]{1,0:T(8,128)}, f32[1536,1]{1,0:T(8,128)}, f32[1,1536]{1,0:T(1,128)}) custom-call(bf16[1536,768]{1,0:T(8,128)(2,1)} %get-tuple-element.94.o_ref, bf16[1536,768]{1,0:T(8,128)(2,1)} %x_ref.5, bf16[768,768]{1,0:T(8,128)(2,1)} %wo_ref.3, ...), custom_call_target="tpu_custom_call" | custom-call | bytes 65536 | tf_op jit(solution)/shard_map/pallas_call | solution.py:506
  87.2 10.9 %shard_map.233 = bf16[2048,768]{1,0:T(8,128)(2,1)} custom-call(s32[1,1536]{1,0:T(1,128)} %compare_select_fusion.12.slot_ref, f32[1,1536]{1,0:T(1,128)} %get-tuple-element.98.gate_ref, bf16[1536,768]{1,0:T(8,128)(2,1)} %get-tuple-element.99.rows_ref), custom_call_target="tpu_custom_call" | custom-call | bytes 65536 | tf_op jit(solution)/shard_map/pallas_call | solution.py:139
  98.1 43.7 %shard_map.234 = (bf16[8,64,768]{2,1,0:T(8,128)(2,1)}, bf16[8,64,768]{2,1,0:T(8,128)(2,1)}, bf16[8,64,768]{2,1,0:T(8,128)(2,1)}, bf16[8,64,768]{2,1,0:T(8,128)(2...) custom-call(bf16[8,4,64,768]{3,2,1,0:T(8,128)(2,1)} %bitcast.51, ...), custom_call_target="tpu_custom_call" | custom-call | bytes 65536 | tf_op jit(solution)/shard_map/pallas_call | solution.py:729
  143.0 2.9 collective-permute-start.5
  147.3 74.8 %shard_map.235 = (bf16[8,4,64,768]{3,2,1,0:T(8,128)(2,1)}, bf16[8,4,64,768]{3,2,1,0:T(8,128)(2,1)}) custom-call(bf16[2,8,64,768]{3,2,1,0:T(8,128)(2,1)} %get-tuple-element.101.u_ref, bf16[4,512,768]{2,1,0:T(8,128)(2,1)} %bitcast.47, bf16[4,768,3072]{2,1,0:T(8,128)(2,1)} %refs_15_.1, bf16[4,3072,768]{2,1,0:T(8,128)(2,1)} %refs_16_.1, ...), custom_call_target="tpu_custom_call" | custom-call | flops 38654705664 | bytes 9437184 | tf_op jit(solution)/shard_map/pallas_call | solution.py:750
  223.9 37.9 %shard_map.236 = (bf16[1536,768]{1,0:T(8,128)(2,1)}, f32[1536,768]{1,0:T(8,128)}, bf16[1536,768]{1,0:T(8,128)(2,1)}, bf16[768,768]{1,0:T(8,128)(2,1)}, f32[32,76...) custom-call(s32[1,1536]{1,0:T(1,128)} %compare_select_fusion.12.slot, ...), custom_call_target="tpu_custom_call" | custom-call | bytes 65536 | tf_op jit(solution)/shard_map/pallas_call | solution.py:1386
  261.8 3.0 collective-permute-start.8
  264.9 1.5 collective-permute-start.6
  266.4 17.7 %shard_map.237 = (bf16[768,768]{1,0:T(8,128)(2,1)}, bf16[768,768]{1,0:T(8,128)(2,1)}) custom-call(s32[2]{0:T(128)} %pad_add_fusion.1.place_ref, bf16[512,768]{1,0:T(8,128)(2,1)} %bitcast.53, bf16[512,768]{1,0:T(8,128)(2,1)} %copy-done.4, bf16[512,768]{1,0:T(8,128)(2,1)} %copy-done.5, bf16[512,768]{1,0:T(8,128)(2,1)} %copy-done.3, ...), custom_call_target="tpu_custom_call" | custom-call | bytes 65536 | tf_op jit(solution)/shard_map/pallas_call | solution.py:808
  286.1 53.9 %shard_map.238 = (bf16[1536,768]{1,0:T(8,128)(2,1)}, bf16[1536,768]{1,0:T(8,128)(2,1)}, bf16[1536,768]{1,0:T(8,128)(2,1)}, f32[12,8,128]{2,1,0:T(8,128)}, bf16[8...) custom-call(f32[12,8,128]{2,1,0:T(8,128)} %concatenate.24.lines_ref, ...), custom_call_target="tpu_custom_call" | custom-call | flops 24159191040 | bytes 16515072 | tf_op jit(solution)/shard_map/pallas_call | solution.py:447
  341.4 17.7 %shard_map.239 = (bf16[768,768]{1,0:T(8,128)(2,1)}, bf16[768,768]{1,0:T(8,128)(2,1)}) custom-call(s32[2]{0:T(128)} %pad_add_fusion.2.place_ref, bf16[512,768]{1,0:T(8,128)(2,1)} %bitcast.55, bf16[512,768]{1,0:T(8,128)(2,1)} %collective-permute-done.6.refs_1_.refs_5_, bf16[512,768]{1,0:T(8,128)(2,1)} %collective-permute-done.7.refs_2_.refs_6_, ...), custom_call_target="tpu_custom_call" | custom-call | bytes 65536 | tf_op jit(solution)/shard_map/pallas_call | solution.py:808
  359.0 20.4 %shard_map.240 = (f32[1536,768]{1,0:T(8,128)}, bf16[2304,768]{1,0:T(8,128)(2,1)}, f32[1,768]{1,0:T(1,128)}) custom-call(bf16[1536,768]{1,0:T(8,128)(2,1)} %x_ref.5, f32[1536,768]{1,0:T(8,128)} %get-tuple-element.115.dh_ref, bf16[1536,768]{1,0:T(8,128)(2,1)} %get-tuple-element.140.dq_ref, bf16[1536,768]{1,0:T(8,128)(2,1)} %get-tuple-element.141.dk_ref, ...), custom_call_target="tpu_custom_call" | custom-call | bytes 65536 | tf_op jit(solution)/shard_map/pallas_call | solution.py:1463
  380.8 95.6 %shard_map.241 = (bf16[2,768,768]{2,1,0:T(8,128)(2,1)}, bf16[2,768,768]{2,1,0:T(8,128)(2,1)}, bf16[768,768]{1,0:T(8,128)(2,1)}, bf16[768,768]{1,0:T(8,128)(2,1)}...) custom-call(bf16[512,768]{1,0:T(8,128)(2,1)} %bitcast.54, bf16[512,768]{1,0:T(8,128)(2,1)} %copy-done.4, ...), custom_call_target="tpu_custom_call" | custom-call | bytes 65536 | tf_op jit(solution)/shard_map/pallas_call | solution.py:1238
  477.9 1.4 slice_reduce_fusion
  479.4 1.5 slice_bitcast_fusion
  482.3 15.0 %shard_map.242 = (f32[4,768,768]{2,1,0:T(8,128)}, f32[4,768,768]{2,1,0:T(8,128)}, f32[768,768]{1,0:T(8,128)}, f32[768,768]{1,0:T(8,128)}, f32[768,768]{1,0:T(8,128)}, /*index=5*/f32[768,768]{1,0:T(8,128)}) custom-call(s32[4]{0:T(128)} %broadcast_select_fusion.place_ref, bf16[2,768,768]{2,1,0:T(8,128)(2,1)} %get-tuple-element.152.refs_0_, ...), custom_call_target="tpu_custom_call" | custom-call | tf_op jit(solution)/shard_map/pallas_call | solution.py:878
  497.4 1.4 copy.47
  (76 shorter events, 18.5 us)
Async XLA Ops:
  0.6 22.3 %copy-start = (f32[32,12]{0,1:T(8,128)S(1)}, f32[32,12]{0,1:T(8,128)}, u32[]{:S(2)}) copy-start(f32[32,12]{0,1:T(8,128)} %param.21) | copy-start | bytes 4612
  0.7 19.9 %copy-start.12 = (s32[1536,1]{0,1:T(1,128)S(1)}, s32[1536,1]{0,1:T(1,128)}, u32[]{:S(2)}) copy-start(s32[1536,1]{0,1:T(1,128)} %param.25) | copy-start | bytes 18436
  0.7 21.0 %copy-start.13 = (f32[768]{0:T(1024)S(1)}, f32[768]{0:T(1024)}, u32[]{:S(2)}) copy-start(f32[768]{0:T(1024)} %param.19) | copy-start | bytes 9220
  0.7 21.6 %copy-start.14 = (f32[768]{0:T(1024)S(1)}, f32[768]{0:T(1024)}, u32[]{:S(2)}) copy-start(f32[768]{0:T(1024)} %param.20) | copy-start | bytes 9220
  0.7 22.6 %copy-start.11 = (f32[768,32]{0,1:T(8,128)S(1)}, f32[768,32]{0,1:T(8,128)}, u32[]{:S(2)}) copy-start(f32[768,32]{0,1:T(8,128)} %param.22) | copy-start | bytes 294916
  14.9 126.9 %collective-permute-start.2 = (bf16[8,2,64,768]{3,2,1,0:T(8,128)(2,1)}, bf16[8,2,64,768]{3,2,1,0:T(8,128)(2,1)S(1)}, u32[]{:S(2)}, u32[]{:S(2)}) collective-permute-start(bf16[8,2,64,768]{3,2,1,0:T(8,128)(2,1)} %bitcast.72), channel_id=1, source_target_pairs={{0,1},{1,0},{2,3},{3,2},{4,5},{5,4},{6,7},{7,6},{8,9},{9,8},{10,11... | collective-permute-start | bytes 4718600 | tf_op jit(solution)/shard_map/ppermute | solution.py:1519
  17.9 206.0 %collective-permute-start.1 = (bf16[8,2,64,768]{3,2,1,0:T(8,128)(2,1)}, bf16[8,2,64,768]{3,2,1,0:T(8,128)(2,1)}, u32[]{:S(2)}, u32[]{:S(2)}) collective-permute-start(bf16[8,2,64,768]{3,2,1,0:T(8,128)(2,1)} %bitcast.73), channel_id=1, source_target_pairs={{0,3},{1,2},{2,1},{3,0},{4,7},{5,6},{6,5},{7,4},{8,11},{9,10},{10,... | collective-permute-start | bytes 4718600 | tf_op jit(solution)/shard_map/ppermute | solution.py:1519
  20.4 203.5 %collective-permute-start = (bf16[8,2,64,768]{3,2,1,0:T(8,128)(2,1)}, bf16[8,2,64,768]{3,2,1,0:T(8,128)(2,1)}, u32[]{:S(2)}, u32[]{:S(2)}) collective-permute-start(bf16[8,2,64,768]{3,2,1,0:T(8,128)(2,1)} %bitcast.75), channel_id=1, source_target_pairs={{0,2},{1,3},{2,0},{3,1},{4,6},{5,7},{6,4},{7,5},{8,10},{9,11},{10,... | collective-permute-start | bytes 4718600 | tf_op jit(solution)/shard_map/ppermute | solution.py:1519
  143.0 121.9 %collective-permute-start.5 = (bf16[512,768]{1,0:T(8,128)(2,1)}, bf16[512,768]{1,0:T(8,128)(2,1)S(1)}, u32[]{:S(2)}, u32[]{:S(2)}) collective-permute-start(bf16[512,768]{1,0:T(8,128)(2,1)} %bitcast.79), channel_id=1, source_target_pairs={{0,3},{1,2},{2,1},{3,0},{4,7},{5,6},{6,5},{7,4},{8,11},{9,10},{10,... | collective-permute-start | bytes 2359304 | tf_op jit(solution)/shard_map/ppermute | solution.py:1519
  145.9 119.0 %collective-permute-start.3 = (bf16[512,768]{1,0:T(8,128)(2,1)}, bf16[512,768]{1,0:T(8,128)(2,1)S(1)}, u32[]{:S(2)}, u32[]{:S(2)}) collective-permute-start(bf16[512,768]{1,0:T(8,128)(2,1)} %bitcast.80), channel_id=1, source_target_pairs={{0,1},{1,0},{2,3},{3,2},{4,5},{5,4},{6,7},{7,6},{8,9},{9,8},{10,11... | collective-permute-start | bytes 2359304 | tf_op jit(solution)/shard_map/ppermute | solution.py:1519
  146.3 118.5 %collective-permute-start.4 = (bf16[512,768]{1,0:T(8,128)(2,1)}, bf16[512,768]{1,0:T(8,128)(2,1)S(1)}, u32[]{:S(2)}, u32[]{:S(2)}) collective-permute-start(bf16[512,768]{1,0:T(8,128)(2,1)} %bitcast.52), channel_id=1, source_target_pairs={{0,2},{1,3},{2,0},{3,1},{4,6},{5,7},{6,4},{7,5},{8,10},{9,11},{10,... | collective-permute-start | bytes 2359304 | tf_op jit(solution)/shard_map/ppermute | solution.py:1519
  223.9 40.9 %copy-start.2 = (bf16[8,64,768]{2,1,0:T(8,128)(2,1)S(1)}, bf16[8,64,768]{2,1,0:T(8,128)(2,1)}, u32[]{:S(2)}) copy-start(bf16[8,64,768]{2,1,0:T(8,128)(2,1)} %get-tuple-element.105) | copy-start | bytes 2359300
  261.8 79.5 %collective-permute-start.8 = (bf16[512,768]{1,0:T(8,128)(2,1)}, bf16[512,768]{1,0:T(8,128)(2,1)}, u32[]{:S(2)}, u32[]{:S(2)}) collective-permute-start(bf16[512,768]{1,0:T(8,128)(2,1)} %bitcast.7), channel_id=1, source_target_pairs={{0,3},{1,2},{2,1},{3,0},{4,7},{5,6},{6,5},{7,4},{8,11},{9,10},{10,... | collective-permute-start | bytes 2359304 | tf_op jit(solution)/shard_map/ppermute | solution.py:1519
  264.8 76.6 %collective-permute-start.7 = (bf16[512,768]{1,0:T(8,128)(2,1)S(1)}, bf16[512,768]{1,0:T(8,128)(2,1)}, u32[]{:S(2)}, u32[]{:S(2)}) collective-permute-start(bf16[512,768]{1,0:T(8,128)(2,1)S(1)} %bitcast.57), channel_id=1, source_target_pairs={{0,2},{1,3},{2,0},{3,1},{4,6},{5,7},{6,4},{7,5},{8,10},{9,11},{10,... | collective-permute-start | bytes 2359304 | tf_op jit(solution)/shard_map/ppermute | solution.py:1519
  264.8 1.6 copy-start.5
  264.8 1.6 copy-start.3
  264.9 1.5 copy-start.4
  264.9 76.5 %collective-permute-start.6 = (bf16[512,768]{1,0:T(8,128)(2,1)}, bf16[512,768]{1,0:T(8,128)(2,1)}, u32[]{:S(2)}, u32[]{:S(2)}) collective-permute-start(bf16[512,768]{1,0:T(8,128)(2,1)} %bitcast.7), channel_id=1, source_target_pairs={{0,1},{1,0},{2,3},{3,2},{4,5},{5,4},{6,7},{7,6},{8,9},{9,8},{10,11... | collective-permute-start | bytes 2359304 | tf_op jit(solution)/shard_map/ppermute | solution.py:1519
  284.1 196.8 %collective-permute-start.9 = (bf16[768,768]{1,0:T(8,128)(2,1)}, bf16[768,768]{1,0:T(8,128)(2,1)S(1)}, u32[]{:S(2)}, u32[]{:S(2)}) collective-permute-start(bf16[768,768]{1,0:T(8,128)(2,1)} %get-tuple-element.154), channel_id=1, source_target_pairs={{0,1},{1,0},{2,3},{3,2},{4,5},{5,4},{6,7},{7,6},{8,9},{9,8},{10,11... | collective-permute-start | bytes 3538952 | tf_op jit(solution)/shard_map/ppermute | solution.py:1519
  285.4 195.5 %collective-permute-start.10 = (bf16[768,768]{1,0:T(8,128)(2,1)}, bf16[768,768]{1,0:T(8,128)(2,1)S(1)}, u32[]{:S(2)}, u32[]{:S(2)}) collective-permute-start(bf16[768,768]{1,0:T(8,128)(2,1)} %get-tuple-element.156), channel_id=1, source_target_pairs={{0,1},{1,0},{2,3},{3,2},{4,5},{5,4},{6,7},{7,6},{8,9},{9,8},{10,11... | collective-permute-start | bytes 3538952 | tf_op jit(solution)/shard_map/ppermute | solution.py:1519
  359.0 20.4 %copy-start.10 = (f32[32,768]{1,0:T(8,128)S(1)}, f32[32,768]{1,0:T(8,128)}, u32[]{:S(2)}) copy-start(f32[32,768]{1,0:T(8,128)} %get-tuple-element.148) | copy-start | bytes 294916
  359.0 20.4 %copy-start.15 = (f32[1,768]{1,0:T(1,128)S(1)}, f32[1,768]{1,0:T(1,128)}, u32[]{:S(2)}) copy-start(f32[1,768]{1,0:T(1,128)} %get-tuple-element.150) | copy-start | bytes 9220
  482.3 15.1 %copy-start.6 = (bf16[1536,768]{1,0:T(8,128)(2,1)S(1)}, bf16[1536,768]{1,0:T(8,128)(2,1)}, u32[]{:S(2)}) copy-start(bf16[1536,768]{1,0:T(8,128)(2,1)} %get-tuple-element.220) | copy-start | bytes 7077892
  497.4 1.4 copy-start.1
  (3 other events, 3.6 us)

commit v7 on v6

--- a/solution.py
+++ b/solution.py
@@ -495,7 +495,7 @@
 def router(o, x, wo, gain, wr, expert):
     tokens, width = x.shape
     experts = wr.shape[1]
-    size = 256
+    size = 512
 
     def rows(columns):
         return pl.BlockSpec((size, columns), lambda t: (t, 0))
@@ -806,7 +806,7 @@
     rows, width = us[0].shape
     block = pl.BlockSpec((rows, width), lambda f, p: (0, 0))
     return pl.pallas_call(
-        functools.partial(weights_kernel, 3, sources, capacity, padded),
+        functools.partial(weights_kernel, 1, sources, capacity, padded),
         grid_spec=pltpu.PrefetchScalarGridSpec(
             num_scalar_prefetch=1,
             grid=(1,),
@@ -1456,7 +1456,7 @@
 
 def last(x, dh, dq, dk, dv, wq, wk, wv, gain):
     tokens, width = x.shape
-    size = 256
+    size = 512
     rows = pl.BlockSpec((size, width), lambda t: (t, 0))
     square = pl.BlockSpec((width, width), lambda t: (0, 0))
     one = pl.BlockSpec((1, width), lambda t: (0, 0))

time: 508 us -> 506 us (level)
  no operation moved by 1% of the time
where the time goes in v7:
time: 506 us; the launch traced here: 499 us
  Pallas kernels  458 us (91%)
  starting transfers between devices  16.5 us (3%)
  local copies, waits for them, and re-layouts  14 us (3%)
  other arithmetic  7.96 us (2%)
    pallas_call x1, Pallas kernels, tail(): pl.pallas_call(functools.partial(tail_kernel, 3, sources, experts, capaci...  95.5 us
    pallas_call x1, Pallas kernels, expert_pass(): pl.pallas_call(functools.partial(expert_rest_kernel, 3), grid=(late, hidd...  74.8 us
    pallas_call x1, Pallas kernels, attention_back(): pl.pallas_call(functools.partial(attention_back_kernel, parts), grid=(pai...  54 us
    pallas_call x1, Pallas kernels, expert_pass(): pl.pallas_call(functools.partial(expert_kernel, 3, experts), grid=(early,...  43.9 us
    pallas_call x1, Pallas kernels, attention(): pl.pallas_call(attention_kernel, grid=(pairs, seqs), in_specs=[pl.BlockSp...  41 us
    pallas_call x1, Pallas kernels, combine(): pl.pallas_call(functools.partial(combine_kernel, parts, local - 1), grid=...  37.7 us
    pallas_call x2, Pallas kernels, weight_grads(): pl.pallas_call(functools.partial(weights_kernel, 1, sources, capacity, pa...  34.3 us
    pallas_call x1, Pallas kernels, last(): pl.pallas_call(last_kernel, grid=(tokens // size,), in_specs=[rows] * 5 +...  20.6 us
  transfers between devices with their start and end apart: 11, of which 0 were waited for; matrix products, arithmetic and copies ran while one was open for 3% of the time, Pallas kernels for 87%

profile of v7, /device:TPU:0, one launch (start us, length us, event | category | flops | bytes accessed | tf_op | source)
XLA Modules:
  0.0 499.1 jit_solution(7296609749934401797)
XLA Ops:
  2.2 2.0 convert_reduce_fusion
  4.2 1.5 compare_select_fusion.11
  5.6 9.3 %shard_map.229 = (bf16[1024,768]{1,0:T(8,128)(2,1)}, bf16[1024,768]{1,0:T(8,128)(2,1)}) custom-call(s32[1,1536]{1,0:T(1,128)} %get-tuple-element.204.slot_ref, bf16[1536,768]{1,0:T(8,128)(2,1)} %c_ref.1), custom_call_target="tpu_custom_call" | custom-call | bytes 65536 | tf_op jit(solution)/shard_map/pallas_call | solution.py:169
  14.9 3.0 collective-permute-start.2
  17.9 2.5 collective-permute-start.1
  24.8 9.5 %shard_map.230 = (bf16[1536,768]{1,0:T(8,128)(2,1)}, bf16[1536,768]{1,0:T(8,128)(2,1)}, bf16[1536,768]{1,0:T(8,128)(2,1)}) custom-call(bf16[1536,768]{1,0:T(8,128)(2,1)} %x_ref.5, f32[1,768]{1,0:T(1,128)} %broadcast_in_dim.13.gain_ref, bf16[768,768]{1,0:T(8,128)(2,1)} %wq_ref.3, bf16[768,768]{1,0:T(8,128)(2,1)} %wk_ref.3, bf16[768,768]{1,0:T(8,128)(2,1)} %wv_ref.3), custom_call_target="tpu_custom_call" | custom-call | bytes 65536 | tf_op jit(solution)/shard_map/pallas_call | solution.py:200
  34.4 41.0 %shard_map.231 = (bf16[1536,768]{1,0:T(8,128)(2,1)}, f32[6,3,2,512]{3,2,1,0:T(2,128)}, bf16[4,8,64,768]{3,2,1,0:T(8,128)(2,1)}) custom-call(f32[12,8,128]{2,1,0:T(8,128)} %concatenate.24.lines_ref, bf16[8,2,64,768]{3,2,1,0:T(8,128)(2,1)} %bitcast.76, bf16[8,2,64,768]{3,2,1,0:T(8,128)(2,1)} %bitcast.74, bf16[1536,768]{1,0:T(8,128)(2,1)} %get-tuple-element.91.q_ref, ...), custom_call_target="tpu_custom_call" | custom-call | bytes 65536 | tf_op jit(solution)/shard_map/pallas_call | solution.py:321
  75.4 11.9 %shard_map.232 = (f32[1536,768]{1,0:T(8,128)}, bf16[1536,768]{1,0:T(8,128)(2,1)}, f32[1536,32]{1,0:T(8,128)}, f32[1536,1]{1,0:T(8,128)}, f32[1,1536]{1,0:T(1,128)}) custom-call(bf16[1536,768]{1,0:T(8,128)(2,1)} %get-tuple-element.94.o_ref, bf16[1536,768]{1,0:T(8,128)(2,1)} %x_ref.5, bf16[768,768]{1,0:T(8,128)(2,1)} %wo_ref.3, ...), custom_call_target="tpu_custom_call" | custom-call | bytes 65536 | tf_op jit(solution)/shard_map/pallas_call | solution.py:506
  87.9 10.9 %shard_map.233 = bf16[2048,768]{1,0:T(8,128)(2,1)} custom-call(s32[1,1536]{1,0:T(1,128)} %compare_select_fusion.12.slot_ref, f32[1,1536]{1,0:T(1,128)} %get-tuple-element.98.gate_ref, bf16[1536,768]{1,0:T(8,128)(2,1)} %get-tuple-element.99.rows_ref), custom_call_target="tpu_custom_call" | custom-call | bytes 65536 | tf_op jit(solution)/shard_map/pallas_call | solution.py:139
  98.8 43.9 %shard_map.234 = (bf16[8,64,768]{2,1,0:T(8,128)(2,1)}, bf16[8,64,768]{2,1,0:T(8,128)(2,1)}, bf16[8,64,768]{2,1,0:T(8,128)(2,1)}, bf16[8,64,768]{2,1,0:T(8,128)(2...) custom-call(bf16[8,4,64,768]{3,2,1,0:T(8,128)(2,1)} %bitcast.51, ...), custom_call_target="tpu_custom_call" | custom-call | bytes 65536 | tf_op jit(solution)/shard_map/pallas_call | solution.py:729
  143.9 2.9 collective-permute-start.5
  148.2 74.8 %shard_map.235 = (bf16[8,4,64,768]{3,2,1,0:T(8,128)(2,1)}, bf16[8,4,64,768]{3,2,1,0:T(8,128)(2,1)}) custom-call(bf16[2,8,64,768]{3,2,1,0:T(8,128)(2,1)} %get-tuple-element.101.u_ref, bf16[4,512,768]{2,1,0:T(8,128)(2,1)} %bitcast.47, bf16[4,768,3072]{2,1,0:T(8,128)(2,1)} %refs_15_.1, bf16[4,3072,768]{2,1,0:T(8,128)(2,1)} %refs_16_.1, ...), custom_call_target="tpu_custom_call" | custom-call | flops 38654705664 | bytes 9437184 | tf_op jit(solution)/shard_map/pallas_call | solution.py:750
  224.8 37.7 %shard_map.236 = (bf16[1536,768]{1,0:T(8,128)(2,1)}, f32[1536,768]{1,0:T(8,128)}, bf16[1536,768]{1,0:T(8,128)(2,1)}, bf16[768,768]{1,0:T(8,128)(2,1)}, f32[32,76...) custom-call(s32[1,1536]{1,0:T(1,128)} %compare_select_fusion.12.slot, ...), custom_call_target="tpu_custom_call" | custom-call | bytes 65536 | tf_op jit(solution)/shard_map/pallas_call | solution.py:1386
  262.5 3.0 collective-permute-start.8
  265.5 1.5 collective-permute-start.6
  267.1 17.1 %shard_map.237 = (bf16[768,768]{1,0:T(8,128)(2,1)}, bf16[768,768]{1,0:T(8,128)(2,1)}) custom-call(s32[2]{0:T(128)} %pad_add_fusion.1.place_ref, bf16[512,768]{1,0:T(8,128)(2,1)} %bitcast.53, bf16[512,768]{1,0:T(8,128)(2,1)} %copy-done.4, bf16[512,768]{1,0:T(8,128)(2,1)} %copy-done.5, bf16[512,768]{1,0:T(8,128)(2,1)} %copy-done.3, ...), custom_call_target="tpu_custom_call" | custom-call | bytes 65536 | tf_op jit(solution)/shard_map/pallas_call | solution.py:808
  286.2 54.0 %shard_map.238 = (bf16[1536,768]{1,0:T(8,128)(2,1)}, bf16[1536,768]{1,0:T(8,128)(2,1)}, bf16[1536,768]{1,0:T(8,128)(2,1)}, f32[12,8,128]{2,1,0:T(8,128)}, bf16[8...) custom-call(f32[12,8,128]{2,1,0:T(8,128)} %concatenate.24.lines_ref, ...), custom_call_target="tpu_custom_call" | custom-call | flops 24159191040 | bytes 16515072 | tf_op jit(solution)/shard_map/pallas_call | solution.py:447
  341.6 17.1 %shard_map.239 = (bf16[768,768]{1,0:T(8,128)(2,1)}, bf16[768,768]{1,0:T(8,128)(2,1)}) custom-call(s32[2]{0:T(128)} %pad_add_fusion.2.place_ref, bf16[512,768]{1,0:T(8,128)(2,1)} %bitcast.55, bf16[512,768]{1,0:T(8,128)(2,1)} %collective-permute-done.6.refs_1_.refs_5_, bf16[512,768]{1,0:T(8,128)(2,1)} %collective-permute-done.7.refs_2_.refs_6_, ...), custom_call_target="tpu_custom_call" | custom-call | bytes 65536 | tf_op jit(solution)/shard_map/pallas_call | solution.py:808
  358.8 20.6 %shard_map.240 = (f32[1536,768]{1,0:T(8,128)}, bf16[2304,768]{1,0:T(8,128)(2,1)}, f32[1,768]{1,0:T(1,128)}) custom-call(bf16[1536,768]{1,0:T(8,128)(2,1)} %x_ref.5, f32[1536,768]{1,0:T(8,128)} %get-tuple-element.115.dh_ref, bf16[1536,768]{1,0:T(8,128)(2,1)} %get-tuple-element.140.dq_ref, bf16[1536,768]{1,0:T(8,128)(2,1)} %get-tuple-element.141.dk_ref, ...), custom_call_target="tpu_custom_call" | custom-call | bytes 65536 | tf_op jit(solution)/shard_map/pallas_call | solution.py:1463
  380.8 95.5 %shard_map.241 = (bf16[2,768,768]{2,1,0:T(8,128)(2,1)}, bf16[2,768,768]{2,1,0:T(8,128)(2,1)}, bf16[768,768]{1,0:T(8,128)(2,1)}, bf16[768,768]{1,0:T(8,128)(2,1)}...) custom-call(bf16[512,768]{1,0:T(8,128)(2,1)} %bitcast.54, bf16[512,768]{1,0:T(8,128)(2,1)} %copy-done.4, ...), custom_call_target="tpu_custom_call" | custom-call | bytes 65536 | tf_op jit(solution)/shard_map/pallas_call | solution.py:1238
  477.8 1.4 slice_reduce_fusion
  479.2 1.5 slice_bitcast_fusion
  482.2 15.0 %shard_map.242 = (f32[4,768,768]{2,1,0:T(8,128)}, f32[4,768,768]{2,1,0:T(8,128)}, f32[768,768]{1,0:T(8,128)}, f32[768,768]{1,0:T(8,128)}, f32[768,768]{1,0:T(8,128)}, /*index=5*/f32[768,768]{1,0:T(8,128)}) custom-call(s32[4]{0:T(128)} %broadcast_select_fusion.place_ref, bf16[2,768,768]{2,1,0:T(8,128)(2,1)} %get-tuple-element.152.refs_0_, ...), custom_call_target="tpu_custom_call" | custom-call | tf_op jit(solution)/shard_map/pallas_call | solution.py:878
  497.2 1.4 copy.47
  (76 shorter events, 18.5 us)
Async XLA Ops:
  0.6 22.3 %copy-start = (f32[32,12]{0,1:T(8,128)S(1)}, f32[32,12]{0,1:T(8,128)}, u32[]{:S(2)}) copy-start(f32[32,12]{0,1:T(8,128)} %param.21) | copy-start | bytes 4612
  0.7 19.9 %copy-start.12 = (s32[1536,1]{0,1:T(1,128)S(1)}, s32[1536,1]{0,1:T(1,128)}, u32[]{:S(2)}) copy-start(s32[1536,1]{0,1:T(1,128)} %param.25) | copy-start | bytes 18436
  0.7 21.0 %copy-start.13 = (f32[768]{0:T(1024)S(1)}, f32[768]{0:T(1024)}, u32[]{:S(2)}) copy-start(f32[768]{0:T(1024)} %param.19) | copy-start | bytes 9220
  0.7 21.6 %copy-start.14 = (f32[768]{0:T(1024)S(1)}, f32[768]{0:T(1024)}, u32[]{:S(2)}) copy-start(f32[768]{0:T(1024)} %param.20) | copy-start | bytes 9220
  0.7 22.6 %copy-start.11 = (f32[768,32]{0,1:T(8,128)S(1)}, f32[768,32]{0,1:T(8,128)}, u32[]{:S(2)}) copy-start(f32[768,32]{0,1:T(8,128)} %param.22) | copy-start | bytes 294916
  14.9 127.8 %collective-permute-start.2 = (bf16[8,2,64,768]{3,2,1,0:T(8,128)(2,1)}, bf16[8,2,64,768]{3,2,1,0:T(8,128)(2,1)S(1)}, u32[]{:S(2)}, u32[]{:S(2)}) collective-permute-start(bf16[8,2,64,768]{3,2,1,0:T(8,128)(2,1)} %bitcast.72), channel_id=1, source_target_pairs={{0,1},{1,0},{2,3},{3,2},{4,5},{5,4},{6,7},{7,6},{8,9},{9,8},{10,11... | collective-permute-start | bytes 4718600 | tf_op jit(solution)/shard_map/ppermute | solution.py:1519
  17.9 206.9 %collective-permute-start.1 = (bf16[8,2,64,768]{3,2,1,0:T(8,128)(2,1)}, bf16[8,2,64,768]{3,2,1,0:T(8,128)(2,1)}, u32[]{:S(2)}, u32[]{:S(2)}) collective-permute-start(bf16[8,2,64,768]{3,2,1,0:T(8,128)(2,1)} %bitcast.73), channel_id=1, source_target_pairs={{0,3},{1,2},{2,1},{3,0},{4,7},{5,6},{6,5},{7,4},{8,11},{9,10},{10,... | collective-permute-start | bytes 4718600 | tf_op jit(solution)/shard_map/ppermute | solution.py:1519
  20.4 204.4 %collective-permute-start = (bf16[8,2,64,768]{3,2,1,0:T(8,128)(2,1)}, bf16[8,2,64,768]{3,2,1,0:T(8,128)(2,1)}, u32[]{:S(2)}, u32[]{:S(2)}) collective-permute-start(bf16[8,2,64,768]{3,2,1,0:T(8,128)(2,1)} %bitcast.75), channel_id=1, source_target_pairs={{0,2},{1,3},{2,0},{3,1},{4,6},{5,7},{6,4},{7,5},{8,10},{9,11},{10,... | collective-permute-start | bytes 4718600 | tf_op jit(solution)/shard_map/ppermute | solution.py:1519
  143.9 121.6 %collective-permute-start.5 = (bf16[512,768]{1,0:T(8,128)(2,1)}, bf16[512,768]{1,0:T(8,128)(2,1)S(1)}, u32[]{:S(2)}, u32[]{:S(2)}) collective-permute-start(bf16[512,768]{1,0:T(8,128)(2,1)} %bitcast.79), channel_id=1, source_target_pairs={{0,3},{1,2},{2,1},{3,0},{4,7},{5,6},{6,5},{7,4},{8,11},{9,10},{10,... | collective-permute-start | bytes 2359304 | tf_op jit(solution)/shard_map/ppermute | solution.py:1519
  146.8 118.7 %collective-permute-start.3 = (bf16[512,768]{1,0:T(8,128)(2,1)}, bf16[512,768]{1,0:T(8,128)(2,1)S(1)}, u32[]{:S(2)}, u32[]{:S(2)}) collective-permute-start(bf16[512,768]{1,0:T(8,128)(2,1)} %bitcast.80), channel_id=1, source_target_pairs={{0,1},{1,0},{2,3},{3,2},{4,5},{5,4},{6,7},{7,6},{8,9},{9,8},{10,11... | collective-permute-start | bytes 2359304 | tf_op jit(solution)/shard_map/ppermute | solution.py:1519
  147.2 118.2 %collective-permute-start.4 = (bf16[512,768]{1,0:T(8,128)(2,1)}, bf16[512,768]{1,0:T(8,128)(2,1)S(1)}, u32[]{:S(2)}, u32[]{:S(2)}) collective-permute-start(bf16[512,768]{1,0:T(8,128)(2,1)} %bitcast.52), channel_id=1, source_target_pairs={{0,2},{1,3},{2,0},{3,1},{4,6},{5,7},{6,4},{7,5},{8,10},{9,11},{10,... | collective-permute-start | bytes 2359304 | tf_op jit(solution)/shard_map/ppermute | solution.py:1519
  224.8 40.7 %copy-start.2 = (bf16[8,64,768]{2,1,0:T(8,128)(2,1)S(1)}, bf16[8,64,768]{2,1,0:T(8,128)(2,1)}, u32[]{:S(2)}) copy-start(bf16[8,64,768]{2,1,0:T(8,128)(2,1)} %get-tuple-element.105) | copy-start | bytes 2359300
  262.5 79.1 %collective-permute-start.8 = (bf16[512,768]{1,0:T(8,128)(2,1)}, bf16[512,768]{1,0:T(8,128)(2,1)}, u32[]{:S(2)}, u32[]{:S(2)}) collective-permute-start(bf16[512,768]{1,0:T(8,128)(2,1)} %bitcast.7), channel_id=1, source_target_pairs={{0,3},{1,2},{2,1},{3,0},{4,7},{5,6},{6,5},{7,4},{8,11},{9,10},{10,... | collective-permute-start | bytes 2359304 | tf_op jit(solution)/shard_map/ppermute | solution.py:1519
  265.5 76.1 %collective-permute-start.7 = (bf16[512,768]{1,0:T(8,128)(2,1)S(1)}, bf16[512,768]{1,0:T(8,128)(2,1)}, u32[]{:S(2)}, u32[]{:S(2)}) collective-permute-start(bf16[512,768]{1,0:T(8,128)(2,1)S(1)} %bitcast.57), channel_id=1, source_target_pairs={{0,2},{1,3},{2,0},{3,1},{4,6},{5,7},{6,4},{7,5},{8,10},{9,11},{10,... | collective-permute-start | bytes 2359304 | tf_op jit(solution)/shard_map/ppermute | solution.py:1519
  265.5 1.6 copy-start.5
  265.5 1.6 copy-start.3
  265.5 1.5 copy-start.4
  265.5 76.1 %collective-permute-start.6 = (bf16[512,768]{1,0:T(8,128)(2,1)}, bf16[512,768]{1,0:T(8,128)(2,1)}, u32[]{:S(2)}, u32[]{:S(2)}) collective-permute-start(bf16[512,768]{1,0:T(8,128)(2,1)} %bitcast.7), channel_id=1, source_target_pairs={{0,1},{1,0},{2,3},{3,2},{4,5},{5,4},{6,7},{7,6},{8,9},{9,8},{10,11... | collective-permute-start | bytes 2359304 | tf_op jit(solution)/shard_map/ppermute | solution.py:1519
  284.2 196.5 %collective-permute-start.9 = (bf16[768,768]{1,0:T(8,128)(2,1)}, bf16[768,768]{1,0:T(8,128)(2,1)S(1)}, u32[]{:S(2)}, u32[]{:S(2)}) collective-permute-start(bf16[768,768]{1,0:T(8,128)(2,1)} %get-tuple-element.154), channel_id=1, source_target_pairs={{0,1},{1,0},{2,3},{3,2},{4,5},{5,4},{6,7},{7,6},{8,9},{9,8},{10,11... | collective-permute-start | bytes 3538952 | tf_op jit(solution)/shard_map/ppermute | solution.py:1519
  285.5 195.3 %collective-permute-start.10 = (bf16[768,768]{1,0:T(8,128)(2,1)}, bf16[768,768]{1,0:T(8,128)(2,1)S(1)}, u32[]{:S(2)}, u32[]{:S(2)}) collective-permute-start(bf16[768,768]{1,0:T(8,128)(2,1)} %get-tuple-element.156), channel_id=1, source_target_pairs={{0,1},{1,0},{2,3},{3,2},{4,5},{5,4},{6,7},{7,6},{8,9},{9,8},{10,11... | collective-permute-start | bytes 3538952 | tf_op jit(solution)/shard_map/ppermute | solution.py:1519
  358.8 20.6 %copy-start.10 = (f32[32,768]{1,0:T(8,128)S(1)}, f32[32,768]{1,0:T(8,128)}, u32[]{:S(2)}) copy-start(f32[32,768]{1,0:T(8,128)} %get-tuple-element.148) | copy-start | bytes 294916
  358.8 20.6 %copy-start.15 = (f32[1,768]{1,0:T(1,128)S(1)}, f32[1,768]{1,0:T(1,128)}, u32[]{:S(2)}) copy-start(f32[1,768]{1,0:T(1,128)} %get-tuple-element.150) | copy-start | bytes 9220
  482.2 15.1 %copy-start.6 = (bf16[1536,768]{1,0:T(8,128)(2,1)S(1)}, bf16[1536,768]{1,0:T(8,128)(2,1)}, u32[]{:S(2)}) copy-start(bf16[1536,768]{1,0:T(8,128)(2,1)} %get-tuple-element.220) | copy-start | bytes 7077892
  497.2 1.4 copy-start.1
  (3 other events, 3.6 us)
